TPU v7x, 32 devices: a whole 2x2x4 slice. The times are simulated.
32 devices in a mesh: gen: 4 (over y, core), bus: 8 (over z, x).
Axes of the slice: x: 2, y: 2, z: 4, core: 2. Of those that a mesh axis runs over, the one named last changes fastest.
Arguments:
- bus_price: float32 [16, 12, 4096], P(None, None, 'bus'), may hold values from -4 to 4
- bus_demand: float32 [16, 12, 4096], P('gen', None, 'bus'), may hold values from 0 to 2
- multipliers: float32 [2, 16, 12, 6144], P(None, 'gen', None, 'bus'), may hold values from 0 to 1
- line_limits: float32 [6144], P('bus'), may hold values from 0.3 to 3
- ptdf_blocks: bfloat16 [48, 16, 128, 128], P('bus'), may hold values from -0.125 to 0.125
- ptdf_pattern: int32 [48, 16], P('bus'), may hold values from 0 to 31, as said below
- gen_bus: int32 [512], P(('gen', 'bus')), may hold values from 0 to 4095, as said below
- state_counts: int32 [512], P(('gen', 'bus')), may hold values from 64 to 512, as said below
- transitions: int32 [512, 3, 512], P(('gen', 'bus')), may hold values from 0 to 511, as said below
- state_level: float32 [512, 512], P(('gen', 'bus')), may hold values from 0 to 3
- state_cost: float32 [512, 512], P(('gen', 'bus')), may hold values from 0 to 2
Outputs:
- new_multipliers: float32 [2, 16, 12, 6144], P(None, 'gen', None, 'bus')
- new_price: float32 [16, 12, 4096], P(None, None, 'bus')
Inputs may be any that keep to these rules, and one draw needn't show every extreme that they name: Generator i sits in bus block (i // 16) % 8: gen_bus[i] // 512 equals that number. `state_counts`: among the generators of each aligned group of 16, at most 6 have a count above 256, and some group has exactly 6. `transitions`: every successor of a state below its generator's count is below that count; a state at or above the count has itself as every successor. `ptdf_pattern`: the 16 bus blocks named in one row are different.
All inputs are finite; a program needn't handle non-finite values.
Results may differ from a plain program's by a relative error of at most 0.0031.
Values may be sent and summed in bfloat16 or wider, within the bound.
No kernel may reach another device: no remote copies, remote signals or barrier semaphores. Data moves between devices by JAX's collectives and lax.ppermute only.
A program may use at most 128 MiB of HBM per device.

v0:
```python
import jax
import jax.numpy as jnp
from jax import lax
from jax.sharding import PartitionSpec as P

STATES = 512
BLK = 128
NNZB = 16


HIGHEST_PRECISION = lax.Precision.HIGHEST
STEP_SIZE = 1.0


def successor_matrix(trans_rows, state_span):
    columns = jnp.arange(state_span, dtype=jnp.int32)
    operator_table = jnp.zeros((trans_rows.shape[0], state_span, state_span), jnp.bfloat16)
    for branch in range(trans_rows.shape[1]):
        operator_table = operator_table + (
            trans_rows[:, branch, :state_span, None] == columns[None, None, :]
        ).astype(jnp.bfloat16)
    return operator_table


def smoothed_plan(level_rows, cost_rows, valid_rows, operator_table, hourly_prices):
    weights = valid_rows[None, :, None, :] * jnp.exp(
        hourly_prices[..., None] * level_rows[None, :, None, :] - cost_rows[None, :, None, :]
    )
    opening = weights[0] / jnp.sum(weights[0], axis=-1, keepdims=True)

    def forward(state_now, present_weight):
        pushed = jnp.einsum(
            "hkj,hjf->hkf",
            state_now.astype(jnp.bfloat16),
            operator_table,
            preferred_element_type=jnp.float32,
        )
        raised = pushed * present_weight
        scale_now = jnp.sum(raised, axis=-1, keepdims=True)
        state_next = raised / scale_now
        return (state_next, (state_next, scale_now))

    unused_state, (states_later, scales) = lax.scan(forward, opening, weights[1:])
    states_all = jnp.concatenate([opening[None], states_later], axis=0)

    def backward(back_now, inputs):
        present_weight, scale_now = inputs
        fetched_entries = (present_weight * back_now / scale_now).astype(jnp.bfloat16)
        back_prev = jnp.einsum(
            "fjc,fhc->fjh", fetched_entries, operator_table, preferred_element_type=jnp.float32
        )
        return (back_prev, back_prev)

    ones_back = jnp.ones_like(opening)
    unused_back, backs_earlier = lax.scan(backward, ones_back, (weights[1:], scales), reverse=True)
    backs_all = jnp.concatenate([backs_earlier, ones_back[None]], axis=0)
    combined_probability = states_all * backs_all
    return jnp.sum(combined_probability * level_rows[None, :, None, :], axis=-1) / jnp.sum(
        combined_probability, axis=-1
    )


def shards(
    bus_price,
    bus_demand,
    multipliers,
    line_limits,
    ptdf_blocks,
    ptdf_pattern,
    gen_bus,
    state_counts,
    transitions,
    state_level,
    state_cost,
):
    scn_all, hour_count, bus_dev = bus_price.shape
    scn_dev = bus_demand.shape[0]
    gen_index = lax.axis_index("gen")
    bus_index = lax.axis_index("bus")
    block_total = lax.axis_size("bus") * bus_dev // BLK
    local_bus = gen_bus - bus_index * bus_dev
    local_place = local_bus.astype(jnp.float32)
    onehot_all = (local_bus[:, None] == jnp.arange(bus_dev, dtype=jnp.int32)[None, :]).astype(
        jnp.float32
    )
    valid_all = (jnp.arange(STATES, dtype=jnp.int32)[None, :] < state_counts[:, None]).astype(
        jnp.float32
    )
    groups = (
        state_level,
        state_cost,
        valid_all,
        successor_matrix(transitions, STATES),
        onehot_all,
        local_place,
    )
    level_rows, cost_rows, valid_rows, operator_table, onehot_rows, place_rows = groups
    hourly_prices = jnp.einsum("rtb,gb->tgr", bus_price, onehot_rows, precision=HIGHEST_PRECISION)
    outputs = smoothed_plan(level_rows, cost_rows, valid_rows, operator_table, hourly_prices)
    plan = jnp.transpose(outputs, (2, 0, 1))
    place_copies = jnp.broadcast_to(
        place_rows[None, None, :], (lax.axis_size("gen"), 1, place_rows.shape[0])
    )
    received, received_place = (
        lax.all_to_all(plan, "gen", split_axis=0, concat_axis=2, tiled=True),
        lax.all_to_all(place_copies, "gen", split_axis=0, concat_axis=2, tiled=True),
    )
    placing_rows = (
        received_place[0, 0][:, None] == jnp.arange(bus_dev, dtype=jnp.float32)[None, :]
    ).astype(jnp.float32)
    injections = jnp.einsum("rtg,gb->rtb", received, placing_rows, precision=HIGHEST_PRECISION)
    row_total = scn_dev * hour_count
    network_row_block = (injections - bus_demand).astype(jnp.bfloat16).reshape(row_total, bus_dev)
    line_blocks = ptdf_blocks.shape[0]
    wanted = ptdf_pattern.reshape(-1)
    piece_cols = lax.all_gather(network_row_block, "bus", axis=1, tiled=True)
    block_count = piece_cols.shape[1] // BLK
    block_ids = jnp.arange(block_count, dtype=jnp.int32)
    chooser = (wanted[:, None] == block_ids[None, :]).astype(jnp.bfloat16)
    blocked = piece_cols.reshape(piece_cols.shape[0], block_count, BLK)
    picked_blocks = jnp.einsum("rjb,mj->rmb", blocked, chooser, preferred_element_type=jnp.float32)
    gathered = picked_blocks.astype(jnp.bfloat16).reshape(row_total, line_blocks, NNZB, BLK)
    flows = jnp.einsum("rlkb,lkbc->rlc", gathered, ptdf_blocks, preferred_element_type=jnp.float32)
    flow_lines = flows.reshape(scn_dev, hour_count, line_blocks * BLK)
    upper_old = multipliers[0]
    lower_old = multipliers[1]
    upper_new = jnp.maximum(0.0, upper_old + STEP_SIZE * (flow_lines - line_limits[None, None, :]))
    lower_new = jnp.maximum(0.0, lower_old + STEP_SIZE * (-flow_lines - line_limits[None, None, :]))
    change = (
        (upper_new - upper_old - (lower_new - lower_old))
        .astype(jnp.bfloat16)
        .reshape(row_total, line_blocks, BLK)
    )
    spread = jnp.einsum("rlc,lkbc->rlkb", change, ptdf_blocks, preferred_element_type=jnp.float32)
    placing = (
        ptdf_pattern[:, :, None] == jnp.arange(block_total, dtype=jnp.int32)[None, None, :]
    ).astype(jnp.float32)
    partial_change = jnp.einsum(
        "rlkb,lkj->rjb", spread, placing, precision=HIGHEST_PRECISION
    ).reshape(scn_dev, hour_count, block_total * BLK)
    own_change = lax.psum_scatter(partial_change, "bus", scatter_dimension=2, tiled=True)
    own_price = lax.dynamic_slice_in_dim(bus_price, gen_index * scn_dev, scn_dev, 0)
    new_share = own_price - own_change
    new_price = lax.all_gather(new_share, "gen", axis=0, tiled=True)
    return (jnp.stack([upper_new, lower_new]), new_price)


def solution(mesh):
    in_specs = (
        P(None, None, "bus"),
        P("gen", None, "bus"),
        P(None, "gen", None, "bus"),
        P("bus"),
        P("bus", None, None, None),
        P("bus", None),
        P(("gen", "bus")),
        P(("gen", "bus")),
        P(("gen", "bus"), None, None),
        P(("gen", "bus"), None),
        P(("gen", "bus"), None),
    )
    out_specs = (P(None, "gen", None, "bus"), P(None, None, "bus"))
    return jax.shard_map(shards, mesh=mesh, in_specs=in_specs, out_specs=out_specs, check_vma=False)
```

profile of v0, /device:TPU:0, one launch (start us, length us, event | category | flops | bytes accessed | tf_op | source)
XLA Modules:
  0.0 415.1 jit_solution(3284740924716350638)
XLA Ops:
  8.6 4.2 %all-to-all-start.1 = ((f32[4,1,16]{2,1,0:T(1,128)}), f32[4,1,16]{2,1,0:T(1,128)S(1)}, u32[]{:S(2)}, u32[]{:S(2)}) async-start(f32[4,1,16]{2,1,0:T(1,128)} %broadcast_in_dim.26), calls=%async_computation.1 | async-start | bytes 4096 | tf_op jit(solution)/shard_map/all_to_all | solution.py:106
  13.5 1.8 convolution_bitcast_fusion.1
  15.4 1.9 exponential_multiply_fusion
  18.4 3.1 slice.31
  21.5 3.2 broadcast.51.clone
  24.7 123.2 %while.32 = (s32[]{:T(128)}, bf16[16,16,512]{2,1,0:T(8,128)(2,1)S(1)}, f32[11,16,16,512]{3,2,1,0:T(8,128)}, f32[11,16,16,1]{2,1,3,0:T(8,128)}, f32[11,16,16,512]...) while((s32[]{:T(128)}, ...), condition=%wide.region_3.4_spmd.clone, body=%wide.region_1.3_spmd.clone.sunk | while | flops 185073408 | bytes 2731121 | solution.py:43
  24.7 9.7 %fusion.77 = (f32[16,16]{1,0:T(8,128)S(1)}, f32[16,16,512]{2,1,0:T(8,128)S(1)}) fusion(f32[11,16,16,512]{3,2,1,0:T(8,128)} %get-tuple-element.391, s32[]{:T(128)S(6)} %copy.85, s32[16,512]{1,0:T(8,128)S(1)} %get-tuple-element.394, s32[16,512]{1,0:T(8,128)S(1)} %get-tuple-element.393, s32[16,512]{1,0:T(8,128)S(1)} %get-tuple-element.392, ...), kind=kOutput, calls=%fused_computation.85.clone.1 | convolution fusion | flops 184811264 | bytes 1410052 | tf_op jit(solution)/shard_map/while/body/eval_jaxpr/hkj,hjf->hkf/dot_general | solution.py:32
  35.9 9.7 %fusion.77 = (f32[16,16]{1,0:T(8,128)S(1)}, f32[16,16,512]{2,1,0:T(8,128)S(1)}) fusion(f32[11,16,16,512]{3,2,1,0:T(8,128)} %get-tuple-element.391, s32[]{:T(128)S(6)} %copy.85, s32[16,512]{1,0:T(8,128)S(1)} %get-tuple-element.394, s32[16,512]{1,0:T(8,128)S(1)} %get-tuple-element.393, s32[16,512]{1,0:T(8,128)S(1)} %get-tuple-element.392, ...), kind=kOutput, calls=%fused_computation.85.clone.1 | convolution fusion | flops 184811264 | bytes 1410052 | tf_op jit(solution)/shard_map/while/body/eval_jaxpr/hkj,hjf->hkf/dot_general | solution.py:32
  47.1 9.7 %fusion.77 = (f32[16,16]{1,0:T(8,128)S(1)}, f32[16,16,512]{2,1,0:T(8,128)S(1)}) fusion(f32[11,16,16,512]{3,2,1,0:T(8,128)} %get-tuple-element.391, s32[]{:T(128)S(6)} %copy.85, s32[16,512]{1,0:T(8,128)S(1)} %get-tuple-element.394, s32[16,512]{1,0:T(8,128)S(1)} %get-tuple-element.393, s32[16,512]{1,0:T(8,128)S(1)} %get-tuple-element.392, ...), kind=kOutput, calls=%fused_computation.85.clone.1 | convolution fusion | flops 184811264 | bytes 1410052 | tf_op jit(solution)/shard_map/while/body/eval_jaxpr/hkj,hjf->hkf/dot_general | solution.py:32
  57.4 0.9 bitcast_dynamic-update-slice_fusion.6
  58.3 9.7 %fusion.77 = (f32[16,16]{1,0:T(8,128)S(1)}, f32[16,16,512]{2,1,0:T(8,128)S(1)}) fusion(f32[11,16,16,512]{3,2,1,0:T(8,128)} %get-tuple-element.391, s32[]{:T(128)S(6)} %copy.85, s32[16,512]{1,0:T(8,128)S(1)} %get-tuple-element.394, s32[16,512]{1,0:T(8,128)S(1)} %get-tuple-element.393, s32[16,512]{1,0:T(8,128)S(1)} %get-tuple-element.392, ...), kind=kOutput, calls=%fused_computation.85.clone.1 | convolution fusion | flops 184811264 | bytes 1410052 | tf_op jit(solution)/shard_map/while/body/eval_jaxpr/hkj,hjf->hkf/dot_general | solution.py:32
  68.6 1.0 bitcast_dynamic-update-slice_fusion.6
  69.6 9.7 %fusion.77 = (f32[16,16]{1,0:T(8,128)S(1)}, f32[16,16,512]{2,1,0:T(8,128)S(1)}) fusion(f32[11,16,16,512]{3,2,1,0:T(8,128)} %get-tuple-element.391, s32[]{:T(128)S(6)} %copy.85, s32[16,512]{1,0:T(8,128)S(1)} %get-tuple-element.394, s32[16,512]{1,0:T(8,128)S(1)} %get-tuple-element.393, s32[16,512]{1,0:T(8,128)S(1)} %get-tuple-element.392, ...), kind=kOutput, calls=%fused_computation.85.clone.1 | convolution fusion | flops 184811264 | bytes 1410052 | tf_op jit(solution)/shard_map/while/body/eval_jaxpr/hkj,hjf->hkf/dot_general | solution.py:32
  80.7 9.7 %fusion.77 = (f32[16,16]{1,0:T(8,128)S(1)}, f32[16,16,512]{2,1,0:T(8,128)S(1)}) fusion(f32[11,16,16,512]{3,2,1,0:T(8,128)} %get-tuple-element.391, s32[]{:T(128)S(6)} %copy.85, s32[16,512]{1,0:T(8,128)S(1)} %get-tuple-element.394, s32[16,512]{1,0:T(8,128)S(1)} %get-tuple-element.393, s32[16,512]{1,0:T(8,128)S(1)} %get-tuple-element.392, ...), kind=kOutput, calls=%fused_computation.85.clone.1 | convolution fusion | flops 184811264 | bytes 1410052 | tf_op jit(solution)/shard_map/while/body/eval_jaxpr/hkj,hjf->hkf/dot_general | solution.py:32
  91.9 9.7 %fusion.77 = (f32[16,16]{1,0:T(8,128)S(1)}, f32[16,16,512]{2,1,0:T(8,128)S(1)}) fusion(f32[11,16,16,512]{3,2,1,0:T(8,128)} %get-tuple-element.391, s32[]{:T(128)S(6)} %copy.85, s32[16,512]{1,0:T(8,128)S(1)} %get-tuple-element.394, s32[16,512]{1,0:T(8,128)S(1)} %get-tuple-element.393, s32[16,512]{1,0:T(8,128)S(1)} %get-tuple-element.392, ...), kind=kOutput, calls=%fused_computation.85.clone.1 | convolution fusion | flops 184811264 | bytes 1410052 | tf_op jit(solution)/shard_map/while/body/eval_jaxpr/hkj,hjf->hkf/dot_general | solution.py:32
  102.2 0.9 bitcast_dynamic-update-slice_fusion.6
  103.1 9.7 %fusion.77 = (f32[16,16]{1,0:T(8,128)S(1)}, f32[16,16,512]{2,1,0:T(8,128)S(1)}) fusion(f32[11,16,16,512]{3,2,1,0:T(8,128)} %get-tuple-element.391, s32[]{:T(128)S(6)} %copy.85, s32[16,512]{1,0:T(8,128)S(1)} %get-tuple-element.394, s32[16,512]{1,0:T(8,128)S(1)} %get-tuple-element.393, s32[16,512]{1,0:T(8,128)S(1)} %get-tuple-element.392, ...), kind=kOutput, calls=%fused_computation.85.clone.1 | convolution fusion | flops 184811264 | bytes 1410052 | tf_op jit(solution)/shard_map/while/body/eval_jaxpr/hkj,hjf->hkf/dot_general | solution.py:32
  113.4 0.9 bitcast_dynamic-update-slice_fusion.6
  114.3 9.7 %fusion.77 = (f32[16,16]{1,0:T(8,128)S(1)}, f32[16,16,512]{2,1,0:T(8,128)S(1)}) fusion(f32[11,16,16,512]{3,2,1,0:T(8,128)} %get-tuple-element.391, s32[]{:T(128)S(6)} %copy.85, s32[16,512]{1,0:T(8,128)S(1)} %get-tuple-element.394, s32[16,512]{1,0:T(8,128)S(1)} %get-tuple-element.393, s32[16,512]{1,0:T(8,128)S(1)} %get-tuple-element.392, ...), kind=kOutput, calls=%fused_computation.85.clone.1 | convolution fusion | flops 184811264 | bytes 1410052 | tf_op jit(solution)/shard_map/while/body/eval_jaxpr/hkj,hjf->hkf/dot_general | solution.py:32
  124.6 0.9 bitcast_dynamic-update-slice_fusion.6
  125.5 9.7 %fusion.77 = (f32[16,16]{1,0:T(8,128)S(1)}, f32[16,16,512]{2,1,0:T(8,128)S(1)}) fusion(f32[11,16,16,512]{3,2,1,0:T(8,128)} %get-tuple-element.391, s32[]{:T(128)S(6)} %copy.85, s32[16,512]{1,0:T(8,128)S(1)} %get-tuple-element.394, s32[16,512]{1,0:T(8,128)S(1)} %get-tuple-element.393, s32[16,512]{1,0:T(8,128)S(1)} %get-tuple-element.392, ...), kind=kOutput, calls=%fused_computation.85.clone.1 | convolution fusion | flops 184811264 | bytes 1410052 | tf_op jit(solution)/shard_map/while/body/eval_jaxpr/hkj,hjf->hkf/dot_general | solution.py:32
  135.8 0.9 bitcast_dynamic-update-slice_fusion.6
  136.8 9.7 %fusion.77 = (f32[16,16]{1,0:T(8,128)S(1)}, f32[16,16,512]{2,1,0:T(8,128)S(1)}) fusion(f32[11,16,16,512]{3,2,1,0:T(8,128)} %get-tuple-element.391, s32[]{:T(128)S(6)} %copy.85, s32[16,512]{1,0:T(8,128)S(1)} %get-tuple-element.394, s32[16,512]{1,0:T(8,128)S(1)} %get-tuple-element.393, s32[16,512]{1,0:T(8,128)S(1)} %get-tuple-element.392, ...), kind=kOutput, calls=%fused_computation.85.clone.1 | convolution fusion | flops 184811264 | bytes 1410052 | tf_op jit(solution)/shard_map/while/body/eval_jaxpr/hkj,hjf->hkf/dot_general | solution.py:32
  148.8 3.3 broadcast.51
  152.1 120.3 %while.33 = (s32[]{:T(128)}, f32[16,16,512]{2,1,0:T(8,128)}, f32[11,16,16,512]{3,2,1,0:T(8,128)}, f32[11,16,16,512]{3,2,1,0:T(8,128)}, f32[11,16,16,1]{2,1,3,0:T...) while((s32[]{:T(128)}, f32[16,16,512]{2,1,0:T(8,128)}, ...), condition=%wide.region_5.6_spmd.clone, body=%wide.region_4.5_spmd.clone.sunk | while | flops 184942592 | bytes 3248245 | solution.py:55
  152.1 1.0 copy.103
  153.9 9.2 %bitcast_dynamic-update-slice_fusion.8 = (f32[11,16,16,512]{3,2,1,0:T(8,128)}, f32[16,16,512]{2,1,0:T(8,128)}) fusion(f32[11,16,16,512]{3,2,1,0:T(8,128)} %get-tuple-element.408, s32[]{:T(128)S(6)} %sub.133, s32[16,512]{1,0:T(8,128)S(1)} %get-tuple-element.423, s32[16,512]{1,0:T(8,128)S(1)} %get-tuple-element.422, ...), kind=kOutput, calls=%fused_computation.31.clone.1 | convolution fusion | flops 184942592 | bytes 2197504 | tf_op jit(solution)/shard_map/while/body/eval_jaxpr/fjc,fhc->fjh/dot_general | solution.py:49
  163.1 1.0 copy.103
  164.8 9.2 %bitcast_dynamic-update-slice_fusion.8 = (f32[11,16,16,512]{3,2,1,0:T(8,128)}, f32[16,16,512]{2,1,0:T(8,128)}) fusion(f32[11,16,16,512]{3,2,1,0:T(8,128)} %get-tuple-element.408, s32[]{:T(128)S(6)} %sub.133, s32[16,512]{1,0:T(8,128)S(1)} %get-tuple-element.423, s32[16,512]{1,0:T(8,128)S(1)} %get-tuple-element.422, ...), kind=kOutput, calls=%fused_computation.31.clone.1 | convolution fusion | flops 184942592 | bytes 2197504 | tf_op jit(solution)/shard_map/while/body/eval_jaxpr/fjc,fhc->fjh/dot_general | solution.py:49
  174.0 1.0 copy.103
  175.7 9.2 %bitcast_dynamic-update-slice_fusion.8 = (f32[11,16,16,512]{3,2,1,0:T(8,128)}, f32[16,16,512]{2,1,0:T(8,128)}) fusion(f32[11,16,16,512]{3,2,1,0:T(8,128)} %get-tuple-element.408, s32[]{:T(128)S(6)} %sub.133, s32[16,512]{1,0:T(8,128)S(1)} %get-tuple-element.423, s32[16,512]{1,0:T(8,128)S(1)} %get-tuple-element.422, ...), kind=kOutput, calls=%fused_computation.31.clone.1 | convolution fusion | flops 184942592 | bytes 2197504 | tf_op jit(solution)/shard_map/while/body/eval_jaxpr/fjc,fhc->fjh/dot_general | solution.py:49
  184.9 1.0 copy.103
  186.7 9.2 %bitcast_dynamic-update-slice_fusion.8 = (f32[11,16,16,512]{3,2,1,0:T(8,128)}, f32[16,16,512]{2,1,0:T(8,128)}) fusion(f32[11,16,16,512]{3,2,1,0:T(8,128)} %get-tuple-element.408, s32[]{:T(128)S(6)} %sub.133, s32[16,512]{1,0:T(8,128)S(1)} %get-tuple-element.423, s32[16,512]{1,0:T(8,128)S(1)} %get-tuple-element.422, ...), kind=kOutput, calls=%fused_computation.31.clone.1 | convolution fusion | flops 184942592 | bytes 2197504 | tf_op jit(solution)/shard_map/while/body/eval_jaxpr/fjc,fhc->fjh/dot_general | solution.py:49
  195.9 1.0 copy.103
  197.6 9.2 %bitcast_dynamic-update-slice_fusion.8 = (f32[11,16,16,512]{3,2,1,0:T(8,128)}, f32[16,16,512]{2,1,0:T(8,128)}) fusion(f32[11,16,16,512]{3,2,1,0:T(8,128)} %get-tuple-element.408, s32[]{:T(128)S(6)} %sub.133, s32[16,512]{1,0:T(8,128)S(1)} %get-tuple-element.423, s32[16,512]{1,0:T(8,128)S(1)} %get-tuple-element.422, ...), kind=kOutput, calls=%fused_computation.31.clone.1 | convolution fusion | flops 184942592 | bytes 2197504 | tf_op jit(solution)/shard_map/while/body/eval_jaxpr/fjc,fhc->fjh/dot_general | solution.py:49
  206.8 1.0 copy.103
  208.6 9.2 %bitcast_dynamic-update-slice_fusion.8 = (f32[11,16,16,512]{3,2,1,0:T(8,128)}, f32[16,16,512]{2,1,0:T(8,128)}) fusion(f32[11,16,16,512]{3,2,1,0:T(8,128)} %get-tuple-element.408, s32[]{:T(128)S(6)} %sub.133, s32[16,512]{1,0:T(8,128)S(1)} %get-tuple-element.423, s32[16,512]{1,0:T(8,128)S(1)} %get-tuple-element.422, ...), kind=kOutput, calls=%fused_computation.31.clone.1 | convolution fusion | flops 184942592 | bytes 2197504 | tf_op jit(solution)/shard_map/while/body/eval_jaxpr/fjc,fhc->fjh/dot_general | solution.py:49
  217.7 1.0 copy.103
  219.5 9.2 %bitcast_dynamic-update-slice_fusion.8 = (f32[11,16,16,512]{3,2,1,0:T(8,128)}, f32[16,16,512]{2,1,0:T(8,128)}) fusion(f32[11,16,16,512]{3,2,1,0:T(8,128)} %get-tuple-element.408, s32[]{:T(128)S(6)} %sub.133, s32[16,512]{1,0:T(8,128)S(1)} %get-tuple-element.423, s32[16,512]{1,0:T(8,128)S(1)} %get-tuple-element.422, ...), kind=kOutput, calls=%fused_computation.31.clone.1 | convolution fusion | flops 184942592 | bytes 2197504 | tf_op jit(solution)/shard_map/while/body/eval_jaxpr/fjc,fhc->fjh/dot_general | solution.py:49
  228.7 1.0 copy.103
  230.4 9.2 %bitcast_dynamic-update-slice_fusion.8 = (f32[11,16,16,512]{3,2,1,0:T(8,128)}, f32[16,16,512]{2,1,0:T(8,128)}) fusion(f32[11,16,16,512]{3,2,1,0:T(8,128)} %get-tuple-element.408, s32[]{:T(128)S(6)} %sub.133, s32[16,512]{1,0:T(8,128)S(1)} %get-tuple-element.423, s32[16,512]{1,0:T(8,128)S(1)} %get-tuple-element.422, ...), kind=kOutput, calls=%fused_computation.31.clone.1 | convolution fusion | flops 184942592 | bytes 2197504 | tf_op jit(solution)/shard_map/while/body/eval_jaxpr/fjc,fhc->fjh/dot_general | solution.py:49
  239.6 1.0 copy.103
  241.4 9.2 %bitcast_dynamic-update-slice_fusion.8 = (f32[11,16,16,512]{3,2,1,0:T(8,128)}, f32[16,16,512]{2,1,0:T(8,128)}) fusion(f32[11,16,16,512]{3,2,1,0:T(8,128)} %get-tuple-element.408, s32[]{:T(128)S(6)} %sub.133, s32[16,512]{1,0:T(8,128)S(1)} %get-tuple-element.423, s32[16,512]{1,0:T(8,128)S(1)} %get-tuple-element.422, ...), kind=kOutput, calls=%fused_computation.31.clone.1 | convolution fusion | flops 184942592 | bytes 2197504 | tf_op jit(solution)/shard_map/while/body/eval_jaxpr/fjc,fhc->fjh/dot_general | solution.py:49
  250.6 1.0 copy.103
  252.3 9.2 %bitcast_dynamic-update-slice_fusion.8 = (f32[11,16,16,512]{3,2,1,0:T(8,128)}, f32[16,16,512]{2,1,0:T(8,128)}) fusion(f32[11,16,16,512]{3,2,1,0:T(8,128)} %get-tuple-element.408, s32[]{:T(128)S(6)} %sub.133, s32[16,512]{1,0:T(8,128)S(1)} %get-tuple-element.423, s32[16,512]{1,0:T(8,128)S(1)} %get-tuple-element.422, ...), kind=kOutput, calls=%fused_computation.31.clone.1 | convolution fusion | flops 184942592 | bytes 2197504 | tf_op jit(solution)/shard_map/while/body/eval_jaxpr/fjc,fhc->fjh/dot_general | solution.py:49
  261.5 1.0 copy.103
  263.3 9.2 %bitcast_dynamic-update-slice_fusion.8 = (f32[11,16,16,512]{3,2,1,0:T(8,128)}, f32[16,16,512]{2,1,0:T(8,128)}) fusion(f32[11,16,16,512]{3,2,1,0:T(8,128)} %get-tuple-element.408, s32[]{:T(128)S(6)} %sub.133, s32[16,512]{1,0:T(8,128)S(1)} %get-tuple-element.423, s32[16,512]{1,0:T(8,128)S(1)} %get-tuple-element.422, ...), kind=kOutput, calls=%fused_computation.31.clone.1 | convolution fusion | flops 184942592 | bytes 2197504 | tf_op jit(solution)/shard_map/while/body/eval_jaxpr/fjc,fhc->fjh/dot_general | solution.py:49
  272.5 5.2 %fusion.39 = (f32[12,16,16]{2,1,0:T(8,128)S(1)}, f32[12,16,16]{2,1,0:T(8,128)S(1)}) fusion(f32[11,16,16,512]{3,2,1,0:T(8,128)} %get-tuple-element.159, f32[11,16,16,512]{3,2,1,0:T(8,128)} %get-tuple-element.157, f32[1,16,16,512]{3,2,1,0:T(8,128)} %slice_divide_fusion, f32[16,512]{1,0:T(8,128)S(1)} %copy-done.3), kind=kLoop, calls=%fused_computation.45 | loop fusion | flops 7858176 | bytes 12115968 | tf_op jit(solution)/shard_map/reduce_sum | solution.py:58
  278.5 3.3 all-to-all-start
  281.9 1.7 fusion.67
  287.5 31.7 %all_gather.6 = bf16[48,4096]{1,0:T(8,128)(2,1)S(1)} all-gather(bf16[48,512]{1,0:T(8,128)(2,1)S(1)} %reshape.88), channel_id=1, replica_groups=mesh['gen'=4,'bus'=8] {'bus'}, dimensions={1}, use_global_device_ids=true | all-gather | bytes 442368 | tf_op jit(solution)/shard_map/all_gather | solution.py:116
  321.3 1.0 reshape.91
  322.3 1.9 add_maximum_fusion.1
  324.2 1.6 squeeze.27
  325.8 1.7 squeeze.26
  327.5 2.2 convolution_bitcast_fusion
  329.7 2.5 fusion.40
  332.2 2.2 reshape.92
  334.5 1.0 constant_dynamic-slice_fusion
  335.5 1.0 pad_maximum_fusion
  337.3 61.8 %reduce-scatter.2.cloned.1.call-done = f32[4,12,512]{2,1,0:T(8,128)} async-done(((f32[4,12,4096]{2,1,0:T(8,128)}), f32[4,12,512]{2,1,0:T(8,128)}) %reduce-scatter.2.cloned.1.call-update) | async-done | bytes 98320 | tf_op jit(solution)/shard_map/reduce_scatter | solution.py:141
  399.2 0.9 copy_subtract_fusion
  400.1 7.1 %all_gather.7 = f32[16,12,512]{2,1,0:T(8,128)S(1)} all-gather(f32[4,12,512]{2,1,0:T(8,128)S(1)} %copy_subtract_fusion), channel_id=1, replica_groups=mesh['gen'=4,'bus'=8] {'gen'}, dimensions={0}, use_global_device_ids=true | all-gather | bytes 491520 | tf_op jit(solution)/shard_map/all_gather | solution.py:144
  407.3 1.0 copy.46
  (74 shorter events, 30.7 us)
Async XLA Ops:
  7.2 312.6 %copy-start = (bf16[6,16,128,128]{3,2,1,0:T(8,128)(2,1)S(1)}, bf16[6,16,128,128]{3,2,1,0:T(8,128)(2,1)}, u32[]{:S(2)}) copy-start(bf16[6,16,128,128]{3,2,1,0:T(8,128)(2,1)} %param.19) | copy-start | bytes 9437188
  8.6 270.0 %all-to-all-start.1 = ((f32[4,1,16]{2,1,0:T(1,128)}), f32[4,1,16]{2,1,0:T(1,128)S(1)}, u32[]{:S(2)}, u32[]{:S(2)}) async-start(f32[4,1,16]{2,1,0:T(1,128)} %broadcast_in_dim.26), calls=%async_computation.1 | async-start | bytes 4096 | tf_op jit(solution)/shard_map/all_to_all | solution.py:106
  17.5 4.0 copy-start.4
  152.1 120.3 %copy-start.3 = (f32[16,512]{1,0:T(8,128)S(1)}, f32[16,512]{1,0:T(8,128)}, u32[]{:S(2)}) copy-start(f32[16,512]{1,0:T(8,128)} %param.24) | copy-start | bytes 98308
  272.5 11.1 %copy-start.6 = (s32[6,16]{1,0:T(8,128)S(1)}, s32[6,16]{1,0:T(8,128)}, u32[]{:S(2)}) copy-start(s32[6,16]{1,0:T(8,128)} %param.20) | copy-start | bytes 1156
  272.5 14.7 %copy-start.2 = (f32[4,12,512]{2,0,1:T(4,128)S(1)}, f32[4,12,512]{2,0,1:T(4,128)}, u32[]{:S(2)}) copy-start(f32[4,12,512]{2,0,1:T(4,128)} %param.16) | copy-start | bytes 294916
  278.5 7.1 %all-to-all-start = ((f32[4,1,768]{2,1,0:T(1,128)}), f32[4,1,768]{2,1,0:T(1,128)S(1)}, u32[]{:S(2)}, u32[]{:S(2)}) async-start(f32[4,1,768]{2,1,0:T(1,128)} %reshape.110), calls=%async_computation | async-start | bytes 24576 | tf_op jit(solution)/shard_map/all_to_all | solution.py:105
  281.8 40.4 %copy-start.5 = (f32[768]{0:T(1024)S(1)}, f32[768]{0:T(1024)}, u32[]{:S(2)}) copy-start(f32[768]{0:T(1024)} %param.18) | copy-start | bytes 9220
  281.8 117.3 %reduce-scatter.2.cloned.1.call-start = ((), (), s32[]{:S(2)}) async-start(), calls=%async_computation.3 | async-start | bytes 1179648 | tf_op jit(solution)/shard_map/reduce_scatter | solution.py:141
  325.8 9.6 %copy-start.1 = (f32[1,4,12,768]{3,2,1,0:T(8,128)S(1)}, f32[1,4,12,768]{3,2,1,0:T(8,128)}, u32[]{:S(2)}) copy-start(f32[1,4,12,768]{3,2,1,0:T(8,128)} %get-tuple-element.250) | copy-start | bytes 442372
Sparse Core Ops, SparseCore 0:
  334.6 64.5 reduce-scatter.1
where the time goes:
time: 418 us; the launch traced here: 415 us
  matrix products  216 us (52%)
  waiting for transfers between devices  62.6 us (15%)
  local copies, waits for them, and re-layouts  51 us (12%)
  blocking collectives  38.9 us (9%)
  other arithmetic  25.1 us (6%)
  between operations  14.2 us (3%)
  starting transfers between devices  7.55 us (2%)
    dot_general x11, matrix products, forward(): jnp.einsum('hkj,hjf->hkf', state_now.astype(jnp.bfloat16), operator_table...  106 us
    dot_general x11, matrix products, backward(): jnp.einsum('fjc,fhc->fjh', fetched_entries, operator_table, preferred_ele...  101 us
    reduce_scatter x1, waiting for transfers between devices, shards(): lax.psum_scatter(partial_change, 'bus', scatter_dimension=2, tiled=True)  61.8 us
    all_gather x1, blocking collectives, shards(): piece_cols = lax.all_gather(network_row_block, 'bus', axis=1, tiled=True)  31.7 us
    while x11, local copies, waits for them, and re-layouts  11.5 us
    dynamic_update_slice x11, other arithmetic, smoothed_plan(): lax.scan(forward, opening, weights[1:])  10.2 us
  transfers between devices with their start and end apart: 3, of which 2 were waited for; matrix products, arithmetic and copies ran while one was open for 65% of the time, Pallas kernels for 0%

commit v1 on v0

v1 whole, which is shorter than its diff:
```python
import functools

import jax
import jax.numpy as jnp
from jax import lax
from jax.experimental import pallas as pl
from jax.experimental.pallas import tpu as pltpu
from jax.sharding import PartitionSpec as P

STATES = 512
HALF = 256
BLK = 128
NNZB = 16
GROUP = 16
BIG_GROUP = 6
LANES = 128
SUBLANES = 8
EXACT = lax.Precision.HIGHEST


def plan_kernel(
    counts_smem,
    bus_smem,
    price_ref,
    trans_ref,
    level_ref,
    cost_ref,
    out_ref,
    order,
    level_slot,
    cost_slot,
    gen_price,
    big_table,
    small_table,
    big_state,
    small_state,
):
    scn, hours, bus_dev = price_ref.shape
    gens = level_ref.shape[0]
    big_total = BIG_GROUP * (gens // GROUP)
    parts = out_ref.shape[0]
    scn_dev = scn // parts
    per_row = LANES // gens

    def place(gen, taken):
        big = (counts_smem[gen] > HALF).astype(jnp.int32)
        slot = jnp.where(big == 1, taken, gens - 1 - (gen - taken))
        order[slot] = gen
        return taken + big

    lax.fori_loop(0, gens, place, jnp.int32(0))

    lane = lax.broadcasted_iota(jnp.int32, (1, LANES), 1)
    local_row = jnp.zeros((1, LANES), jnp.int32)
    bus_row = jnp.zeros((1, LANES), jnp.int32)
    for slot in range(gens):
        local = lax.rem(bus_smem[order[slot]], bus_dev)
        local_row = jnp.where(lane == slot, local, local_row)
        bus_row = jnp.where(lane == slot, local, bus_row)
    chooser = (
        lax.broadcasted_iota(jnp.int32, (bus_dev, LANES), 0) == local_row
    ).astype(jnp.float32)
    for n in range(scn):
        gen_price[n] = lax.dot_general(
            price_ref[n],
            chooser,
            (((1,), (0,)), ((), ())),
            precision=EXACT,
            preferred_element_type=jnp.float32,
        )

    state_ids = lax.broadcasted_iota(jnp.int32, (1, STATES), 1)
    spans = []
    for slot in range(gens):
        gen = order[slot]
        span = STATES if slot < big_total else HALF
        spans.append(span)
        level_slot[slot] = jnp.broadcast_to(level_ref[pl.ds(gen, 1), :], (SUBLANES, STATES))
        cost_row = jnp.where(state_ids < counts_smem[gen], cost_ref[pl.ds(gen, 1), :], 1e30)
        cost_slot[slot] = jnp.broadcast_to(cost_row, (SUBLANES, STATES))
        successors = trans_ref[gen]
        table = big_table.at[slot] if slot < big_total else small_table.at[slot - big_total]
        for first in range(0, span, HALF):
            shifted = (successors[:, :span] - first).astype(jnp.float32).astype(jnp.bfloat16)
            rows = lax.broadcasted_iota(jnp.int32, (HALF, span), 0).astype(jnp.float32).astype(jnp.bfloat16)
            one = jnp.ones((HALF, span), jnp.bfloat16)
            none = jnp.zeros((HALF, span), jnp.bfloat16)
            total = none
            for branch in range(successors.shape[0]):
                total = total + jnp.where(rows == shifted[branch : branch + 1, :], one, none)
            table[pl.ds(first, HALF), :] = total

    def repeat_rows(block, copies):
        return block if copies == 1 else jnp.concatenate([block] * copies, axis=0)

    outs = [jnp.zeros((scn, LANES), jnp.float32) for _ in range(-(-hours // per_row))]
    for hour in range(hours - 1, -1, -1):
        chains = hours - 1 - hour
        for slot in range(gens):
            span = spans[slot]
            if slot < big_total:
                state, table = big_state.at[slot], big_table.at[slot]
            else:
                state, table = small_state.at[slot - big_total], small_table.at[slot - big_total]
            level = repeat_rows(level_slot[slot][:, :span], scn // SUBLANES)
            cost = repeat_rows(cost_slot[slot][:, :span], scn // SUBLANES)
            price = gen_price[:, hour, slot : slot + 1]
            weight = jnp.exp(price * level - cost)
            base = weight if chains == 0 else weight * state[:scn, :]
            total = jnp.sum(base, axis=-1, keepdims=True)
            if hour > 0:
                share = 1.0 / total
                base = base * share
                weight = weight * share
                pieces = [base.astype(jnp.bfloat16)]
                for chain in range(chains):
                    pieces.append(
                        (weight * state[(chain + 1) * scn : (chain + 2) * scn, :]).astype(jnp.bfloat16)
                    )
                pieces.append((base * level).astype(jnp.bfloat16))
                moved = jnp.dot(
                    jnp.concatenate(pieces, axis=0), table[...], preferred_element_type=jnp.float32
                )
                state[: (chains + 2) * scn, :] = moved
            else:
                for at in range(hours):
                    if at == 0:
                        marked = base * level
                    else:
                        chain = hours - 1 - at
                        marked = weight * state[(chain + 1) * scn : (chain + 2) * scn, :]
                    mean = jnp.sum(marked, axis=-1, keepdims=True) / total
                    here = lane == (at % per_row) * gens + slot
                    outs[at // per_row] = jnp.where(here, mean, outs[at // per_row])
    for slot in range(gens):
        here = lane == (hours % per_row) * gens + slot
        bus = jnp.sum(jnp.where(lane == slot, bus_row, 0)).astype(jnp.float32)
        outs[-1] = jnp.where(here, bus, outs[-1])
    for part in range(parts):
        for row, block in enumerate(outs):
            out_ref[part, row] = block[part * scn_dev : (part + 1) * scn_dev, :]


def run_plan(state_counts, gen_bus, bus_price, transitions, state_level, state_cost, parts):
    scn, hours, _ = bus_price.shape
    gens = state_level.shape[0]
    big_total = BIG_GROUP * (gens // GROUP)
    rows = -(-hours // (LANES // gens))
    smem = pl.BlockSpec(memory_space=pltpu.SMEM)
    vmem = pl.BlockSpec(memory_space=pltpu.VMEM)
    return pl.pallas_call(
        plan_kernel,
        out_shape=jax.ShapeDtypeStruct((parts, rows, scn // parts, LANES), jnp.float32),
        in_specs=[smem, smem, vmem, vmem, vmem, vmem],
        out_specs=vmem,
        scratch_shapes=[
            pltpu.SMEM((gens,), jnp.int32),
            pltpu.VMEM((gens, SUBLANES, STATES), jnp.float32),
            pltpu.VMEM((gens, SUBLANES, STATES), jnp.float32),
            pltpu.VMEM((scn, hours, LANES), jnp.float32),
            pltpu.VMEM((big_total, STATES, STATES), jnp.bfloat16),
            pltpu.VMEM((gens - big_total, HALF, HALF), jnp.bfloat16),
            pltpu.VMEM((big_total, (hours + 1) * scn, STATES), jnp.float32),
            pltpu.VMEM((gens - big_total, (hours + 1) * scn, HALF), jnp.float32),
        ],
        compiler_params=pltpu.CompilerParams(vmem_limit_bytes=56 * 2**20),
        name="plan",
    )(state_counts, gen_bus, bus_price, transitions, state_level, state_cost)


def shards(
    bus_price,
    bus_demand,
    multipliers,
    line_limits,
    ptdf_blocks,
    ptdf_pattern,
    gen_bus,
    state_counts,
    transitions,
    state_level,
    state_cost,
):
    scn_dev, hours, bus_dev = bus_demand.shape
    gen_index = lax.axis_index("gen")
    parts = lax.axis_size("gen")
    gens = state_level.shape[0]
    per_row = LANES // gens
    block_total = lax.axis_size("bus") * bus_dev // BLK
    plan = run_plan(
        state_counts, gen_bus, bus_price, transitions, state_level, state_cost, parts
    )
    received = lax.all_to_all(plan, "gen", split_axis=0, concat_axis=0, tiled=True)
    rows = received.shape[1]
    spread = received.reshape(parts, rows, scn_dev, per_row, gens)
    places = spread[:, hours // per_row, 0, hours % per_row, :].reshape(-1)
    hourly = jnp.transpose(spread, (2, 1, 3, 0, 4)).reshape(scn_dev, rows * per_row, parts * gens)[:, :hours]
    placing_rows = (places[:, None] == jnp.arange(bus_dev, dtype=jnp.float32)[None, :]).astype(jnp.float32)
    injections = jnp.einsum("rtg,gb->rtb", hourly, placing_rows, precision=EXACT)
    row_total = scn_dev * hours
    network_row_block = (injections - bus_demand).astype(jnp.bfloat16).reshape(row_total, bus_dev)
    line_blocks = ptdf_blocks.shape[0]
    wanted = ptdf_pattern.reshape(-1)
    piece_cols = lax.all_gather(network_row_block, "bus", axis=1, tiled=True)
    block_count = piece_cols.shape[1] // BLK
    block_ids = jnp.arange(block_count, dtype=jnp.int32)
    chooser = (wanted[:, None] == block_ids[None, :]).astype(jnp.bfloat16)
    blocked = piece_cols.reshape(piece_cols.shape[0], block_count, BLK)
    picked_blocks = jnp.einsum("rjb,mj->rmb", blocked, chooser, preferred_element_type=jnp.float32)
    gathered = picked_blocks.astype(jnp.bfloat16).reshape(row_total, line_blocks, NNZB, BLK)
    flows = jnp.einsum("rlkb,lkbc->rlc", gathered, ptdf_blocks, preferred_element_type=jnp.float32)
    flow_lines = flows.reshape(scn_dev, hours, line_blocks * BLK)
    upper_old = multipliers[0]
    lower_old = multipliers[1]
    upper_new = jnp.maximum(0.0, upper_old + (flow_lines - line_limits[None, None, :]))
    lower_new = jnp.maximum(0.0, lower_old + (-flow_lines - line_limits[None, None, :]))
    change = (
        (upper_new - upper_old - (lower_new - lower_old))
        .astype(jnp.bfloat16)
        .reshape(row_total, line_blocks, BLK)
    )
    spread = jnp.einsum("rlc,lkbc->rlkb", change, ptdf_blocks, preferred_element_type=jnp.float32)
    placing = (
        ptdf_pattern[:, :, None] == jnp.arange(block_total, dtype=jnp.int32)[None, None, :]
    ).astype(jnp.float32)
    partial_change = jnp.einsum("rlkb,lkj->rjb", spread, placing, precision=EXACT).reshape(
        scn_dev, hours, block_total * BLK
    )
    own_change = lax.psum_scatter(partial_change, "bus", scatter_dimension=2, tiled=True)
    own_price = lax.dynamic_slice_in_dim(bus_price, gen_index * scn_dev, scn_dev, 0)
    new_share = own_price - own_change
    new_price = lax.all_gather(new_share, "gen", axis=0, tiled=True)
    return (jnp.stack([upper_new, lower_new]), new_price)


def solution(mesh):
    in_specs = (
        P(None, None, "bus"),
        P("gen", None, "bus"),
        P(None, "gen", None, "bus"),
        P("bus"),
        P("bus", None, None, None),
        P("bus", None),
        P(("gen", "bus")),
        P(("gen", "bus")),
        P(("gen", "bus"), None, None),
        P(("gen", "bus"), None),
        P(("gen", "bus"), None),
    )
    out_specs = (P(None, "gen", None, "bus"), P(None, None, "bus"))
    return jax.shard_map(shards, mesh=mesh, in_specs=in_specs, out_specs=out_specs, check_vma=False)
```

time: 418 us -> 166 us (0.40)
  matrix products: 216 us -> 6.26 us
  local copies, waits for them, and re-layouts: 51 us -> 14.5 us
  other arithmetic: 25.1 us -> 2.91 us
  Pallas kernels: 0 us -> 19.7 us
    dot_general x25 -> x2, matrix products: 212 us -> 2.84 us  [the longest x1 2.56 us: shards(): jnp.einsum('rlkb,lkj->rjb', spread, placing, precision=EXACT)]
    pallas_call x0 -> x1, Pallas kernels: none -> 19.7 us  [run_plan(): pl.pallas_call(plan_kernel, out_shape=jax.ShapeDtypeStruct((parts, rows,...]
    while x11 -> x0, local copies, waits for them, and re-layouts: 11.5 us -> none
    dynamic_update_slice x11 -> x0, other arithmetic: 10.2 us -> none  [smoothed_plan(): lax.scan(forward, opening, weights[1:])]
    div x12 -> x0, local copies, waits for them, and re-layouts: 7.78 us -> none  [the longest x11 7.67 us: backward(): present_weight * back_now / scale_now]
    dynamic_update_slice x11 -> x0, local copies, waits for them, and re-layouts: 6.66 us -> none  [smoothed_plan(): lax.scan(forward, opening, weights[1:])]
    another operation x2 -> x0, local copies, waits for them, and re-layouts: 6.48 us -> none
    reduce_sum x2 -> x0, other arithmetic: 5.32 us -> none  [the longest x1 5.21 us: smoothed_plan(): jnp.sum(combined_probability, axis=-1)]
  transfers between devices with their start and end apart: 3 -> 2, of which waited for: 2 -> 2; matrix products, arithmetic and copies ran while one was open for 65% -> 2% of each run, Pallas kernels for 0% -> 0%
where the time goes in v1:
time: 166 us
  waiting for transfers between devices  65.2 us (39%)
  blocking collectives  38.9 us (23%)
  Pallas kernels  19.7 us (12%)
  local copies, waits for them, and re-layouts  14.5 us (9%)
  between operations  14.2 us (9%)
  matrix products  6.26 us (4%)
  starting transfers between devices  4.25 us (3%)
  other arithmetic  2.91 us (2%)
    reduce_scatter x1, waiting for transfers between devices, shards(): lax.psum_scatter(partial_change, 'bus', scatter_dimension=2, tiled=True)  63.1 us
    all_gather x1, blocking collectives, shards(): piece_cols = lax.all_gather(network_row_block, 'bus', axis=1, tiled=True)  31.8 us
    pallas_call x1, Pallas kernels, run_plan(): pl.pallas_call(plan_kernel, out_shape=jax.ShapeDtypeStruct((parts, rows,...  19.7 us
    all_gather x1, blocking collectives, shards(): new_price = lax.all_gather(new_share, 'gen', axis=0, tiled=True)  7.14 us
    unnamed x17, local copies, waits for them, and re-layouts  5.77 us
    all_to_all x1, starting transfers between devices, shards(): lax.all_to_all(plan, 'gen', split_axis=0, concat_axis=0, tiled=True)  4.24 us
  transfers between devices with their start and end apart: 2, of which 2 were waited for; matrix products, arithmetic and copies ran while one was open for 2% of the time, Pallas kernels for 0%

profile of v1, /device:TPU:0, one launch (start us, length us, event | category | flops | bytes accessed | tf_op | source)
XLA Modules:
  0.0 165.9 jit_solution(17910953293965933785)
XLA Ops:
  7.2 0.0 copy-start
  7.2 0.0 copy-start.5
  7.2 0.0 copy-start.3
  7.2 2.2 %copy.37.price_ref = f32[16,12,512]{2,1,0:T(8,128)} copy(f32[16,12,512]{2,0,1:T(8,128)} %param.11) | data formatting | bytes 786432 | tf_op args[0]
  9.4 1.6 copy.38.trans_ref
  11.0 19.7 %plan.1 = f32[4,2,4,128]{3,2,1,0:T(4,128)} custom-call(s32[16]{0:T(128)} %counts_smem.1, s32[16]{0:T(128)} %bus_smem.1, f32[16,12,512]{2,1,0:T(8,128)} %copy.37.price_ref, s32[16,3,512]{2,1,0:T(4,128)} %copy.38.trans_ref, f32[16,512]{1,0:T(8,128)} %level_ref.1, f32[16,512]{1,0:T(8,128)} %cost_ref.1), custom_call_target="tpu_custom_call" | custom-call | tf_op jit(solution)/shard_map/plan/pallas_call | solution.py:151
  30.7 4.2 %all-to-all-start = ((f32[4,2,4,128]{3,2,1,0:T(4,128)}), f32[4,2,4,128]{3,2,1,0:T(4,128)S(1)}, u32[]{:S(2)}, u32[]{:S(2)}) async-start(f32[4,2,4,128]{3,2,1,0:T(4,128)} %plan.1), calls=%async_computation | async-start | bytes 32768 | tf_op jit(solution)/shard_map/all_to_all | solution.py:193
  34.9 0.0 reduce-scatter.2.cloned.1.call-start
  35.0 1.7 %fusion.24 = (f32[1,4,12,768]{3,1,2,0:T(4,128)}, f32[1,4,12,768]{3,1,2,0:T(4,128)}) fusion(f32[2,4,12,768]{3,1,2,0:T(4,128)} %param.13), kind=kLoop, calls=%fused_computation.28 | loop fusion | bytes 589824 | tf_op jit(solution)/shard_map/slice | solution.py:213
  36.7 0.0 copy-done.5
  36.7 0.1 eq.43
  36.7 2.1 %all-to-all-done = f32[4,2,4,128]{3,2,1,0:T(4,128)S(1)} async-done(((f32[4,2,4,128]{3,2,1,0:T(4,128)}), f32[4,2,4,128]{3,2,1,0:T(4,128)S(1)}, u32[]{:S(2)}, u32[]{:S(2)}) %all-to-all-start) | async-done | bytes 16416 | tf_op jit(solution)/shard_map/all_to_all | solution.py:193
  38.8 0.1 reshape.57
  38.9 0.1 eq.47
  39.0 0.1 copy.39
  39.1 0.1 reshape.58
  39.2 0.0 copy-done.3
  39.2 0.3 fusion.10
  39.5 31.8 %all_gather.6 = bf16[48,4096]{1,0:T(8,128)(2,1)S(1)} all-gather(bf16[48,512]{1,0:T(8,128)(2,1)S(1)} %reshape.59), channel_id=1, replica_groups=mesh['gen'=4,'bus'=8] {'bus'}, dimensions={1}, use_global_device_ids=true | all-gather | bytes 442368 | tf_op jit(solution)/shard_map/all_gather | solution.py:204
  71.3 0.1 copy.59
  71.4 0.5 convolution_convert_fusion
  71.9 0.0 copy-done
  71.9 0.0 copy-start.4
  71.9 0.8 fusion.7
  72.7 0.7 copy.43
  73.4 1.0 reshape.62
  74.4 0.0 copy-done.4
  74.4 1.9 %add_maximum_fusion.1 = (f32[1,4,12,768]{3,2,1,0:T(8,128)}, f32[1,4,12,768]{3,2,1,0:T(8,128)}, f32[1,4,12,768]{3,2,1,0:T(8,128)}, f32[1,4,12,768]{3,2,1,0:T(8,128)}) fusion(f32[1,4,12,768]{3,2,1,0:T(8,128)S(1)} %reshape.62, f32[768]{0:T(1024)S(1)} %copy-done.4, f32[1,4,12,768]{3,1,2,0:T(4,128)} %get-tuple-element.6, f32[1,4,12,768]{3,1,2,0:T(4,128)} %get-tuple-element.7), kind=kLoop, calls=%fused_computation.12 | loop fusion | flops 258048 | bytes 1035264 | tf_op jit(solution)/shard_map/max | solution.py:215
  76.3 1.0 squeeze.7
  77.3 1.6 squeeze.6
  78.9 2.1 %convolution_bitcast_fusion = f32[48,6,16,128]{3,0,2,1:T(8,128)S(1)} fusion(bf16[6,16,128,128]{3,2,1,0:T(8,128)(2,1)S(1)} %copy-done, f32[48,6,128]{2,1,0:T(8,128)S(1)} %squeeze.7, f32[48,6,128]{2,0,1:T(8,128)S(1)} %fusion.7, f32[48,6,128]{2,1,0:T(8,128)} %squeeze.6, f32[6,128]{1,0:T(8,128)S(1)} %bitcast.43), kind=kOutput, calls=%fused_computation.2 | convolution fusion | flops 151400448 | bytes 5950464 | tf_op jit(solution)/shard_map/rlc,lkbc->rlkb/dot_general | solution.py:222
  81.0 0.0 copy-start.1
  81.0 0.0 copy-start.2
  81.0 2.6 %fusion.2 = f32[48,32,128]{2,1,0:T(8,128)} fusion(f32[48,6,16,128]{3,0,2,1:T(8,128)S(1)} %convolution_bitcast_fusion, s32[6,16]{1,0:T(8,128)S(1)} %copy-done.5), kind=kOutput, calls=%fused_computation.4 | convolution fusion | flops 226495488 | bytes 3146112 | tf_op jit(solution)/shard_map/rlkb,lkj->rjb/dot_general | solution.py:226
  83.6 2.2 %reshape.63 = f32[4,12,4096]{2,1,0:T(8,128)} reshape(f32[48,32,128]{2,1,0:T(8,128)} %fusion.2) | data formatting | bytes 1572864 | tf_op jit(solution)/shard_map/reshape | solution.py:226
  85.8 0.0 reduce-scatter.2.cloned.1.call-update
  85.9 0.0 copy-done.1
  85.9 0.0 copy-done.2
  85.9 0.9 copy.51
  86.8 63.1 %reduce-scatter.2.cloned.1.call-done = f32[4,12,512]{2,1,0:T(8,128)} async-done(((f32[4,12,4096]{2,1,0:T(8,128)}), f32[4,12,512]{2,1,0:T(8,128)}) %reduce-scatter.2.cloned.1.call-update) | async-done | bytes 98320 | tf_op jit(solution)/shard_map/reduce_scatter | solution.py:229
  150.0 1.0 dynamic-slice_subtract_fusion
  150.9 7.1 %all_gather.7 = f32[16,12,512]{2,1,0:T(8,128)S(1)} all-gather(f32[4,12,512]{2,1,0:T(8,128)S(1)} %dynamic-slice_subtract_fusion), channel_id=1, replica_groups=mesh['gen'=4,'bus'=8] {'gen'}, dimensions={0}, use_global_device_ids=true | all-gather | bytes 491520 | tf_op jit(solution)/shard_map/all_gather | solution.py:232
  158.1 1.0 copy.52
  (3 shorter events, 0.0 us)
Async XLA Ops:
  7.2 64.7 %copy-start = (bf16[6,16,128,128]{3,2,1,0:T(8,128)(2,1)S(1)}, bf16[6,16,128,128]{3,2,1,0:T(8,128)(2,1)}, u32[]{:S(2)}) copy-start(bf16[6,16,128,128]{3,2,1,0:T(8,128)(2,1)} %param.15) | copy-start | bytes 9437188
  7.2 29.5 %copy-start.5 = (s32[6,16]{1,0:T(8,128)S(1)}, s32[6,16]{1,0:T(8,128)}, u32[]{:S(2)}) copy-start(s32[6,16]{1,0:T(8,128)} %param.16) | copy-start | bytes 1156
  7.2 32.0 %copy-start.3 = (f32[4,12,512]{2,0,1:T(4,128)S(1)}, f32[4,12,512]{2,0,1:T(4,128)}, u32[]{:S(2)}) copy-start(f32[4,12,512]{2,0,1:T(4,128)} %param.12) | copy-start | bytes 294916
  30.7 8.1 %all-to-all-start = ((f32[4,2,4,128]{3,2,1,0:T(4,128)}), f32[4,2,4,128]{3,2,1,0:T(4,128)S(1)}, u32[]{:S(2)}, u32[]{:S(2)}) async-start(f32[4,2,4,128]{3,2,1,0:T(4,128)} %plan.1), calls=%async_computation | async-start | bytes 32768 | tf_op jit(solution)/shard_map/all_to_all | solution.py:193
  34.9 115.0 %reduce-scatter.2.cloned.1.call-start = ((), (), s32[]{:S(2)}) async-start(), calls=%async_computation.2 | async-start | bytes 1179648 | tf_op jit(solution)/shard_map/reduce_scatter | solution.py:229
  71.9 2.5 %copy-start.4 = (f32[768]{0:T(1024)S(1)}, f32[768]{0:T(1024)}, u32[]{:S(2)}) copy-start(f32[768]{0:T(1024)} %param.14) | copy-start | bytes 9220
  81.0 4.9 %copy-start.1 = (f32[1,4,12,768]{3,2,1,0:T(8,128)S(1)}, f32[1,4,12,768]{3,2,1,0:T(8,128)}, u32[]{:S(2)}) copy-start(f32[1,4,12,768]{3,2,1,0:T(8,128)} %get-tuple-element.8) | copy-start | bytes 442372
  81.0 4.9 %copy-start.2 = (f32[1,4,12,768]{3,2,1,0:T(8,128)S(1)}, f32[1,4,12,768]{3,2,1,0:T(8,128)}, u32[]{:S(2)}) copy-start(f32[1,4,12,768]{3,2,1,0:T(8,128)} %get-tuple-element.9) | copy-start | bytes 442372
Sparse Core Ops, SparseCore 0:
  86.0 63.9 reduce-scatter.1

commit v2 on v1

--- a/solution.py
+++ b/solution.py
@@ -168,6 +168,123 @@
     )(state_counts, gen_bus, bus_price, transitions, state_level, state_cost)
 
 
+def net_kernel(plan_ref, demand_ref, net_ref, *, gens):
+    parts, rows, scn_dev, _ = plan_ref.shape
+    _, hours, bus_dev = demand_ref.shape
+    per_row = LANES // gens
+    lane = lax.broadcasted_iota(jnp.int32, (1, LANES), 1)
+    hour_of_lane = lax.broadcasted_iota(jnp.int32, (per_row, LANES), 1) // gens
+    hour_of_row = lax.broadcasted_iota(jnp.int32, (per_row, LANES), 0)
+    bus_ids = lax.broadcasted_iota(jnp.int32, (bus_dev, LANES), 0).astype(jnp.float32)
+    bus_start = (hours % per_row) * gens
+    left, places = [], []
+    for part in range(parts):
+        pieces = []
+        for n in range(scn_dev):
+            for row in range(rows):
+                values = jnp.broadcast_to(plan_ref[part, row][n : n + 1, :], (per_row, LANES))
+                keep = (hour_of_lane == hour_of_row) & (hour_of_row < hours - row * per_row)
+                pieces.append(jnp.where(keep, values, 0.0))
+        left.append(jnp.concatenate(pieces, axis=0))
+        bus = plan_ref[part, rows - 1][:1, :]
+        bus = jnp.where((lane >= bus_start) & (lane < bus_start + gens), bus, 0.0)
+        bus = jnp.broadcast_to(bus, (SUBLANES, LANES))
+        shift = gens
+        while shift < LANES:
+            bus = bus + pltpu.roll(bus, shift, 1)
+            shift *= 2
+        places.append((bus_ids == bus[:1, :]).astype(jnp.bfloat16))
+    left = jnp.concatenate(left, axis=1)
+    high = left.astype(jnp.bfloat16)
+    rest = left - high.astype(jnp.float32)
+    middle = rest.astype(jnp.bfloat16)
+    low = (rest - middle.astype(jnp.float32)).astype(jnp.bfloat16)
+    placed = lax.dot_general(
+        jnp.concatenate([high, middle, low], axis=0),
+        jnp.concatenate(places, axis=1),
+        (((1,), (1,)), ((), ())),
+        preferred_element_type=jnp.float32,
+    )
+    count = left.shape[0]
+    injections = placed[:count] + (placed[count : 2 * count] + placed[2 * count :])
+    stride = rows * per_row
+    net = [injections[n * stride : n * stride + hours] - demand_ref[n] for n in range(scn_dev)]
+    net_ref[...] = jnp.concatenate(net, axis=0).astype(jnp.bfloat16)
+
+
+def line_kernel(
+    pattern_smem,
+    place_smem,
+    own_ref,
+    *refs,
+    half,
+):
+    far_refs = refs[: half - 1]
+    other_ref, blocks_ref, limits_ref, old_ref, new_ref, near_out, far_out, net_all, spread_all = refs[half - 1 :]
+    line_blocks, branches = pattern_smem.shape
+    _, scn_dev, hours, _ = old_ref.shape
+    row_total, bus_dev = own_ref.shape
+    per_dev = bus_dev // BLK
+    me = place_smem[0]
+    my_pair, my_side = me // 2, lax.rem(me, 2)
+
+    net_all[0] = own_ref[...]
+    for step in range(1, half):
+        net_all[step] = far_refs[step - 1][...]
+    for step in range(half):
+        net_all[half + step] = other_ref[step]
+    spread_all[...] = jnp.zeros(spread_all.shape, jnp.float32)
+
+    def spot(line, branch):
+        block = pattern_smem[line, branch]
+        owner = block // per_dev
+        column = pl.multiple_of(lax.rem(block, per_dev) * BLK, BLK)
+        step = lax.rem(my_pair - owner // 2 + half, half)
+        side = jnp.where(lax.rem(owner, 2) == my_side, 0, half)
+        return side + step, column
+
+    for line in range(line_blocks):
+        spots = [spot(line, branch) for branch in range(branches)]
+        picked = [net_all[at, :, pl.ds(column, BLK)] for at, column in spots]
+        table = blocks_ref[line].reshape(branches * BLK, BLK)
+        flow = jnp.dot(
+            jnp.concatenate(picked, axis=1), table, preferred_element_type=jnp.float32
+        )
+        lanes = pl.ds(line * BLK, BLK)
+        limit = limits_ref[:, lanes]
+        changes = []
+        for n in range(scn_dev):
+            here = flow[n * hours : (n + 1) * hours]
+            upper_old = old_ref[0, n, :, lanes]
+            lower_old = old_ref[1, n, :, lanes]
+            upper = jnp.maximum(0.0, upper_old + (here - limit))
+            lower = jnp.maximum(0.0, lower_old + (-here - limit))
+            new_ref[0, n, :, lanes] = upper
+            new_ref[1, n, :, lanes] = lower
+            changes.append((upper - upper_old) - (lower - lower_old))
+        change = jnp.concatenate(changes, axis=0).astype(jnp.bfloat16)
+        spread = lax.dot_general(
+            change, table, (((1,), (1,)), ((), ())), preferred_element_type=jnp.float32
+        )
+        for branch, (at, column) in enumerate(spots):
+            spread_all[at, :, pl.ds(column, BLK)] += spread[:, branch * BLK : (branch + 1) * BLK]
+    near_out[...] = spread_all[:half]
+    far_out[...] = spread_all[half:].astype(jnp.bfloat16)
+
+
+def price_kernel(place_smem, price_ref, *refs):
+    share_refs, out_ref = refs[:-1], refs[-1]
+    scn, hours, _ = price_ref.shape
+    parts = len(share_refs)
+    scn_dev = scn // parts
+    me = place_smem[0]
+    for step, share in enumerate(share_refs):
+        start = lax.rem(me - step + parts, parts) * scn_dev
+        for n in range(scn_dev):
+            change = share[n * hours : (n + 1) * hours, :].astype(jnp.float32)
+            out_ref[start + n] = price_ref[start + n] - change
+
+
 def shards(
     bus_price,
     bus_demand,
@@ -182,55 +299,69 @@
     state_cost,
 ):
     scn_dev, hours, bus_dev = bus_demand.shape
-    gen_index = lax.axis_index("gen")
     parts = lax.axis_size("gen")
+    ring = lax.axis_size("bus")
+    half = ring // 2
     gens = state_level.shape[0]
-    per_row = LANES // gens
-    block_total = lax.axis_size("bus") * bus_dev // BLK
-    plan = run_plan(
-        state_counts, gen_bus, bus_price, transitions, state_level, state_cost, parts
-    )
+    row_total = scn_dev * hours
+    gen_place = lax.axis_index("gen").astype(jnp.int32).reshape(1)
+    bus_place = lax.axis_index("bus").astype(jnp.int32).reshape(1)
+    smem = pl.BlockSpec(memory_space=pltpu.SMEM)
+    vmem = pl.BlockSpec(memory_space=pltpu.VMEM)
+    roomy = pltpu.CompilerParams(vmem_limit_bytes=56 * 2**20)
+    pairs = [(i, i ^ 1) for i in range(ring)]
+
+    def shifted(step):
+        return [(i, (i + 2 * step) % ring) for i in range(ring)]
+
+    plan = run_plan(state_counts, gen_bus, bus_price, transitions, state_level, state_cost, parts)
     received = lax.all_to_all(plan, "gen", split_axis=0, concat_axis=0, tiled=True)
-    rows = received.shape[1]
-    spread = received.reshape(parts, rows, scn_dev, per_row, gens)
-    places = spread[:, hours // per_row, 0, hours % per_row, :].reshape(-1)
-    hourly = jnp.transpose(spread, (2, 1, 3, 0, 4)).reshape(scn_dev, rows * per_row, parts * gens)[:, :hours]
-    placing_rows = (places[:, None] == jnp.arange(bus_dev, dtype=jnp.float32)[None, :]).astype(jnp.float32)
-    injections = jnp.einsum("rtg,gb->rtb", hourly, placing_rows, precision=EXACT)
-    row_total = scn_dev * hours
-    network_row_block = (injections - bus_demand).astype(jnp.bfloat16).reshape(row_total, bus_dev)
-    line_blocks = ptdf_blocks.shape[0]
-    wanted = ptdf_pattern.reshape(-1)
-    piece_cols = lax.all_gather(network_row_block, "bus", axis=1, tiled=True)
-    block_count = piece_cols.shape[1] // BLK
-    block_ids = jnp.arange(block_count, dtype=jnp.int32)
-    chooser = (wanted[:, None] == block_ids[None, :]).astype(jnp.bfloat16)
-    blocked = piece_cols.reshape(piece_cols.shape[0], block_count, BLK)
-    picked_blocks = jnp.einsum("rjb,mj->rmb", blocked, chooser, preferred_element_type=jnp.float32)
-    gathered = picked_blocks.astype(jnp.bfloat16).reshape(row_total, line_blocks, NNZB, BLK)
-    flows = jnp.einsum("rlkb,lkbc->rlc", gathered, ptdf_blocks, preferred_element_type=jnp.float32)
-    flow_lines = flows.reshape(scn_dev, hours, line_blocks * BLK)
-    upper_old = multipliers[0]
-    lower_old = multipliers[1]
-    upper_new = jnp.maximum(0.0, upper_old + (flow_lines - line_limits[None, None, :]))
-    lower_new = jnp.maximum(0.0, lower_old + (-flow_lines - line_limits[None, None, :]))
-    change = (
-        (upper_new - upper_old - (lower_new - lower_old))
-        .astype(jnp.bfloat16)
-        .reshape(row_total, line_blocks, BLK)
-    )
-    spread = jnp.einsum("rlc,lkbc->rlkb", change, ptdf_blocks, preferred_element_type=jnp.float32)
-    placing = (
-        ptdf_pattern[:, :, None] == jnp.arange(block_total, dtype=jnp.int32)[None, None, :]
-    ).astype(jnp.float32)
-    partial_change = jnp.einsum("rlkb,lkj->rjb", spread, placing, precision=EXACT).reshape(
-        scn_dev, hours, block_total * BLK
-    )
-    own_change = lax.psum_scatter(partial_change, "bus", scatter_dimension=2, tiled=True)
-    own_price = lax.dynamic_slice_in_dim(bus_price, gen_index * scn_dev, scn_dev, 0)
-    new_share = own_price - own_change
-    new_price = lax.all_gather(new_share, "gen", axis=0, tiled=True)
-    return (jnp.stack([upper_new, lower_new]), new_price)
+    net = pl.pallas_call(
+        functools.partial(net_kernel, gens=gens),
+        out_shape=jax.ShapeDtypeStruct((row_total, bus_dev), jnp.bfloat16),
+        in_specs=[vmem, vmem],
+        out_specs=vmem,
+        compiler_params=roomy,
+        name="net",
+    )(received, bus_demand)
+
+    far = [lax.ppermute(net, "bus", shifted(step)) for step in range(1, half)]
+    other = lax.ppermute(jnp.stack([net] + far), "bus", pairs)
+    new_multipliers, near_part, far_part = pl.pallas_call(
+        functools.partial(line_kernel, half=half),
+        out_shape=(
+            jax.ShapeDtypeStruct(multipliers.shape, jnp.float32),
+            jax.ShapeDtypeStruct((half, row_total, bus_dev), jnp.float32),
+            jax.ShapeDtypeStruct((half, row_total, bus_dev), jnp.bfloat16),
+        ),
+        in_specs=[smem, smem] + [vmem] * (half + 4),
+        out_specs=(vmem, vmem, vmem),
+        scratch_shapes=[
+            pltpu.VMEM((ring, row_total, bus_dev), jnp.bfloat16),
+            pltpu.VMEM((ring, row_total, bus_dev), jnp.float32),
+        ],
+        compiler_params=roomy,
+        name="lines",
+    )(ptdf_pattern, bus_place, net, *far, other, ptdf_blocks, line_limits.reshape(1, -1), multipliers)
+
+    traded = lax.ppermute(far_part, "bus", pairs)
+    own_change = near_part[0] + traded[0].astype(jnp.float32)
+    for step in range(1, half):
+        share = (near_part[step] + traded[step].astype(jnp.float32)).astype(jnp.bfloat16)
+        own_change = own_change + lax.ppermute(share, "bus", shifted(half - step)).astype(jnp.float32)
+    shares = [own_change] + [
+        lax.ppermute(own_change, "gen", [(i, (i + step) % parts) for i in range(parts)])
+        for step in range(1, parts)
+    ]
+    new_price = pl.pallas_call(
+        price_kernel,
+        out_shape=jax.ShapeDtypeStruct(bus_price.shape, jnp.float32),
+        in_specs=[smem] + [vmem] * (parts + 1),
+        out_specs=vmem,
+        compiler_params=roomy,
+        name="price",
+    )(gen_place, bus_price, *shares)
+    return (new_multipliers, new_price)
 
 
 def solution(mesh):

time: 166 us -> 85.8 us (0.52)
  waiting for transfers between devices: 65.2 us -> 21.3 us
  blocking collectives: 38.9 us -> 0 us
  between operations: 14.2 us -> 0.68 us
  starting transfers between devices: 4.25 us -> 16.5 us
  Pallas kernels: 19.7 us -> 29.8 us
  matrix products: 6.26 us -> 0 us
    reduce_scatter x1 -> x0, waiting for transfers between devices: 63.1 us -> none  [shards(): lax.psum_scatter(partial_change, 'bus', scatter_dimension=2, tiled=True)]
    all_gather x2 -> x0, blocking collectives: 38.9 us -> none  [the longest x1 31.8 us: shards(): piece_cols = lax.all_gather(network_row_block, 'bus', axis=1, tiled=True)]
    ppermute x0 -> x11, waiting for transfers between devices: none -> 19 us  [the longest x3 5.07 us: shards(): far = [lax.ppermute(net, 'bus', shifted(step)) for step in range(1, half)]]
    ppermute x0 -> x11, starting transfers between devices: none -> 12.2 us  [the longest x3 5.05 us: shards(): far = [lax.ppermute(net, 'bus', shifted(step)) for step in range(1, half)]]
    pallas_call x0 -> x3, Pallas kernels: none -> 10.1 us  [the longest x1 5.96 us: shards(): pl.pallas_call(functools.partial(line_kernel, half=half), out_shape=(jax....]
    unnamed x17 -> x24, local copies, waits for them, and re-layouts: 5.77 us -> 12.8 us
    dot_general x5 -> x0, matrix products: 6.26 us -> none  [the longest x1 2.56 us: shards(): jnp.einsum('rlkb,lkj->rjb', spread, placing, precision=EXACT)]
    squeeze x2 -> x0, local copies, waits for them, and re-layouts: 2.58 us -> none  [the longest x1 1.63 us: shards(): upper_old = multipliers[0]]
  transfers between devices with their start and end apart: 2 -> 12, of which waited for: 2 -> 12; matrix products, arithmetic and copies ran while one was open for 2% -> 8% of each run, Pallas kernels for 0% -> 0%
where the time goes in v2:
time: 85.8 us; the launch traced here: 85.1 us
  Pallas kernels  29.8 us (35%)
  waiting for transfers between devices  21.3 us (25%)
  starting transfers between devices  16.5 us (19%)
  local copies, waits for them, and re-layouts  14.1 us (16%)
  other arithmetic  2.79 us (3%)
    pallas_call x1, Pallas kernels, run_plan(): pl.pallas_call(plan_kernel, out_shape=jax.ShapeDtypeStruct((parts, rows,...  19.7 us
    unnamed x24, local copies, waits for them, and re-layouts  12.8 us
    pallas_call x1, Pallas kernels, shards(): pl.pallas_call(functools.partial(line_kernel, half=half), out_shape=(jax....  5.96 us
    ppermute x3, waiting for transfers between devices, shards(): far = [lax.ppermute(net, 'bus', shifted(step)) for step in range(1, half)]  5.07 us
    ppermute x3, starting transfers between devices, shards(): far = [lax.ppermute(net, 'bus', shifted(step)) for step in range(1, half)]  5.05 us
    ppermute x3, waiting for transfers between devices, shards(): lax.ppermute(share, 'bus', shifted(half - step)).astype(jnp.float32)  4.55 us
    ppermute x1, waiting for transfers between devices, shards(): traded = lax.ppermute(far_part, 'bus', pairs)  4.39 us
    all_to_all x1, starting transfers between devices, shards(): lax.all_to_all(plan, 'gen', split_axis=0, concat_axis=0, tiled=True)  4.25 us
  transfers between devices with their start and end apart: 12, of which 12 were waited for; matrix products, arithmetic and copies ran while one was open for 8% of the time, Pallas kernels for 0%

profile of v2, /device:TPU:0, one launch (start us, length us, event | category | flops | bytes accessed | tf_op | source)
XLA Modules:
  0.0 85.1 jit_solution(12094298792919721603)
XLA Ops:
  0.6 1.6 %copy.14.trans_ref = s32[16,3,512]{2,1,0:T(4,128)} copy(s32[16,3,512]{2,0,1:T(8,128)} %param.19) | data formatting | bytes 196608 | tf_op args[8]
  2.2 2.0 %copy.13.price_ref = f32[16,12,512]{2,1,0:T(8,128)} copy(f32[16,12,512]{2,0,1:T(8,128)} %param.11) | data formatting | bytes 786432 | tf_op args[0]
  4.3 19.7 %plan.1 = f32[4,2,4,128]{3,2,1,0:T(4,128)} custom-call(s32[16]{0:T(128)} %counts_smem.1, s32[16]{0:T(128)} %bus_smem.1, f32[16,12,512]{2,1,0:T(8,128)} %copy.13.price_ref, s32[16,3,512]{2,1,0:T(4,128)} %copy.14.trans_ref, f32[16,512]{1,0:T(8,128)} %level_ref.1, f32[16,512]{1,0:T(8,128)} %cost_ref.1), custom_call_target="tpu_custom_call" | custom-call | tf_op jit(solution)/shard_map/plan/pallas_call | solution.py:151
  24.0 4.3 %all-to-all-start = ((f32[4,2,4,128]{3,2,1,0:T(4,128)}), f32[4,2,4,128]{3,2,1,0:T(4,128)S(1)}, u32[]{:S(2)}, u32[]{:S(2)}) async-start(f32[4,2,4,128]{3,2,1,0:T(4,128)} %plan.1), calls=%async_computation | async-start | bytes 32768 | tf_op jit(solution)/shard_map/all_to_all | solution.py:318
  28.2 1.6 %copy.15.demand_ref = f32[4,12,512]{2,1,0:T(8,128)} copy(f32[4,12,512]{2,0,1:T(4,128)} %param.12) | data formatting | bytes 196608 | tf_op args[1]
  29.8 2.3 %all-to-all-done.plan_ref = f32[4,2,4,128]{3,2,1,0:T(4,128)S(1)} async-done(((f32[4,2,4,128]{3,2,1,0:T(4,128)}), f32[4,2,4,128]{3,2,1,0:T(4,128)S(1)}, u32[]{:S(2)}, u32[]{:S(2)}) %all-to-all-start) | async-done | bytes 16416 | tf_op jit(solution)/shard_map/all_to_all | solution.py:318
  32.1 0.0 copy-start.8
  32.1 0.6 copy-done.8
  32.7 2.1 %net.1.own_ref = bf16[48,512]{1,0:T(8,128)(2,1)} custom-call(f32[4,2,4,128]{3,2,1,0:T(4,128)} %copy-done.8, f32[4,12,512]{2,1,0:T(8,128)} %copy.15.demand_ref), custom_call_target="tpu_custom_call" | custom-call | tf_op jit(solution)/shard_map/net/pallas_call | solution.py:319
  34.8 4.0 %collective-permute-start.2 = (bf16[48,512]{1,0:T(8,128)(2,1)}, bf16[48,512]{1,0:T(8,128)(2,1)S(1)}, u32[]{:S(2)}, u32[]{:S(2)}) collective-permute-start(bf16[48,512]{1,0:T(8,128)(2,1)} %net.1.own_ref), channel_id=1, source_target_pairs={{0,6},{1,7},{2,0},{3,1},{4,2},{5,3},{6,4},{7,5},{8,14},{9,15},{10,... | collective-permute-start | bytes 147464 | tf_op jit(solution)/shard_map/ppermute | solution.py:328
  38.8 0.0 collective-permute-start.1
  38.8 1.0 %collective-permute-start = (bf16[48,512]{1,0:T(8,128)(2,1)}, bf16[48,512]{1,0:T(8,128)(2,1)S(1)}, u32[]{:S(2)}, u32[]{:S(2)}) collective-permute-start(bf16[48,512]{1,0:T(8,128)(2,1)} %net.1.own_ref), channel_id=1, source_target_pairs={{0,2},{1,3},{2,4},{3,5},{4,6},{5,7},{6,0},{7,1},{8,10},{9,11},{10,... | collective-permute-start | bytes 147464 | tf_op jit(solution)/shard_map/ppermute | solution.py:328
  39.9 1.3 %collective-permute-done.2.refs_2_ = bf16[48,512]{1,0:T(8,128)(2,1)S(1)} collective-permute-done((bf16[48,512]{1,0:T(8,128)(2,1)}, bf16[48,512]{1,0:T(8,128)(2,1)S(1)}, u32[]{:S(2)}, u32[]{:S(2)}) %collective-permute-start.2) | collective-permute-done | bytes 49184 | tf_op jit(solution)/shard_map/ppermute | solution.py:328
  41.1 0.0 copy-start.1
  41.1 2.9 %collective-permute-done.1.refs_1_ = bf16[48,512]{1,0:T(8,128)(2,1)S(1)} collective-permute-done((bf16[48,512]{1,0:T(8,128)(2,1)}, bf16[48,512]{1,0:T(8,128)(2,1)S(1)}, u32[]{:S(2)}, u32[]{:S(2)}) %collective-permute-start.1) | collective-permute-done | bytes 49184 | tf_op jit(solution)/shard_map/ppermute | solution.py:328
  44.0 0.0 copy-start.2
  44.0 0.9 %collective-permute-done.refs_0_ = bf16[48,512]{1,0:T(8,128)(2,1)S(1)} collective-permute-done((bf16[48,512]{1,0:T(8,128)(2,1)}, bf16[48,512]{1,0:T(8,128)(2,1)S(1)}, u32[]{:S(2)}, u32[]{:S(2)}) %collective-permute-start) | collective-permute-done | bytes 49184 | tf_op jit(solution)/shard_map/ppermute | solution.py:328
  44.9 0.0 copy-start.3
  44.9 0.8 pad_maximum_fusion
  45.8 1.6 %collective-permute-start.3 = (bf16[4,48,512]{2,1,0:T(8,128)(2,1)S(1)}, bf16[4,48,512]{2,1,0:T(8,128)(2,1)S(1)}, u32[]{:S(2)}, u32[]{:S(2)}) collective-permute-start(bf16[4,48,512]{2,1,0:T(8,128)(2,1)S(1)} %pad_maximum_fusion), channel_id=1, source_target_pairs={{0,1},{1,0},{2,3},{3,2},{4,5},{5,4},{6,7},{7,6},{8,9},{9,8},{10,11... | collective-permute-start | bytes 589832 | tf_op jit(solution)/shard_map/ppermute | solution.py:329
  47.3 1.3 %reshape.25.refs_5_ = f32[1,768]{1,0:T(1,128)} reshape(f32[768]{0:T(1024)} %param.14) | data formatting | bytes 6144 | tf_op jit(solution)/shard_map/reshape | solution.py:345
  48.6 1.8 %copy.16.refs_6_ = f32[2,4,12,768]{3,2,1,0:T(8,128)} copy(f32[2,4,12,768]{3,1,2,0:T(4,128)} %param.13) | data formatting | bytes 589824 | tf_op args[2]
  50.4 1.1 %collective-permute-done.3.refs_3_ = bf16[4,48,512]{2,1,0:T(8,128)(2,1)S(1)} collective-permute-done((bf16[4,48,512]{2,1,0:T(8,128)(2,1)S(1)}, bf16[4,48,512]{2,1,0:T(8,128)(2,1)S(1)}, u32[]{:S(2)}, u32[]{:S(2)}) %collective-permute-start.3) | collective-permute-done | bytes 196640 | tf_op jit(solution)/shard_map/ppermute | solution.py:329
  51.5 0.0 copy-start.4
  51.5 0.0 copy-done.1
  51.5 0.0 copy-done.2
  51.5 0.0 copy-done.3
  51.5 0.7 copy-done.4
  52.2 6.0 %lines.1 = (f32[2,4,12,768]{3,2,1,0:T(8,128)}, f32[4,48,512]{2,1,0:T(8,128)}, bf16[4,48,512]{2,1,0:T(8,128)(2,1)}) custom-call(s32[6,16]{1,0:T(8,128)} %pattern_smem.1, s32[1]{0:T(128)} %bitcast.place_smem, bf16[48,512]{1,0:T(8,128)(2,1)} %net.1.own_ref, bf16[48,512]{1,0:T(8,128)(2,1)} %copy-done.3, bf16[48,512]{1,0:T(8,128)(2,1)} %copy-done.2, ...), custom_call_target="tpu_custom_call" | custom-call | tf_op jit(solution)/shard_map/lines/pallas_call | solution.py:330
  58.2 1.5 %collective-permute-start.4 = (bf16[4,48,512]{2,1,0:T(8,128)(2,1)}, bf16[4,48,512]{2,1,0:T(8,128)(2,1)S(1)}, u32[]{:S(2)}, u32[]{:S(2)}) collective-permute-start(bf16[4,48,512]{2,1,0:T(8,128)(2,1)} %get-tuple-element.7), channel_id=1, source_target_pairs={{0,1},{1,0},{2,3},{3,2},{4,5},{5,4},{6,7},{7,6},{8,9},{9,8},{10,11... | collective-permute-start | bytes 589832 | tf_op jit(solution)/shard_map/ppermute | solution.py:347
  59.6 4.4 %collective-permute-done.4 = bf16[4,48,512]{2,1,0:T(8,128)(2,1)S(1)} collective-permute-done((bf16[4,48,512]{2,1,0:T(8,128)(2,1)}, bf16[4,48,512]{2,1,0:T(8,128)(2,1)S(1)}, u32[]{:S(2)}, u32[]{:S(2)}) %collective-permute-start.4) | collective-permute-done | bytes 196640 | tf_op jit(solution)/shard_map/ppermute | solution.py:347
  64.0 1.0 %fusion.2 = (bf16[48,512]{1,0:T(8,128)(2,1)S(1)}, bf16[48,512]{1,0:T(8,128)(2,1)S(1)}, bf16[48,512]{1,0:T(8,128)(2,1)S(1)}) fusion(f32[4,48,512]{2,1,0:T(8,128)} %get-tuple-element.6, bf16[4,48,512]{2,1,0:T(8,128)(2,1)S(1)} %collective-permute-done.4), kind=kLoop, calls=%fused_computation.7 | loop fusion | flops 221184 | bytes 589824 | tf_op jit(solution)/shard_map/convert_element_type | solution.py:350
  65.1 1.2 %collective-permute-start.5 = (bf16[48,512]{1,0:T(8,128)(2,1)S(1)}, bf16[48,512]{1,0:T(8,128)(2,1)S(1)}, u32[]{:S(2)}, u32[]{:S(2)}) collective-permute-start(bf16[48,512]{1,0:T(8,128)(2,1)S(1)} %get-tuple-element.10), channel_id=1, source_target_pairs={{0,6},{1,7},{2,0},{3,1},{4,2},{5,3},{6,4},{7,5},{8,14},{9,15},{10,... | collective-permute-start | bytes 147464 | tf_op jit(solution)/shard_map/ppermute | solution.py:351
  66.3 0.8 collective-permute-start.7
  67.1 1.5 %collective-permute-start.6 = (bf16[48,512]{1,0:T(8,128)(2,1)S(1)}, bf16[48,512]{1,0:T(8,128)(2,1)S(1)}, u32[]{:S(2)}, u32[]{:S(2)}) collective-permute-start(bf16[48,512]{1,0:T(8,128)(2,1)S(1)} %get-tuple-element.12), channel_id=1, source_target_pairs={{0,4},{1,5},{2,6},{3,7},{4,0},{5,1},{6,2},{7,3},{8,12},{9,13},{10,... | collective-permute-start | bytes 147464 | tf_op jit(solution)/shard_map/ppermute | solution.py:351
  68.6 0.6 collective-permute-done.5
  69.2 3.1 %collective-permute-done.7 = bf16[48,512]{1,0:T(8,128)(2,1)S(1)} collective-permute-done((bf16[48,512]{1,0:T(8,128)(2,1)S(1)}, bf16[48,512]{1,0:T(8,128)(2,1)S(1)}, u32[]{:S(2)}, u32[]{:S(2)}) %collective-permute-start.7) | collective-permute-done | bytes 49184 | tf_op jit(solution)/shard_map/ppermute | solution.py:351
  72.3 0.9 %collective-permute-done.6 = bf16[48,512]{1,0:T(8,128)(2,1)S(1)} collective-permute-done((bf16[48,512]{1,0:T(8,128)(2,1)S(1)}, bf16[48,512]{1,0:T(8,128)(2,1)S(1)}, u32[]{:S(2)}, u32[]{:S(2)}) %collective-permute-start.6) | collective-permute-done | bytes 49184 | tf_op jit(solution)/shard_map/ppermute | solution.py:351
  73.2 0.9 %fusion.1.refs_0_ = f32[48,512]{1,0:T(8,128)S(1)} fusion(bf16[48,512]{1,0:T(8,128)(2,1)S(1)} %collective-permute-done.7, bf16[48,512]{1,0:T(8,128)(2,1)S(1)} %collective-permute-done.6, bf16[48,512]{1,0:T(8,128)(2,1)S(1)} %collective-permute-done.5, f32[4,48,512]{2,1,0:T(8,128)} %get-tuple-element.6, bf16[4,48,512]{2,1,0:T(8,128)(2,1)S(1)} %collective-permute-done.4), kind=kLoop, calls=%fused_computation.3 | loop fusion | flops 196608 | bytes 393216 | tf_op jit(solution)/shard_map/add | solution.py:351
  74.1 0.0 copy-start
  74.1 0.1 collective-permute-start.10
  74.2 0.1 collective-permute-start.9
  74.3 0.4 collective-permute-start.8
  74.7 1.9 %copy.18 = f32[2,4,12,768]{3,1,2,0:T(4,128)} copy(f32[2,4,12,768]{3,2,1,0:T(8,128)} %get-tuple-element.8) | data formatting | bytes 589824
  76.6 0.8 collective-permute-done.10.refs_3_
  77.4 0.0 copy-start.5
  77.4 2.5 %collective-permute-done.9.refs_2_ = f32[48,512]{1,0:T(8,128)S(1)} collective-permute-done((f32[48,512]{1,0:T(8,128)S(1)}, f32[48,512]{1,0:T(8,128)S(1)}, u32[]{:S(2)}, u32[]{:S(2)}) %collective-permute-start.9) | collective-permute-done | bytes 98336 | tf_op jit(solution)/shard_map/ppermute | solution.py:353
  79.9 0.0 copy-start.6
  79.9 0.6 collective-permute-done.8.refs_1_
  80.5 0.0 copy-start.7
  80.5 0.0 copy-done
  80.5 0.0 copy-done.5
  80.5 0.0 copy-done.6
  80.5 0.6 copy-done.7
  81.1 2.0 %price.1 = f32[16,12,512]{2,1,0:T(8,128)} custom-call(s32[1]{0:T(128)} %bitcast.5.place_smem, f32[16,12,512]{2,1,0:T(8,128)} %copy.13.price_ref, f32[48,512]{1,0:T(8,128)} %copy-done, f32[48,512]{1,0:T(8,128)} %copy-done.7, f32[48,512]{1,0:T(8,128)} %copy-done.6, f32[48,512]{1,0:T(8,128)} %copy-done.5), custom_call_target="tpu_custom_call" | custom-call | tf_op jit(solution)/shard_map/price/pallas_call | solution.py:356
  83.1 2.0 %copy.19 = f32[16,12,512]{2,0,1:T(8,128)} copy(f32[16,12,512]{2,1,0:T(8,128)} %price.1) | data formatting | bytes 786432
Async XLA Ops:
  24.0 8.1 %all-to-all-start = ((f32[4,2,4,128]{3,2,1,0:T(4,128)}), f32[4,2,4,128]{3,2,1,0:T(4,128)S(1)}, u32[]{:S(2)}, u32[]{:S(2)}) async-start(f32[4,2,4,128]{3,2,1,0:T(4,128)} %plan.1), calls=%async_computation | async-start | bytes 32768 | tf_op jit(solution)/shard_map/all_to_all | solution.py:318
  32.1 0.6 copy-start.8
  34.8 6.3 %collective-permute-start.2 = (bf16[48,512]{1,0:T(8,128)(2,1)}, bf16[48,512]{1,0:T(8,128)(2,1)S(1)}, u32[]{:S(2)}, u32[]{:S(2)}) collective-permute-start(bf16[48,512]{1,0:T(8,128)(2,1)} %net.1.own_ref), channel_id=1, source_target_pairs={{0,6},{1,7},{2,0},{3,1},{4,2},{5,3},{6,4},{7,5},{8,14},{9,15},{10,... | collective-permute-start | bytes 147464 | tf_op jit(solution)/shard_map/ppermute | solution.py:328
  38.8 5.2 %collective-permute-start.1 = (bf16[48,512]{1,0:T(8,128)(2,1)}, bf16[48,512]{1,0:T(8,128)(2,1)S(1)}, u32[]{:S(2)}, u32[]{:S(2)}) collective-permute-start(bf16[48,512]{1,0:T(8,128)(2,1)} %net.1.own_ref), channel_id=1, source_target_pairs={{0,4},{1,5},{2,6},{3,7},{4,0},{5,1},{6,2},{7,3},{8,12},{9,13},{10,... | collective-permute-start | bytes 147464 | tf_op jit(solution)/shard_map/ppermute | solution.py:328
  38.8 6.1 %collective-permute-start = (bf16[48,512]{1,0:T(8,128)(2,1)}, bf16[48,512]{1,0:T(8,128)(2,1)S(1)}, u32[]{:S(2)}, u32[]{:S(2)}) collective-permute-start(bf16[48,512]{1,0:T(8,128)(2,1)} %net.1.own_ref), channel_id=1, source_target_pairs={{0,2},{1,3},{2,4},{3,5},{4,6},{5,7},{6,0},{7,1},{8,10},{9,11},{10,... | collective-permute-start | bytes 147464 | tf_op jit(solution)/shard_map/ppermute | solution.py:328
  41.1 10.4 %copy-start.1 = (bf16[48,512]{1,0:T(8,128)(2,1)}, bf16[48,512]{1,0:T(8,128)(2,1)S(1)}, u32[]{:S(2)}) copy-start(bf16[48,512]{1,0:T(8,128)(2,1)S(1)} %collective-permute-done.2.refs_2_) | copy-start | bytes 147460
  44.0 7.5 %copy-start.2 = (bf16[48,512]{1,0:T(8,128)(2,1)}, bf16[48,512]{1,0:T(8,128)(2,1)S(1)}, u32[]{:S(2)}) copy-start(bf16[48,512]{1,0:T(8,128)(2,1)S(1)} %collective-permute-done.1.refs_1_) | copy-start | bytes 147460
  44.9 6.6 %copy-start.3 = (bf16[48,512]{1,0:T(8,128)(2,1)}, bf16[48,512]{1,0:T(8,128)(2,1)S(1)}, u32[]{:S(2)}) copy-start(bf16[48,512]{1,0:T(8,128)(2,1)S(1)} %collective-permute-done.refs_0_) | copy-start | bytes 147460
  45.8 5.7 %collective-permute-start.3 = (bf16[4,48,512]{2,1,0:T(8,128)(2,1)S(1)}, bf16[4,48,512]{2,1,0:T(8,128)(2,1)S(1)}, u32[]{:S(2)}, u32[]{:S(2)}) collective-permute-start(bf16[4,48,512]{2,1,0:T(8,128)(2,1)S(1)} %pad_maximum_fusion), channel_id=1, source_target_pairs={{0,1},{1,0},{2,3},{3,2},{4,5},{5,4},{6,7},{7,6},{8,9},{9,8},{10,11... | collective-permute-start | bytes 589832 | tf_op jit(solution)/shard_map/ppermute | solution.py:329
  51.5 0.7 copy-start.4
  58.2 5.9 %collective-permute-start.4 = (bf16[4,48,512]{2,1,0:T(8,128)(2,1)}, bf16[4,48,512]{2,1,0:T(8,128)(2,1)S(1)}, u32[]{:S(2)}, u32[]{:S(2)}) collective-permute-start(bf16[4,48,512]{2,1,0:T(8,128)(2,1)} %get-tuple-element.7), channel_id=1, source_target_pairs={{0,1},{1,0},{2,3},{3,2},{4,5},{5,4},{6,7},{7,6},{8,9},{9,8},{10,11... | collective-permute-start | bytes 589832 | tf_op jit(solution)/shard_map/ppermute | solution.py:347
  65.1 4.1 %collective-permute-start.5 = (bf16[48,512]{1,0:T(8,128)(2,1)S(1)}, bf16[48,512]{1,0:T(8,128)(2,1)S(1)}, u32[]{:S(2)}, u32[]{:S(2)}) collective-permute-start(bf16[48,512]{1,0:T(8,128)(2,1)S(1)} %get-tuple-element.10), channel_id=1, source_target_pairs={{0,6},{1,7},{2,0},{3,1},{4,2},{5,3},{6,4},{7,5},{8,14},{9,15},{10,... | collective-permute-start | bytes 147464 | tf_op jit(solution)/shard_map/ppermute | solution.py:351
  66.3 6.0 %collective-permute-start.7 = (bf16[48,512]{1,0:T(8,128)(2,1)S(1)}, bf16[48,512]{1,0:T(8,128)(2,1)S(1)}, u32[]{:S(2)}, u32[]{:S(2)}) collective-permute-start(bf16[48,512]{1,0:T(8,128)(2,1)S(1)} %get-tuple-element.11), channel_id=1, source_target_pairs={{0,2},{1,3},{2,4},{3,5},{4,6},{5,7},{6,0},{7,1},{8,10},{9,11},{10,... | collective-permute-start | bytes 147464 | tf_op jit(solution)/shard_map/ppermute | solution.py:351
  67.1 6.0 %collective-permute-start.6 = (bf16[48,512]{1,0:T(8,128)(2,1)S(1)}, bf16[48,512]{1,0:T(8,128)(2,1)S(1)}, u32[]{:S(2)}, u32[]{:S(2)}) collective-permute-start(bf16[48,512]{1,0:T(8,128)(2,1)S(1)} %get-tuple-element.12), channel_id=1, source_target_pairs={{0,4},{1,5},{2,6},{3,7},{4,0},{5,1},{6,2},{7,3},{8,12},{9,13},{10,... | collective-permute-start | bytes 147464 | tf_op jit(solution)/shard_map/ppermute | solution.py:351
  74.1 6.3 %copy-start = (f32[48,512]{1,0:T(8,128)}, f32[48,512]{1,0:T(8,128)S(1)}, u32[]{:S(2)}) copy-start(f32[48,512]{1,0:T(8,128)S(1)} %fusion.1.refs_0_) | copy-start | bytes 294916
  74.1 3.2 %collective-permute-start.10 = (f32[48,512]{1,0:T(8,128)S(1)}, f32[48,512]{1,0:T(8,128)S(1)}, u32[]{:S(2)}, u32[]{:S(2)}) collective-permute-start(f32[48,512]{1,0:T(8,128)S(1)} %fusion.1.refs_0_), channel_id=1, source_target_pairs={{0,24},{8,0},{16,8},{24,16},{1,25},{9,1},{17,9},{25,17},{2,26},{10... | collective-permute-start | bytes 294920 | tf_op jit(solution)/shard_map/ppermute | solution.py:353
  74.2 5.7 %collective-permute-start.9 = (f32[48,512]{1,0:T(8,128)S(1)}, f32[48,512]{1,0:T(8,128)S(1)}, u32[]{:S(2)}, u32[]{:S(2)}) collective-permute-start(f32[48,512]{1,0:T(8,128)S(1)} %fusion.1.refs_0_), channel_id=1, source_target_pairs={{0,16},{8,24},{16,0},{24,8},{1,17},{9,25},{17,1},{25,9},{2,18},{10... | collective-permute-start | bytes 294920 | tf_op jit(solution)/shard_map/ppermute | solution.py:353
  74.3 6.2 %collective-permute-start.8 = (f32[48,512]{1,0:T(8,128)S(1)}, f32[48,512]{1,0:T(8,128)S(1)}, u32[]{:S(2)}, u32[]{:S(2)}) collective-permute-start(f32[48,512]{1,0:T(8,128)S(1)} %fusion.1.refs_0_), channel_id=1, source_target_pairs={{0,8},{8,16},{16,24},{24,0},{1,9},{9,17},{17,25},{25,1},{2,10},{10... | collective-permute-start | bytes 294920 | tf_op jit(solution)/shard_map/ppermute | solution.py:353
  77.4 3.1 %copy-start.5 = (f32[48,512]{1,0:T(8,128)}, f32[48,512]{1,0:T(8,128)S(1)}, u32[]{:S(2)}) copy-start(f32[48,512]{1,0:T(8,128)S(1)} %collective-permute-done.10.refs_3_) | copy-start | bytes 294916
  79.9 0.6 copy-start.6
  80.5 0.6 copy-start.7

commit v3 on v2

--- a/solution.py
+++ b/solution.py
@@ -35,7 +35,7 @@
     big_state,
     small_state,
 ):
-    scn, hours, bus_dev = price_ref.shape
+    hours, scn, bus_dev = price_ref.shape
     gens = level_ref.shape[0]
     big_total = BIG_GROUP * (gens // GROUP)
     parts = out_ref.shape[0]
@@ -60,9 +60,9 @@
     chooser = (
         lax.broadcasted_iota(jnp.int32, (bus_dev, LANES), 0) == local_row
     ).astype(jnp.float32)
-    for n in range(scn):
-        gen_price[n] = lax.dot_general(
-            price_ref[n],
+    for hour in range(hours):
+        gen_price[hour] = lax.dot_general(
+            price_ref[hour],
             chooser,
             (((1,), (0,)), ((), ())),
             precision=EXACT,
@@ -78,16 +78,16 @@
         level_slot[slot] = jnp.broadcast_to(level_ref[pl.ds(gen, 1), :], (SUBLANES, STATES))
         cost_row = jnp.where(state_ids < counts_smem[gen], cost_ref[pl.ds(gen, 1), :], 1e30)
         cost_slot[slot] = jnp.broadcast_to(cost_row, (SUBLANES, STATES))
-        successors = trans_ref[gen]
+        successors = [trans_ref[branch, pl.ds(gen, 1), :] for branch in range(trans_ref.shape[0])]
         table = big_table.at[slot] if slot < big_total else small_table.at[slot - big_total]
         for first in range(0, span, HALF):
-            shifted = (successors[:, :span] - first).astype(jnp.float32).astype(jnp.bfloat16)
             rows = lax.broadcasted_iota(jnp.int32, (HALF, span), 0).astype(jnp.float32).astype(jnp.bfloat16)
             one = jnp.ones((HALF, span), jnp.bfloat16)
             none = jnp.zeros((HALF, span), jnp.bfloat16)
             total = none
-            for branch in range(successors.shape[0]):
-                total = total + jnp.where(rows == shifted[branch : branch + 1, :], one, none)
+            for row in successors:
+                shifted = (row[:, :span] - first).astype(jnp.float32).astype(jnp.bfloat16)
+                total = total + jnp.where(rows == shifted, one, none)
             table[pl.ds(first, HALF), :] = total
 
     def repeat_rows(block, copies):
@@ -104,7 +104,7 @@
                 state, table = small_state.at[slot - big_total], small_table.at[slot - big_total]
             level = repeat_rows(level_slot[slot][:, :span], scn // SUBLANES)
             cost = repeat_rows(cost_slot[slot][:, :span], scn // SUBLANES)
-            price = gen_price[:, hour, slot : slot + 1]
+            price = gen_price[hour][:, slot : slot + 1]
             weight = jnp.exp(price * level - cost)
             base = weight if chains == 0 else weight * state[:scn, :]
             total = jnp.sum(base, axis=-1, keepdims=True)
@@ -142,7 +142,7 @@
 
 
 def run_plan(state_counts, gen_bus, bus_price, transitions, state_level, state_cost, parts):
-    scn, hours, _ = bus_price.shape
+    hours, scn, _ = bus_price.shape
     gens = state_level.shape[0]
     big_total = BIG_GROUP * (gens // GROUP)
     rows = -(-hours // (LANES // gens))
@@ -157,37 +157,37 @@
             pltpu.SMEM((gens,), jnp.int32),
             pltpu.VMEM((gens, SUBLANES, STATES), jnp.float32),
             pltpu.VMEM((gens, SUBLANES, STATES), jnp.float32),
-            pltpu.VMEM((scn, hours, LANES), jnp.float32),
+            pltpu.VMEM((hours, scn, LANES), jnp.float32),
             pltpu.VMEM((big_total, STATES, STATES), jnp.bfloat16),
             pltpu.VMEM((gens - big_total, HALF, HALF), jnp.bfloat16),
             pltpu.VMEM((big_total, (hours + 1) * scn, STATES), jnp.float32),
             pltpu.VMEM((gens - big_total, (hours + 1) * scn, HALF), jnp.float32),
         ],
-        compiler_params=pltpu.CompilerParams(vmem_limit_bytes=56 * 2**20),
+        compiler_params=pltpu.CompilerParams(vmem_limit_bytes=28 * 2**20),
         name="plan",
     )(state_counts, gen_bus, bus_price, transitions, state_level, state_cost)
 
 
 def net_kernel(plan_ref, demand_ref, net_ref, *, gens):
     parts, rows, scn_dev, _ = plan_ref.shape
-    _, hours, bus_dev = demand_ref.shape
+    hours, _, bus_dev = demand_ref.shape
     per_row = LANES // gens
     lane = lax.broadcasted_iota(jnp.int32, (1, LANES), 1)
-    hour_of_lane = lax.broadcasted_iota(jnp.int32, (per_row, LANES), 1) // gens
-    hour_of_row = lax.broadcasted_iota(jnp.int32, (per_row, LANES), 0)
     bus_ids = lax.broadcasted_iota(jnp.int32, (bus_dev, LANES), 0).astype(jnp.float32)
-    bus_start = (hours % per_row) * gens
+
+    def of_hour(hour):
+        start = (hour % per_row) * gens
+        return (lane >= start) & (lane < start + gens)
+
     left, places = [], []
     for part in range(parts):
-        pieces = []
-        for n in range(scn_dev):
-            for row in range(rows):
-                values = jnp.broadcast_to(plan_ref[part, row][n : n + 1, :], (per_row, LANES))
-                keep = (hour_of_lane == hour_of_row) & (hour_of_row < hours - row * per_row)
-                pieces.append(jnp.where(keep, values, 0.0))
-        left.append(jnp.concatenate(pieces, axis=0))
-        bus = plan_ref[part, rows - 1][:1, :]
-        bus = jnp.where((lane >= bus_start) & (lane < bus_start + gens), bus, 0.0)
+        values = [plan_ref[part, row] for row in range(rows)]
+        left.append(
+            jnp.concatenate(
+                [jnp.where(of_hour(hour), values[hour // per_row], 0.0) for hour in range(hours)], axis=0
+            )
+        )
+        bus = jnp.where(of_hour(hours), values[-1][:1, :], 0.0)
         bus = jnp.broadcast_to(bus, (SUBLANES, LANES))
         shift = gens
         while shift < LANES:
@@ -207,9 +207,8 @@
     )
     count = left.shape[0]
     injections = placed[:count] + (placed[count : 2 * count] + placed[2 * count :])
-    stride = rows * per_row
-    net = [injections[n * stride : n * stride + hours] - demand_ref[n] for n in range(scn_dev)]
-    net_ref[...] = jnp.concatenate(net, axis=0).astype(jnp.bfloat16)
+    demand = jnp.concatenate([demand_ref[hour] for hour in range(hours)], axis=0)
+    net_ref[...] = (injections - demand).astype(jnp.bfloat16)
 
 
 def line_kernel(
@@ -222,7 +221,7 @@
     far_refs = refs[: half - 1]
     other_ref, blocks_ref, limits_ref, old_ref, new_ref, near_out, far_out, net_all, spread_all = refs[half - 1 :]
     line_blocks, branches = pattern_smem.shape
-    _, scn_dev, hours, _ = old_ref.shape
+    _, hours, scn_dev, _ = old_ref.shape
     row_total, bus_dev = own_ref.shape
     per_dev = bus_dev // BLK
     me = place_smem[0]
@@ -251,18 +250,16 @@
             jnp.concatenate(picked, axis=1), table, preferred_element_type=jnp.float32
         )
         lanes = pl.ds(line * BLK, BLK)
-        limit = limits_ref[:, lanes]
-        changes = []
-        for n in range(scn_dev):
-            here = flow[n * hours : (n + 1) * hours]
-            upper_old = old_ref[0, n, :, lanes]
-            lower_old = old_ref[1, n, :, lanes]
-            upper = jnp.maximum(0.0, upper_old + (here - limit))
-            lower = jnp.maximum(0.0, lower_old + (-here - limit))
-            new_ref[0, n, :, lanes] = upper
-            new_ref[1, n, :, lanes] = lower
-            changes.append((upper - upper_old) - (lower - lower_old))
-        change = jnp.concatenate(changes, axis=0).astype(jnp.bfloat16)
+        limit = limits_ref[lanes].reshape(1, BLK)
+        upper_old = jnp.concatenate([old_ref[0, hour, :, lanes] for hour in range(hours)], axis=0)
+        lower_old = jnp.concatenate([old_ref[1, hour, :, lanes] for hour in range(hours)], axis=0)
+        upper = jnp.maximum(0.0, upper_old + (flow - limit))
+        lower = jnp.maximum(0.0, lower_old + (-flow - limit))
+        for hour in range(hours):
+            here = slice(hour * scn_dev, (hour + 1) * scn_dev)
+            new_ref[0, hour, :, lanes] = upper[here]
+            new_ref[1, hour, :, lanes] = lower[here]
+        change = ((upper - upper_old) - (lower - lower_old)).astype(jnp.bfloat16)
         spread = lax.dot_general(
             change, table, (((1,), (1,)), ((), ())), preferred_element_type=jnp.float32
         )
@@ -273,16 +270,17 @@
 
 
 def price_kernel(place_smem, price_ref, *refs):
-    share_refs, out_ref = refs[:-1], refs[-1]
-    scn, hours, _ = price_ref.shape
+    share_refs, (out_ref, share_all) = refs[:-2], refs[-2:]
+    hours, scn, _ = price_ref.shape
     parts = len(share_refs)
     scn_dev = scn // parts
     me = place_smem[0]
     for step, share in enumerate(share_refs):
-        start = lax.rem(me - step + parts, parts) * scn_dev
-        for n in range(scn_dev):
-            change = share[n * hours : (n + 1) * hours, :].astype(jnp.float32)
-            out_ref[start + n] = price_ref[start + n] - change
+        share_all[step] = share[...]
+    steps = [lax.rem(me - part + parts, parts) for part in range(parts)]
+    for hour in range(hours):
+        change = [share_all[step, hour * scn_dev : (hour + 1) * scn_dev, :] for step in steps]
+        out_ref[hour] = price_ref[hour] - jnp.concatenate(change, axis=0)
 
 
 def shards(
@@ -308,12 +306,16 @@
     bus_place = lax.axis_index("bus").astype(jnp.int32).reshape(1)
     smem = pl.BlockSpec(memory_space=pltpu.SMEM)
     vmem = pl.BlockSpec(memory_space=pltpu.VMEM)
-    roomy = pltpu.CompilerParams(vmem_limit_bytes=56 * 2**20)
+    roomy = pltpu.CompilerParams(vmem_limit_bytes=24 * 2**20)
     pairs = [(i, i ^ 1) for i in range(ring)]
 
     def shifted(step):
         return [(i, (i + 2 * step) % ring) for i in range(ring)]
 
+    bus_price = jnp.transpose(bus_price, (1, 0, 2))
+    bus_demand = jnp.transpose(bus_demand, (1, 0, 2))
+    multipliers = jnp.transpose(multipliers, (0, 2, 1, 3))
+    transitions = jnp.transpose(transitions, (1, 0, 2))
     plan = run_plan(state_counts, gen_bus, bus_price, transitions, state_level, state_cost, parts)
     received = lax.all_to_all(plan, "gen", split_axis=0, concat_axis=0, tiled=True)
     net = pl.pallas_call(
@@ -342,7 +344,7 @@
         ],
         compiler_params=roomy,
         name="lines",
-    )(ptdf_pattern, bus_place, net, *far, other, ptdf_blocks, line_limits.reshape(1, -1), multipliers)
+    )(ptdf_pattern, bus_place, net, *far, other, ptdf_blocks, line_limits, multipliers)
 
     traded = lax.ppermute(far_part, "bus", pairs)
     own_change = near_part[0] + traded[0].astype(jnp.float32)
@@ -358,10 +360,11 @@
         out_shape=jax.ShapeDtypeStruct(bus_price.shape, jnp.float32),
         in_specs=[smem] + [vmem] * (parts + 1),
         out_specs=vmem,
+        scratch_shapes=[pltpu.VMEM((parts, row_total, bus_dev), jnp.float32)],
         compiler_params=roomy,
         name="price",
     )(gen_place, bus_price, *shares)
-    return (new_multipliers, new_price)
+    return (jnp.transpose(new_multipliers, (0, 2, 1, 3)), jnp.transpose(new_price, (1, 0, 2)))
 
 
 def solution(mesh):

time: 85.8 us -> 73.5 us (0.86)
  Pallas kernels: 29.8 us -> 19.1 us
  blocking collectives: 0 us -> 7.9 us
  starting transfers between devices: 16.5 us -> 11.8 us
  local copies, waits for them, and re-layouts: 14.1 us -> 9.82 us
  other arithmetic: 2.79 us -> 0.1 us
  waiting for transfers between devices: 21.3 us -> 23.5 us
    all_to_all x0 -> x1, blocking collectives: none -> 7.9 us  [shards(): lax.all_to_all(plan, 'gen', split_axis=0, concat_axis=0, tiled=True)]
    pallas_call x1, Pallas kernels: 19.7 us -> 13.7 us  [run_plan(): pl.pallas_call(plan_kernel, out_shape=jax.ShapeDtypeStruct((parts, rows,...]
    all_to_all x1 -> x0, starting transfers between devices: 4.25 us -> none  [shards(): lax.all_to_all(plan, 'gen', split_axis=0, concat_axis=0, tiled=True)]
    ppermute x1, waiting for transfers between devices: 1.12 us -> 4.18 us  [shards(): other = lax.ppermute(jnp.stack([net] + far), 'bus', pairs)]
    unnamed x24, local copies, waits for them, and re-layouts: 12.8 us -> 9.82 us
    all_to_all x1 -> x0, waiting for transfers between devices: 2.28 us -> none  [shards(): lax.all_to_all(plan, 'gen', split_axis=0, concat_axis=0, tiled=True)]
    pallas_call x1, Pallas kernels: 5.96 us -> 4.01 us  [shards(): pl.pallas_call(functools.partial(line_kernel, half=half), out_shape=(jax....]
    ppermute x3, waiting for transfers between devices: 3.86 us -> 5.76 us  [shards(): lax.ppermute(own_change, 'gen', [(i, (i + step) % parts) for i in range(p...]
  transfers between devices with their start and end apart: 12 -> 11, of which waited for: 12 -> 11; matrix products, arithmetic and copies ran while one was open for 8% -> 0% of each run, Pallas kernels for 0% -> 0%
where the time goes in v3:
time: 73.5 us; the launch traced here: 73 us
  waiting for transfers between devices  23.5 us (32%)
  Pallas kernels  19.1 us (26%)
  starting transfers between devices  11.8 us (16%)
  local copies, waits for them, and re-layouts  9.82 us (13%)
  blocking collectives  7.9 us (11%)
    pallas_call x1, Pallas kernels, run_plan(): pl.pallas_call(plan_kernel, out_shape=jax.ShapeDtypeStruct((parts, rows,...  13.7 us
    unnamed x24, local copies, waits for them, and re-layouts  9.82 us
    all_to_all x1, blocking collectives, shards(): lax.all_to_all(plan, 'gen', split_axis=0, concat_axis=0, tiled=True)  7.9 us
    ppermute x3, waiting for transfers between devices, shards(): lax.ppermute(own_change, 'gen', [(i, (i + step) % parts) for i in range(p...  5.76 us
    ppermute x3, waiting for transfers between devices, shards(): far = [lax.ppermute(net, 'bus', shifted(step)) for step in range(1, half)]  4.88 us
    ppermute x3, starting transfers between devices, shards(): far = [lax.ppermute(net, 'bus', shifted(step)) for step in range(1, half)]  4.66 us
    ppermute x3, waiting for transfers between devices, shards(): lax.ppermute(share, 'bus', shifted(half - step)).astype(jnp.float32)  4.54 us
    ppermute x1, waiting for transfers between devices, shards(): other = lax.ppermute(jnp.stack([net] + far), 'bus', pairs)  4.18 us
  transfers between devices with their start and end apart: 11, of which 11 were waited for; matrix products, arithmetic and copies ran while one was open for 0% of the time, Pallas kernels for 0%

profile of v3, /device:TPU:0, one launch (start us, length us, event | category | flops | bytes accessed | tf_op | source)
XLA Modules:
  0.0 73.0 jit_solution(1831576205065062631)
XLA Ops:
  0.6 0.0 copy-start.1
  0.6 1.0 %copy-done.1 = f32[16,12,512]{2,0,1:T(8,128)S(1)} copy-done((f32[16,12,512]{2,0,1:T(8,128)S(1)}, f32[16,12,512]{2,0,1:T(8,128)}, u32[]{:S(2)}) %copy-start.1) | copy-done | bytes 393240
  1.6 0.0 copy-start.4
  1.6 0.9 %copy-done.4 = s32[16,3,512]{2,0,1:T(8,128)S(1)} copy-done((s32[16,3,512]{2,0,1:T(8,128)S(1)}, s32[16,3,512]{2,0,1:T(8,128)}, u32[]{:S(2)}) %copy-start.4) | copy-done | bytes 98328
  2.5 0.0 copy-start.6
  2.5 0.8 %copy-done.6 = f32[16,512]{1,0:T(8,128)S(1)} copy-done((f32[16,512]{1,0:T(8,128)S(1)}, f32[16,512]{1,0:T(8,128)}, u32[]{:S(2)}) %copy-start.6) | copy-done | bytes 32792
  3.3 0.0 copy-start.7
  3.3 0.8 %copy-done.7 = f32[16,512]{1,0:T(8,128)S(1)} copy-done((f32[16,512]{1,0:T(8,128)S(1)}, f32[16,512]{1,0:T(8,128)}, u32[]{:S(2)}) %copy-start.7) | copy-done | bytes 32792
  4.0 0.0 copy-start.10
  4.0 0.7 copy-done.10
  4.7 0.0 copy-start.11
  4.7 0.7 copy-done.11
  5.3 0.0 copy-start.2
  5.4 13.7 %plan.1 = f32[4,2,4,128]{3,2,1,0:T(4,128)S(1)} custom-call(s32[16]{0:T(128)S(1)} %copy-done.10, s32[16]{0:T(128)S(1)} %copy-done.11, f32[12,16,512]{2,1,0:T(8,128)S(1)} %bitcast.24, s32[3,16,512]{2,1,0:T(8,128)S(1)} %bitcast.31, f32[16,512]{1,0:T(8,128)S(1)} %copy-done.6, f32[16,512]{1,0:T(8,128)S(1)} %copy-done.7), custom_call_target="tpu_custom_call" | custom-call | tf_op jit(solution)/shard_map/plan/pallas_call | solution.py:151
  19.1 7.9 %all_to_all.5.plan_ref = f32[4,2,4,128]{3,2,1,0:T(4,128)S(1)} all-to-all(f32[4,2,4,128]{3,2,1,0:T(4,128)S(1)} %plan.1), channel_id=1, replica_groups=mesh['gen'=4,'bus'=8] {'gen'}, dimensions={0} | all-to-all | bytes 32768 | tf_op jit(solution)/shard_map/all_to_all | solution.py:320
  27.0 0.0 copy-start.5
  27.0 0.9 %copy-done.5 = f32[4,12,512]{2,0,1:T(4,128)S(1)} copy-done((f32[4,12,512]{2,0,1:T(4,128)S(1)}, f32[4,12,512]{2,0,1:T(4,128)}, u32[]{:S(2)}) %copy-start.5) | copy-done | bytes 98328
  27.9 0.5 net.1.own_ref
  28.4 3.6 %collective-permute-start.2 = (bf16[48,512]{1,0:T(8,128)(2,1)S(1)}, bf16[48,512]{1,0:T(8,128)(2,1)S(1)}, u32[]{:S(2)}, u32[]{:S(2)}) collective-permute-start(bf16[48,512]{1,0:T(8,128)(2,1)S(1)} %net.1.own_ref), channel_id=1, source_target_pairs={{0,6},{1,7},{2,0},{3,1},{4,2},{5,3},{6,4},{7,5},{8,14},{9,15},{10,... | collective-permute-start | bytes 147464 | tf_op jit(solution)/shard_map/ppermute | solution.py:330
  32.1 0.0 collective-permute-start.1
  32.1 1.0 %collective-permute-start = (bf16[48,512]{1,0:T(8,128)(2,1)S(1)}, bf16[48,512]{1,0:T(8,128)(2,1)S(1)}, u32[]{:S(2)}, u32[]{:S(2)}) collective-permute-start(bf16[48,512]{1,0:T(8,128)(2,1)S(1)} %net.1.own_ref), channel_id=1, source_target_pairs={{0,2},{1,3},{2,4},{3,5},{4,6},{5,7},{6,0},{7,1},{8,10},{9,11},{10,... | collective-permute-start | bytes 147464 | tf_op jit(solution)/shard_map/ppermute | solution.py:330
  33.1 1.0 %collective-permute-done.2.refs_2_ = bf16[48,512]{1,0:T(8,128)(2,1)S(1)} collective-permute-done((bf16[48,512]{1,0:T(8,128)(2,1)S(1)}, bf16[48,512]{1,0:T(8,128)(2,1)S(1)}, u32[]{:S(2)}, u32[]{:S(2)}) %collective-permute-start.2) | collective-permute-done | bytes 49184 | tf_op jit(solution)/shard_map/ppermute | solution.py:330
  34.1 3.0 %collective-permute-done.1.refs_1_ = bf16[48,512]{1,0:T(8,128)(2,1)S(1)} collective-permute-done((bf16[48,512]{1,0:T(8,128)(2,1)S(1)}, bf16[48,512]{1,0:T(8,128)(2,1)S(1)}, u32[]{:S(2)}, u32[]{:S(2)}) %collective-permute-start.1) | collective-permute-done | bytes 49184 | tf_op jit(solution)/shard_map/ppermute | solution.py:330
  37.1 0.9 %collective-permute-done.refs_0_ = bf16[48,512]{1,0:T(8,128)(2,1)S(1)} collective-permute-done((bf16[48,512]{1,0:T(8,128)(2,1)S(1)}, bf16[48,512]{1,0:T(8,128)(2,1)S(1)}, u32[]{:S(2)}, u32[]{:S(2)}) %collective-permute-start) | collective-permute-done | bytes 49184 | tf_op jit(solution)/shard_map/ppermute | solution.py:330
  38.0 1.6 %collective-permute-start.3 = (bf16[4,48,512]{2,1,0:T(8,128)(2,1)S(1)}, bf16[4,48,512]{2,1,0:T(8,128)(2,1)S(1)}, u32[]{:S(2)}, u32[]{:S(2)}) collective-permute-start(bf16[4,48,512]{2,1,0:T(8,128)(2,1)S(1)} %pad_maximum_fusion), channel_id=1, source_target_pairs={{0,1},{1,0},{2,3},{3,2},{4,5},{5,4},{6,7},{7,6},{8,9},{9,8},{10,11... | collective-permute-start | bytes 589832 | tf_op jit(solution)/shard_map/ppermute | solution.py:331
  39.5 4.2 %collective-permute-done.3.refs_3_ = bf16[4,48,512]{2,1,0:T(8,128)(2,1)S(1)} collective-permute-done((bf16[4,48,512]{2,1,0:T(8,128)(2,1)S(1)}, bf16[4,48,512]{2,1,0:T(8,128)(2,1)S(1)}, u32[]{:S(2)}, u32[]{:S(2)}) %collective-permute-start.3) | collective-permute-done | bytes 196640 | tf_op jit(solution)/shard_map/ppermute | solution.py:331
  43.7 0.0 copy-start
  43.7 1.9 %copy-done = bf16[6,16,128,128]{3,2,1,0:T(8,128)(2,1)S(1)} copy-done((bf16[6,16,128,128]{3,2,1,0:T(8,128)(2,1)S(1)}, bf16[6,16,128,128]{3,2,1,0:T(8,128)(2,1)}, u32[]{:S(2)}) %copy-start) | copy-done | bytes 3145752
  45.6 0.0 copy-start.3
  45.6 1.0 %copy-done.3 = f32[2,4,12,768]{3,1,2,0:T(4,128)S(1)} copy-done((f32[2,4,12,768]{3,1,2,0:T(4,128)S(1)}, f32[2,4,12,768]{3,1,2,0:T(4,128)}, u32[]{:S(2)}) %copy-start.3) | copy-done | bytes 294936
  46.6 0.0 copy-start.8
  46.6 0.7 copy-done.8
  47.3 0.0 copy-start.9
  47.3 0.7 copy-done.9
  48.0 4.0 %lines.1 = (f32[2,12,4,768]{3,2,1,0:T(4,128)}, f32[4,48,512]{2,1,0:T(8,128)S(1)}, bf16[4,48,512]{2,1,0:T(8,128)(2,1)S(1)}) custom-call(s32[6,16]{1,0:T(8,128)S(1)} %copy-done.8, s32[1]{0:T(128)} %bitcast.place_smem, bf16[48,512]{1,0:T(8,128)(2,1)S(1)} %net.1.own_ref, bf16[48,512]{1,0:T(8,128)(2,1)S(1)} %collective-permute-done.refs_0_, ...), custom_call_target="tpu_custom_call" | custom-call | tf_op jit(solution)/shard_map/lines/pallas_call | solution.py:332
  52.0 1.5 %collective-permute-start.4 = (bf16[4,48,512]{2,1,0:T(8,128)(2,1)S(1)}, bf16[4,48,512]{2,1,0:T(8,128)(2,1)S(1)}, u32[]{:S(2)}, u32[]{:S(2)}) collective-permute-start(bf16[4,48,512]{2,1,0:T(8,128)(2,1)S(1)} %get-tuple-element.7), channel_id=1, source_target_pairs={{0,1},{1,0},{2,3},{3,2},{4,5},{5,4},{6,7},{7,6},{8,9},{9,8},{10,11... | collective-permute-start | bytes 589832 | tf_op jit(solution)/shard_map/ppermute | solution.py:349
  53.5 4.2 %collective-permute-done.4 = bf16[4,48,512]{2,1,0:T(8,128)(2,1)S(1)} collective-permute-done((bf16[4,48,512]{2,1,0:T(8,128)(2,1)S(1)}, bf16[4,48,512]{2,1,0:T(8,128)(2,1)S(1)}, u32[]{:S(2)}, u32[]{:S(2)}) %collective-permute-start.4) | collective-permute-done | bytes 196640 | tf_op jit(solution)/shard_map/ppermute | solution.py:349
  57.7 1.2 %collective-permute-start.5 = (bf16[48,512]{1,0:T(8,128)(2,1)S(1)}, bf16[48,512]{1,0:T(8,128)(2,1)S(1)}, u32[]{:S(2)}, u32[]{:S(2)}) collective-permute-start(bf16[48,512]{1,0:T(8,128)(2,1)S(1)} %get-tuple-element.8), channel_id=1, source_target_pairs={{0,6},{1,7},{2,0},{3,1},{4,2},{5,3},{6,4},{7,5},{8,14},{9,15},{10,... | collective-permute-start | bytes 147464 | tf_op jit(solution)/shard_map/ppermute | solution.py:353
  58.9 0.9 %collective-permute-start.7 = (bf16[48,512]{1,0:T(8,128)(2,1)S(1)}, bf16[48,512]{1,0:T(8,128)(2,1)S(1)}, u32[]{:S(2)}, u32[]{:S(2)}) collective-permute-start(bf16[48,512]{1,0:T(8,128)(2,1)S(1)} %get-tuple-element.9), channel_id=1, source_target_pairs={{0,2},{1,3},{2,4},{3,5},{4,6},{5,7},{6,0},{7,1},{8,10},{9,11},{10,... | collective-permute-start | bytes 147464 | tf_op jit(solution)/shard_map/ppermute | solution.py:353
  59.8 1.5 %collective-permute-start.6 = (bf16[48,512]{1,0:T(8,128)(2,1)S(1)}, bf16[48,512]{1,0:T(8,128)(2,1)S(1)}, u32[]{:S(2)}, u32[]{:S(2)}) collective-permute-start(bf16[48,512]{1,0:T(8,128)(2,1)S(1)} %get-tuple-element.10), channel_id=1, source_target_pairs={{0,4},{1,5},{2,6},{3,7},{4,0},{5,1},{6,2},{7,3},{8,12},{9,13},{10,... | collective-permute-start | bytes 147464 | tf_op jit(solution)/shard_map/ppermute | solution.py:353
  61.2 0.6 collective-permute-done.5
  61.8 3.1 %collective-permute-done.7 = bf16[48,512]{1,0:T(8,128)(2,1)S(1)} collective-permute-done((bf16[48,512]{1,0:T(8,128)(2,1)S(1)}, bf16[48,512]{1,0:T(8,128)(2,1)S(1)}, u32[]{:S(2)}, u32[]{:S(2)}) %collective-permute-start.7) | collective-permute-done | bytes 49184 | tf_op jit(solution)/shard_map/ppermute | solution.py:353
  64.9 0.9 %collective-permute-done.6 = bf16[48,512]{1,0:T(8,128)(2,1)S(1)} collective-permute-done((bf16[48,512]{1,0:T(8,128)(2,1)S(1)}, bf16[48,512]{1,0:T(8,128)(2,1)S(1)}, u32[]{:S(2)}, u32[]{:S(2)}) %collective-permute-start.6) | collective-permute-done | bytes 49184 | tf_op jit(solution)/shard_map/ppermute | solution.py:353
  65.8 0.1 collective-permute-start.10
  65.9 0.1 collective-permute-start.9
  66.0 0.4 collective-permute-start.8
  66.4 2.7 %collective-permute-done.10.refs_3_ = f32[48,512]{1,0:T(8,128)S(1)} collective-permute-done((f32[48,512]{1,0:T(8,128)S(1)}, f32[48,512]{1,0:T(8,128)S(1)}, u32[]{:S(2)}, u32[]{:S(2)}) %collective-permute-start.10) | collective-permute-done | bytes 98336 | tf_op jit(solution)/shard_map/ppermute | solution.py:355
  69.1 2.5 %collective-permute-done.9.refs_2_ = f32[48,512]{1,0:T(8,128)S(1)} collective-permute-done((f32[48,512]{1,0:T(8,128)S(1)}, f32[48,512]{1,0:T(8,128)S(1)}, u32[]{:S(2)}, u32[]{:S(2)}) %collective-permute-start.9) | collective-permute-done | bytes 98336 | tf_op jit(solution)/shard_map/ppermute | solution.py:355
  71.6 0.6 collective-permute-done.8.refs_1_
  72.2 0.0 copy-done.2
  72.2 0.8 %price.1 = f32[12,16,512]{2,1,0:T(8,128)} custom-call(s32[1]{0:T(128)} %bitcast.10.place_smem, f32[12,16,512]{2,1,0:T(8,128)S(1)} %bitcast.25, f32[48,512]{1,0:T(8,128)S(1)} %fusion.1.refs_0_, f32[48,512]{1,0:T(8,128)S(1)} %collective-permute-done.8.refs_1_, f32[48,512]{1,0:T(8,128)S(1)} %collective-permute-done.9.refs_2_, ...), custom_call_target="tpu_custom_call" | custom-call | tf_op jit(solution)/shard_map/price/pallas_call | solution.py:358
  (3 shorter events, 0.1 us)
Async XLA Ops:
  0.6 1.0 %copy-start.1 = (f32[16,12,512]{2,0,1:T(8,128)S(1)}, f32[16,12,512]{2,0,1:T(8,128)}, u32[]{:S(2)}) copy-start(f32[16,12,512]{2,0,1:T(8,128)} %param.11) | copy-start | bytes 1179652
  1.6 0.9 %copy-start.4 = (s32[16,3,512]{2,0,1:T(8,128)S(1)}, s32[16,3,512]{2,0,1:T(8,128)}, u32[]{:S(2)}) copy-start(s32[16,3,512]{2,0,1:T(8,128)} %param.19) | copy-start | bytes 294916
  2.5 0.8 %copy-start.6 = (f32[16,512]{1,0:T(8,128)S(1)}, f32[16,512]{1,0:T(8,128)}, u32[]{:S(2)}) copy-start(f32[16,512]{1,0:T(8,128)} %level_ref.1) | copy-start | bytes 98308
  3.3 0.8 %copy-start.7 = (f32[16,512]{1,0:T(8,128)S(1)}, f32[16,512]{1,0:T(8,128)}, u32[]{:S(2)}) copy-start(f32[16,512]{1,0:T(8,128)} %cost_ref.1) | copy-start | bytes 98308
  4.0 0.7 copy-start.10
  4.7 0.7 copy-start.11
  5.3 66.8 %copy-start.2 = (f32[16,12,512]{2,0,1:T(8,128)S(1)}, f32[16,12,512]{2,0,1:T(8,128)}, u32[]{:S(2)}) copy-start(f32[16,12,512]{2,0,1:T(8,128)} %param.11) | copy-start | bytes 1179652
  27.0 0.9 %copy-start.5 = (f32[4,12,512]{2,0,1:T(4,128)S(1)}, f32[4,12,512]{2,0,1:T(4,128)}, u32[]{:S(2)}) copy-start(f32[4,12,512]{2,0,1:T(4,128)} %param.12) | copy-start | bytes 294916
  28.4 5.6 %collective-permute-start.2 = (bf16[48,512]{1,0:T(8,128)(2,1)S(1)}, bf16[48,512]{1,0:T(8,128)(2,1)S(1)}, u32[]{:S(2)}, u32[]{:S(2)}) collective-permute-start(bf16[48,512]{1,0:T(8,128)(2,1)S(1)} %net.1.own_ref), channel_id=1, source_target_pairs={{0,6},{1,7},{2,0},{3,1},{4,2},{5,3},{6,4},{7,5},{8,14},{9,15},{10,... | collective-permute-start | bytes 147464 | tf_op jit(solution)/shard_map/ppermute | solution.py:330
  32.1 5.0 %collective-permute-start.1 = (bf16[48,512]{1,0:T(8,128)(2,1)S(1)}, bf16[48,512]{1,0:T(8,128)(2,1)S(1)}, u32[]{:S(2)}, u32[]{:S(2)}) collective-permute-start(bf16[48,512]{1,0:T(8,128)(2,1)S(1)} %net.1.own_ref), channel_id=1, source_target_pairs={{0,4},{1,5},{2,6},{3,7},{4,0},{5,1},{6,2},{7,3},{8,12},{9,13},{10,... | collective-permute-start | bytes 147464 | tf_op jit(solution)/shard_map/ppermute | solution.py:330
  32.1 5.9 %collective-permute-start = (bf16[48,512]{1,0:T(8,128)(2,1)S(1)}, bf16[48,512]{1,0:T(8,128)(2,1)S(1)}, u32[]{:S(2)}, u32[]{:S(2)}) collective-permute-start(bf16[48,512]{1,0:T(8,128)(2,1)S(1)} %net.1.own_ref), channel_id=1, source_target_pairs={{0,2},{1,3},{2,4},{3,5},{4,6},{5,7},{6,0},{7,1},{8,10},{9,11},{10,... | collective-permute-start | bytes 147464 | tf_op jit(solution)/shard_map/ppermute | solution.py:330
  38.0 5.7 %collective-permute-start.3 = (bf16[4,48,512]{2,1,0:T(8,128)(2,1)S(1)}, bf16[4,48,512]{2,1,0:T(8,128)(2,1)S(1)}, u32[]{:S(2)}, u32[]{:S(2)}) collective-permute-start(bf16[4,48,512]{2,1,0:T(8,128)(2,1)S(1)} %pad_maximum_fusion), channel_id=1, source_target_pairs={{0,1},{1,0},{2,3},{3,2},{4,5},{5,4},{6,7},{7,6},{8,9},{9,8},{10,11... | collective-permute-start | bytes 589832 | tf_op jit(solution)/shard_map/ppermute | solution.py:331
  43.7 1.9 %copy-start = (bf16[6,16,128,128]{3,2,1,0:T(8,128)(2,1)S(1)}, bf16[6,16,128,128]{3,2,1,0:T(8,128)(2,1)}, u32[]{:S(2)}) copy-start(bf16[6,16,128,128]{3,2,1,0:T(8,128)(2,1)} %refs_4_.1) | copy-start | bytes 9437188
  45.6 1.0 %copy-start.3 = (f32[2,4,12,768]{3,1,2,0:T(4,128)S(1)}, f32[2,4,12,768]{3,1,2,0:T(4,128)}, u32[]{:S(2)}) copy-start(f32[2,4,12,768]{3,1,2,0:T(4,128)} %param.13) | copy-start | bytes 884740
  46.6 0.7 copy-start.8
  47.3 0.7 copy-start.9
  52.0 5.7 %collective-permute-start.4 = (bf16[4,48,512]{2,1,0:T(8,128)(2,1)S(1)}, bf16[4,48,512]{2,1,0:T(8,128)(2,1)S(1)}, u32[]{:S(2)}, u32[]{:S(2)}) collective-permute-start(bf16[4,48,512]{2,1,0:T(8,128)(2,1)S(1)} %get-tuple-element.7), channel_id=1, source_target_pairs={{0,1},{1,0},{2,3},{3,2},{4,5},{5,4},{6,7},{7,6},{8,9},{9,8},{10,11... | collective-permute-start | bytes 589832 | tf_op jit(solution)/shard_map/ppermute | solution.py:349
  57.7 4.1 %collective-permute-start.5 = (bf16[48,512]{1,0:T(8,128)(2,1)S(1)}, bf16[48,512]{1,0:T(8,128)(2,1)S(1)}, u32[]{:S(2)}, u32[]{:S(2)}) collective-permute-start(bf16[48,512]{1,0:T(8,128)(2,1)S(1)} %get-tuple-element.8), channel_id=1, source_target_pairs={{0,6},{1,7},{2,0},{3,1},{4,2},{5,3},{6,4},{7,5},{8,14},{9,15},{10,... | collective-permute-start | bytes 147464 | tf_op jit(solution)/shard_map/ppermute | solution.py:353
  58.9 6.0 %collective-permute-start.7 = (bf16[48,512]{1,0:T(8,128)(2,1)S(1)}, bf16[48,512]{1,0:T(8,128)(2,1)S(1)}, u32[]{:S(2)}, u32[]{:S(2)}) collective-permute-start(bf16[48,512]{1,0:T(8,128)(2,1)S(1)} %get-tuple-element.9), channel_id=1, source_target_pairs={{0,2},{1,3},{2,4},{3,5},{4,6},{5,7},{6,0},{7,1},{8,10},{9,11},{10,... | collective-permute-start | bytes 147464 | tf_op jit(solution)/shard_map/ppermute | solution.py:353
  59.8 6.0 %collective-permute-start.6 = (bf16[48,512]{1,0:T(8,128)(2,1)S(1)}, bf16[48,512]{1,0:T(8,128)(2,1)S(1)}, u32[]{:S(2)}, u32[]{:S(2)}) collective-permute-start(bf16[48,512]{1,0:T(8,128)(2,1)S(1)} %get-tuple-element.10), channel_id=1, source_target_pairs={{0,4},{1,5},{2,6},{3,7},{4,0},{5,1},{6,2},{7,3},{8,12},{9,13},{10,... | collective-permute-start | bytes 147464 | tf_op jit(solution)/shard_map/ppermute | solution.py:353
  65.8 3.2 %collective-permute-start.10 = (f32[48,512]{1,0:T(8,128)S(1)}, f32[48,512]{1,0:T(8,128)S(1)}, u32[]{:S(2)}, u32[]{:S(2)}) collective-permute-start(f32[48,512]{1,0:T(8,128)S(1)} %fusion.1.refs_0_), channel_id=1, source_target_pairs={{0,24},{8,0},{16,8},{24,16},{1,25},{9,1},{17,9},{25,17},{2,26},{10... | collective-permute-start | bytes 294920 | tf_op jit(solution)/shard_map/ppermute | solution.py:355
  65.9 5.7 %collective-permute-start.9 = (f32[48,512]{1,0:T(8,128)S(1)}, f32[48,512]{1,0:T(8,128)S(1)}, u32[]{:S(2)}, u32[]{:S(2)}) collective-permute-start(f32[48,512]{1,0:T(8,128)S(1)} %fusion.1.refs_0_), channel_id=1, source_target_pairs={{0,16},{8,24},{16,0},{24,8},{1,17},{9,25},{17,1},{25,9},{2,18},{10... | collective-permute-start | bytes 294920 | tf_op jit(solution)/shard_map/ppermute | solution.py:355
  66.0 6.2 %collective-permute-start.8 = (f32[48,512]{1,0:T(8,128)S(1)}, f32[48,512]{1,0:T(8,128)S(1)}, u32[]{:S(2)}, u32[]{:S(2)}) collective-permute-start(f32[48,512]{1,0:T(8,128)S(1)} %fusion.1.refs_0_), channel_id=1, source_target_pairs={{0,8},{8,16},{16,24},{24,0},{1,9},{9,17},{17,25},{25,1},{2,10},{10... | collective-permute-start | bytes 294920 | tf_op jit(solution)/shard_map/ppermute | solution.py:355

commit v4 on v3

--- a/solution.py
+++ b/solution.py
@@ -14,33 +14,47 @@
 GROUP = 16
 BIG_GROUP = 6
 LANES = 128
+AHEAD = 5
 SUBLANES = 8
 EXACT = lax.Precision.HIGHEST
 
 
-def plan_kernel(
-    counts_smem,
-    bus_smem,
-    price_ref,
-    trans_ref,
-    level_ref,
-    cost_ref,
-    out_ref,
-    order,
-    level_slot,
-    cost_slot,
-    gen_price,
-    big_table,
-    small_table,
-    big_state,
-    small_state,
-):
+def plan_kernel(*refs, gens, parts):
+    (counts_hbm, bus_hbm, trans_hbm, level_hbm, cost_hbm, price_hbm), refs = refs[:6], refs[6:]
+    ahead_hbm, refs = refs[:AHEAD], refs[AHEAD:]
+    out_ref, refs = refs[0], refs[1:]
+    ahead_refs, refs = refs[:AHEAD], refs[AHEAD:]
+    (
+        counts_smem,
+        bus_smem,
+        trans_ref,
+        level_ref,
+        cost_ref,
+        price_ref,
+        order,
+        level_slot,
+        cost_slot,
+        gen_price,
+        big_table,
+        small_table,
+        big_state,
+        small_state,
+        sems,
+    ) = refs
+    sources = (counts_hbm, bus_hbm, trans_hbm, level_hbm, cost_hbm, price_hbm) + ahead_hbm
+    targets = (counts_smem, bus_smem, trans_ref, level_ref, cost_ref, price_ref) + ahead_refs
+    copies = [
+        pltpu.make_async_copy(source, target, sems.at[at])
+        for at, (source, target) in enumerate(zip(sources, targets))
+    ]
+    for copy in copies:
+        copy.start()
     hours, scn, bus_dev = price_ref.shape
-    gens = level_ref.shape[0]
     big_total = BIG_GROUP * (gens // GROUP)
-    parts = out_ref.shape[0]
     scn_dev = scn // parts
     per_row = LANES // gens
+    for copy in copies[:2]:
+        copy.wait()
 
     def place(gen, taken):
         big = (counts_smem[gen] > HALF).astype(jnp.int32)
@@ -50,6 +64,8 @@
 
     lax.fori_loop(0, gens, place, jnp.int32(0))
 
+    for copy in copies[2:6]:
+        copy.wait()
     lane = lax.broadcasted_iota(jnp.int32, (1, LANES), 1)
     local_row = jnp.zeros((1, LANES), jnp.int32)
     bus_row = jnp.zeros((1, LANES), jnp.int32)
@@ -139,21 +155,30 @@
     for part in range(parts):
         for row, block in enumerate(outs):
             out_ref[part, row] = block[part * scn_dev : (part + 1) * scn_dev, :]
-
-
-def run_plan(state_counts, gen_bus, bus_price, transitions, state_level, state_cost, parts):
+    for copy in copies[6:]:
+        copy.wait()
+
+
+def run_plan(counts, gen_bus, transitions, level, cost, bus_price, ahead, parts):
     hours, scn, _ = bus_price.shape
-    gens = state_level.shape[0]
+    gens = level.shape[0]
     big_total = BIG_GROUP * (gens // GROUP)
     rows = -(-hours // (LANES // gens))
-    smem = pl.BlockSpec(memory_space=pltpu.SMEM)
+    hbm = pl.BlockSpec(memory_space=pltpu.HBM)
     vmem = pl.BlockSpec(memory_space=pltpu.VMEM)
     return pl.pallas_call(
-        plan_kernel,
-        out_shape=jax.ShapeDtypeStruct((parts, rows, scn // parts, LANES), jnp.float32),
-        in_specs=[smem, smem, vmem, vmem, vmem, vmem],
-        out_specs=vmem,
+        functools.partial(plan_kernel, gens=gens, parts=parts),
+        out_shape=(pltpu.VMEM((parts, rows, scn // parts, LANES), jnp.float32),)
+        + tuple(pltpu.VMEM(array.shape, array.dtype) for array in ahead),
+        in_specs=[hbm] * (6 + len(ahead)),
+        out_specs=(vmem,) * (1 + len(ahead)),
         scratch_shapes=[
+            pltpu.SMEM(counts.shape, jnp.int32),
+            pltpu.SMEM(gen_bus.shape, jnp.int32),
+            pltpu.VMEM(transitions.shape, jnp.int32),
+            pltpu.VMEM(level.shape, jnp.float32),
+            pltpu.VMEM(cost.shape, jnp.float32),
+            pltpu.VMEM(bus_price.shape, jnp.float32),
             pltpu.SMEM((gens,), jnp.int32),
             pltpu.VMEM((gens, SUBLANES, STATES), jnp.float32),
             pltpu.VMEM((gens, SUBLANES, STATES), jnp.float32),
@@ -162,10 +187,16 @@
             pltpu.VMEM((gens - big_total, HALF, HALF), jnp.bfloat16),
             pltpu.VMEM((big_total, (hours + 1) * scn, STATES), jnp.float32),
             pltpu.VMEM((gens - big_total, (hours + 1) * scn, HALF), jnp.float32),
+            pltpu.SemaphoreType.DMA((6 + len(ahead),)),
         ],
-        compiler_params=pltpu.CompilerParams(vmem_limit_bytes=28 * 2**20),
+        compiler_params=pltpu.CompilerParams(vmem_limit_bytes=32 * 2**20),
         name="plan",
-    )(state_counts, gen_bus, bus_price, transitions, state_level, state_cost)
+    )(
+        *(
+            pltpu.with_memory_space_constraint(array, pltpu.HBM)
+            for array in (counts, gen_bus, transitions, level, cost, bus_price) + ahead
+        )
+    )
 
 
 def net_kernel(plan_ref, demand_ref, net_ref, *, gens):
@@ -218,8 +249,11 @@
     *refs,
     half,
 ):
-    far_refs = refs[: half - 1]
-    other_ref, blocks_ref, limits_ref, old_ref, new_ref, near_out, far_out, net_all, spread_all = refs[half - 1 :]
+    net_refs, refs = (own_ref,) + refs[: 2 * half - 1], refs[2 * half - 1 :]
+    blocks_ref, limits_ref, old_ref, price_hbm, new_ref, near_out, far_out = refs[:7]
+    net_all, spread_all, price_ref, sem = refs[7:]
+    price_copy = pltpu.make_async_copy(price_hbm, price_ref, sem)
+    price_copy.start()
     line_blocks, branches = pattern_smem.shape
     _, hours, scn_dev, _ = old_ref.shape
     row_total, bus_dev = own_ref.shape
@@ -227,11 +261,8 @@
     me = place_smem[0]
     my_pair, my_side = me // 2, lax.rem(me, 2)
 
-    net_all[0] = own_ref[...]
-    for step in range(1, half):
-        net_all[step] = far_refs[step - 1][...]
-    for step in range(half):
-        net_all[half + step] = other_ref[step]
+    for at, net_ref in enumerate(net_refs):
+        net_all[at] = net_ref[...]
     spread_all[...] = jnp.zeros(spread_all.shape, jnp.float32)
 
     def spot(line, branch):
@@ -265,22 +296,30 @@
         )
         for branch, (at, column) in enumerate(spots):
             spread_all[at, :, pl.ds(column, BLK)] += spread[:, branch * BLK : (branch + 1) * BLK]
+    far_out[...] = spread_all[half:].astype(jnp.bfloat16)
     near_out[...] = spread_all[:half]
-    far_out[...] = spread_all[half:].astype(jnp.bfloat16)
-
-
-def price_kernel(place_smem, price_ref, *refs):
+    price_copy.wait()
+    part = place_smem[1]
+    for hour in range(hours):
+        price = price_ref[hour, :scn_dev, :]
+        for other in range(1, price_ref.shape[1] // scn_dev):
+            price = jnp.where(part == other, price_ref[hour, other * scn_dev : (other + 1) * scn_dev, :], price)
+        here = slice(hour * scn_dev, (hour + 1) * scn_dev)
+        near_out[0, here, :] = spread_all[0, here, :] - price
+
+
+def price_kernel(place_smem, *refs):
     share_refs, (out_ref, share_all) = refs[:-2], refs[-2:]
-    hours, scn, _ = price_ref.shape
+    hours = out_ref.shape[0]
     parts = len(share_refs)
-    scn_dev = scn // parts
-    me = place_smem[0]
+    scn_dev = out_ref.shape[1] // parts
+    me = place_smem[1]
     for step, share in enumerate(share_refs):
         share_all[step] = share[...]
     steps = [lax.rem(me - part + parts, parts) for part in range(parts)]
     for hour in range(hours):
-        change = [share_all[step, hour * scn_dev : (hour + 1) * scn_dev, :] for step in steps]
-        out_ref[hour] = price_ref[hour] - jnp.concatenate(change, axis=0)
+        less = [share_all[step, hour * scn_dev : (hour + 1) * scn_dev, :] for step in steps]
+        out_ref[hour] = -jnp.concatenate(less, axis=0)
 
 
 def shards(
@@ -302,8 +341,7 @@
     half = ring // 2
     gens = state_level.shape[0]
     row_total = scn_dev * hours
-    gen_place = lax.axis_index("gen").astype(jnp.int32).reshape(1)
-    bus_place = lax.axis_index("bus").astype(jnp.int32).reshape(1)
+    place = jnp.stack([lax.axis_index("bus"), lax.axis_index("gen")]).astype(jnp.int32)
     smem = pl.BlockSpec(memory_space=pltpu.SMEM)
     vmem = pl.BlockSpec(memory_space=pltpu.VMEM)
     roomy = pltpu.CompilerParams(vmem_limit_bytes=24 * 2**20)
@@ -316,7 +354,11 @@
     bus_demand = jnp.transpose(bus_demand, (1, 0, 2))
     multipliers = jnp.transpose(multipliers, (0, 2, 1, 3))
     transitions = jnp.transpose(transitions, (1, 0, 2))
-    plan = run_plan(state_counts, gen_bus, bus_price, transitions, state_level, state_cost, parts)
+    ahead = (bus_demand, ptdf_blocks, multipliers, line_limits, ptdf_pattern)
+    plan, *ahead = run_plan(
+        state_counts, gen_bus, transitions, state_level, state_cost, bus_price, ahead, parts
+    )
+    bus_demand, ptdf_blocks, multipliers, line_limits, ptdf_pattern = ahead
     received = lax.all_to_all(plan, "gen", split_axis=0, concat_axis=0, tiled=True)
     net = pl.pallas_call(
         functools.partial(net_kernel, gens=gens),
@@ -328,7 +370,7 @@
     )(received, bus_demand)
 
     far = [lax.ppermute(net, "bus", shifted(step)) for step in range(1, half)]
-    other = lax.ppermute(jnp.stack([net] + far), "bus", pairs)
+    other = [lax.ppermute(piece, "bus", pairs) for piece in [net] + far]
     new_multipliers, near_part, far_part = pl.pallas_call(
         functools.partial(line_kernel, half=half),
         out_shape=(
@@ -336,15 +378,27 @@
             jax.ShapeDtypeStruct((half, row_total, bus_dev), jnp.float32),
             jax.ShapeDtypeStruct((half, row_total, bus_dev), jnp.bfloat16),
         ),
-        in_specs=[smem, smem] + [vmem] * (half + 4),
+        in_specs=[smem, smem] + [vmem] * (ring + 3) + [pl.BlockSpec(memory_space=pltpu.HBM)],
         out_specs=(vmem, vmem, vmem),
         scratch_shapes=[
             pltpu.VMEM((ring, row_total, bus_dev), jnp.bfloat16),
             pltpu.VMEM((ring, row_total, bus_dev), jnp.float32),
+            pltpu.VMEM(bus_price.shape, jnp.float32),
+            pltpu.SemaphoreType.DMA,
         ],
         compiler_params=roomy,
         name="lines",
-    )(ptdf_pattern, bus_place, net, *far, other, ptdf_blocks, line_limits, multipliers)
+    )(
+        ptdf_pattern,
+        place,
+        net,
+        *far,
+        *other,
+        ptdf_blocks,
+        line_limits,
+        multipliers,
+        pltpu.with_memory_space_constraint(bus_price, pltpu.HBM),
+    )
 
     traded = lax.ppermute(far_part, "bus", pairs)
     own_change = near_part[0] + traded[0].astype(jnp.float32)
@@ -358,12 +412,12 @@
     new_price = pl.pallas_call(
         price_kernel,
         out_shape=jax.ShapeDtypeStruct(bus_price.shape, jnp.float32),
-        in_specs=[smem] + [vmem] * (parts + 1),
+        in_specs=[smem] + [vmem] * parts,
         out_specs=vmem,
         scratch_shapes=[pltpu.VMEM((parts, row_total, bus_dev), jnp.float32)],
         compiler_params=roomy,
         name="price",
-    )(gen_place, bus_price, *shares)
+    )(place, *shares)
     return (jnp.transpose(new_multipliers, (0, 2, 1, 3)), jnp.transpose(new_price, (1, 0, 2)))
 
 

time: 73.5 us -> 64.7 us (0.88)
  local copies, waits for them, and re-layouts: 9.82 us -> 0 us
  waiting for transfers between devices: 23.5 us -> 20.5 us
  starting transfers between devices: 11.8 us -> 14.1 us
  Pallas kernels: 19.1 us -> 21.2 us
    unnamed x24 -> x0, local copies, waits for them, and re-layouts: 9.82 us -> none
    ppermute x1 -> x4, starting transfers between devices: 1.55 us -> 4.86 us  [shards(): other = [lax.ppermute(piece, 'bus', pairs) for piece in [net] + far]]
    ppermute x3, waiting for transfers between devices: 4.88 us -> 1.61 us  [shards(): far = [lax.ppermute(net, 'bus', shifted(step)) for step in range(1, half)]]
    pallas_call x1, Pallas kernels: 4.01 us -> 5.18 us  [shards(): pl.pallas_call(functools.partial(line_kernel, half=half), out_shape=(jax....]
    ppermute x1 -> x4, waiting for transfers between devices: 4.18 us -> 3.32 us  [shards(): other = [lax.ppermute(piece, 'bus', pairs) for piece in [net] + far]]
  transfers between devices with their start and end apart: 11 -> 14, of which waited for: 11 -> 9; matrix products, arithmetic and copies ran while one was open for 0% -> 0% of each run, Pallas kernels for 0% -> 0%
where the time goes in v4:
time: 64.7 us; the launch traced here: 64.5 us
  Pallas kernels  21.2 us (33%)
  waiting for transfers between devices  20.5 us (32%)
  starting transfers between devices  14.1 us (22%)
  blocking collectives  7.9 us (12%)
  between operations  0.69 us (1%)
    pallas_call x1, Pallas kernels, run_plan(): pl.pallas_call(functools.partial(plan_kernel, gens=gens, parts=parts), ou...  14.2 us
    all_to_all x1, blocking collectives, shards(): lax.all_to_all(plan, 'gen', split_axis=0, concat_axis=0, tiled=True)  7.9 us
    ppermute x3, waiting for transfers between devices, shards(): lax.ppermute(own_change, 'gen', [(i, (i + step) % parts) for i in range(p...  5.76 us
    pallas_call x1, Pallas kernels, shards(): pl.pallas_call(functools.partial(line_kernel, half=half), out_shape=(jax....  5.18 us
    ppermute x3, waiting for transfers between devices, shards(): lax.ppermute(share, 'bus', shifted(half - step)).astype(jnp.float32)  4.99 us
    ppermute x4, starting transfers between devices, shards(): other = [lax.ppermute(piece, 'bus', pairs) for piece in [net] + far]  4.86 us
    ppermute x1, waiting for transfers between devices, shards(): traded = lax.ppermute(far_part, 'bus', pairs)  4.76 us
    ppermute x3, starting transfers between devices, shards(): far = [lax.ppermute(net, 'bus', shifted(step)) for step in range(1, half)]  4.67 us
  transfers between devices with their start and end apart: 14, of which 9 were waited for; matrix products, arithmetic and copies ran while one was open for 0% of the time, Pallas kernels for 0%

profile of v4, /device:TPU:0, one launch (start us, length us, event | category | flops | bytes accessed | tf_op | source)
XLA Modules:
  0.0 64.5 jit_solution(12094870353092318565)
XLA Ops:
  0.6 14.2 %plan.1 = (f32[4,2,4,128]{3,2,1,0:T(4,128)S(1)}, f32[12,4,512]{2,1,0:T(4,128)S(1)}, bf16[6,16,128,128]{3,2,1,0:T(8,128)(2,1)S(1)}, f32[2,12,4,768]{3,2,1,0:T(4,1...) custom-call(s32[16]{0:T(128)} %refs_0_.1, s32[16]{0:T(128)} %refs_1_.1, s32[3,16,512]{2,1,0:T(8,128)} %bitcast.24, ...), custom_call_target="tpu_custom_call" | custom-call | tf_op jit(solution)/shard_map/plan/pallas_call | solution.py:169
  14.8 7.9 %all_to_all.5.plan_ref = f32[4,2,4,128]{3,2,1,0:T(4,128)S(1)} all-to-all(f32[4,2,4,128]{3,2,1,0:T(4,128)S(1)} %get-tuple-element.12), channel_id=1, replica_groups=mesh['gen'=4,'bus'=8] {'gen'}, dimensions={0} | all-to-all | bytes 32768 | tf_op jit(solution)/shard_map/all_to_all | solution.py:362
  22.7 0.5 net.1.own_ref
  23.2 3.7 %collective-permute-start.2 = (bf16[48,512]{1,0:T(8,128)(2,1)S(1)}, bf16[48,512]{1,0:T(8,128)(2,1)S(1)}, u32[]{:S(2)}, u32[]{:S(2)}) collective-permute-start(bf16[48,512]{1,0:T(8,128)(2,1)S(1)} %net.1.own_ref), channel_id=1, source_target_pairs={{0,6},{1,7},{2,0},{3,1},{4,2},{5,3},{6,4},{7,5},{8,14},{9,15},{10,... | collective-permute-start | bytes 147464 | tf_op jit(solution)/shard_map/ppermute | solution.py:372
  26.9 0.0 collective-permute-start.1
  26.9 1.0 %collective-permute-start = (bf16[48,512]{1,0:T(8,128)(2,1)S(1)}, bf16[48,512]{1,0:T(8,128)(2,1)}, u32[]{:S(2)}, u32[]{:S(2)}) collective-permute-start(bf16[48,512]{1,0:T(8,128)(2,1)S(1)} %net.1.own_ref), channel_id=1, source_target_pairs={{0,2},{1,3},{2,4},{3,5},{4,6},{5,7},{6,0},{7,1},{8,10},{9,11},{10,... | collective-permute-start | bytes 147464 | tf_op jit(solution)/shard_map/ppermute | solution.py:372
  27.9 1.5 %collective-permute-start.3 = (bf16[48,512]{1,0:T(8,128)(2,1)S(1)}, bf16[48,512]{1,0:T(8,128)(2,1)S(1)}, u32[]{:S(2)}, u32[]{:S(2)}) collective-permute-start(bf16[48,512]{1,0:T(8,128)(2,1)S(1)} %net.1.own_ref), channel_id=1, source_target_pairs={{0,1},{1,0},{2,3},{3,2},{4,5},{5,4},{6,7},{7,6},{8,9},{9,8},{10,11... | collective-permute-start | bytes 147464 | tf_op jit(solution)/shard_map/ppermute | solution.py:373
  29.4 0.0 collective-permute-done.2.refs_2_
  29.4 1.0 %collective-permute-start.6 = (bf16[48,512]{1,0:T(8,128)(2,1)S(1)}, bf16[48,512]{1,0:T(8,128)(2,1)S(1)}, u32[]{:S(2)}, u32[]{:S(2)}) collective-permute-start(bf16[48,512]{1,0:T(8,128)(2,1)S(1)} %collective-permute-done.2.refs_2_), channel_id=1, source_target_pairs={{0,1},{1,0},{2,3},{3,2},{4,5},{5,4},{6,7},{7,6},{8,9},{9,8},{10,11... | collective-permute-start | bytes 147464 | tf_op jit(solution)/shard_map/ppermute | solution.py:373
  30.4 1.6 %collective-permute-done.1.refs_1_ = bf16[48,512]{1,0:T(8,128)(2,1)} collective-permute-done((bf16[48,512]{1,0:T(8,128)(2,1)S(1)}, bf16[48,512]{1,0:T(8,128)(2,1)}, u32[]{:S(2)}, u32[]{:S(2)}) %collective-permute-start.1) | collective-permute-done | bytes 49184 | tf_op jit(solution)/shard_map/ppermute | solution.py:372
  32.0 1.5 %collective-permute-start.5 = (bf16[48,512]{1,0:T(8,128)(2,1)}, bf16[48,512]{1,0:T(8,128)(2,1)S(1)}, u32[]{:S(2)}, u32[]{:S(2)}) collective-permute-start(bf16[48,512]{1,0:T(8,128)(2,1)} %collective-permute-done.1.refs_1_), channel_id=1, source_target_pairs={{0,1},{1,0},{2,3},{3,2},{4,5},{5,4},{6,7},{7,6},{8,9},{9,8},{10,11... | collective-permute-start | bytes 147464 | tf_op jit(solution)/shard_map/ppermute | solution.py:373
  33.5 0.0 collective-permute-done.refs_0_
  33.5 0.9 %collective-permute-start.4 = (bf16[48,512]{1,0:T(8,128)(2,1)}, bf16[48,512]{1,0:T(8,128)(2,1)S(1)}, u32[]{:S(2)}, u32[]{:S(2)}) collective-permute-start(bf16[48,512]{1,0:T(8,128)(2,1)} %collective-permute-done.refs_0_), channel_id=1, source_target_pairs={{0,1},{1,0},{2,3},{3,2},{4,5},{5,4},{6,7},{7,6},{8,9},{9,8},{10,11... | collective-permute-start | bytes 147464 | tf_op jit(solution)/shard_map/ppermute | solution.py:373
  34.4 0.1 pad_add_fusion.place_smem
  34.5 0.0 collective-permute-done.3.refs_3_
  34.5 0.0 collective-permute-done.6.refs_6_
  34.5 1.8 %collective-permute-done.5.refs_5_ = bf16[48,512]{1,0:T(8,128)(2,1)S(1)} collective-permute-done((bf16[48,512]{1,0:T(8,128)(2,1)}, bf16[48,512]{1,0:T(8,128)(2,1)S(1)}, u32[]{:S(2)}, u32[]{:S(2)}) %collective-permute-start.5) | collective-permute-done | bytes 49184 | tf_op jit(solution)/shard_map/ppermute | solution.py:373
  36.3 1.5 %collective-permute-done.4.refs_4_ = bf16[48,512]{1,0:T(8,128)(2,1)S(1)} collective-permute-done((bf16[48,512]{1,0:T(8,128)(2,1)}, bf16[48,512]{1,0:T(8,128)(2,1)S(1)}, u32[]{:S(2)}, u32[]{:S(2)}) %collective-permute-start.4) | collective-permute-done | bytes 49184 | tf_op jit(solution)/shard_map/ppermute | solution.py:373
  37.8 5.2 %lines.1 = (f32[2,12,4,768]{3,2,1,0:T(4,128)}, f32[4,48,512]{2,1,0:T(8,128)S(1)}, bf16[4,48,512]{2,1,0:T(8,128)(2,1)S(1)}) custom-call(s32[6,16]{1,0:T(8,128)S(1)} %get-tuple-element.11.pattern_smem, s32[2]{0:T(128)S(1)} %pad_add_fusion.place_smem, bf16[48,512]{1,0:T(8,128)(2,1)S(1)} %net.1.own_ref, bf16[48,512]{1,0:T(8,128)(2,1)} %collective-permute-done.refs_0_, ...), custom_call_target="tpu_custom_call" | custom-call | tf_op jit(solution)/shard_map/lines/pallas_call | solution.py:374
  43.0 1.0 %collective-permute-start.7 = (bf16[4,48,512]{2,1,0:T(8,128)(2,1)S(1)}, bf16[4,48,512]{2,1,0:T(8,128)(2,1)S(1)}, u32[]{:S(2)}, u32[]{:S(2)}) collective-permute-start(bf16[4,48,512]{2,1,0:T(8,128)(2,1)S(1)} %get-tuple-element.19), channel_id=1, source_target_pairs={{0,1},{1,0},{2,3},{3,2},{4,5},{5,4},{6,7},{7,6},{8,9},{9,8},{10,11... | collective-permute-start | bytes 589832 | tf_op jit(solution)/shard_map/ppermute | solution.py:403
  43.9 4.8 %collective-permute-done.7 = bf16[4,48,512]{2,1,0:T(8,128)(2,1)S(1)} collective-permute-done((bf16[4,48,512]{2,1,0:T(8,128)(2,1)S(1)}, bf16[4,48,512]{2,1,0:T(8,128)(2,1)S(1)}, u32[]{:S(2)}, u32[]{:S(2)}) %collective-permute-start.7) | collective-permute-done | bytes 196640 | tf_op jit(solution)/shard_map/ppermute | solution.py:403
  48.8 2.1 %collective-permute-start.8 = (bf16[48,512]{1,0:T(8,128)(2,1)S(1)}, bf16[48,512]{1,0:T(8,128)(2,1)S(1)}, u32[]{:S(2)}, u32[]{:S(2)}) collective-permute-start(bf16[48,512]{1,0:T(8,128)(2,1)S(1)} %get-tuple-element.20), channel_id=1, source_target_pairs={{0,6},{1,7},{2,0},{3,1},{4,2},{5,3},{6,4},{7,5},{8,14},{9,15},{10,... | collective-permute-start | bytes 147464 | tf_op jit(solution)/shard_map/ppermute | solution.py:407
  50.9 0.0 collective-permute-start.10
  50.9 0.9 %collective-permute-start.9 = (bf16[48,512]{1,0:T(8,128)(2,1)S(1)}, bf16[48,512]{1,0:T(8,128)(2,1)S(1)}, u32[]{:S(2)}, u32[]{:S(2)}) collective-permute-start(bf16[48,512]{1,0:T(8,128)(2,1)S(1)} %get-tuple-element.22), channel_id=1, source_target_pairs={{0,4},{1,5},{2,6},{3,7},{4,0},{5,1},{6,2},{7,3},{8,12},{9,13},{10,... | collective-permute-start | bytes 147464 | tf_op jit(solution)/shard_map/ppermute | solution.py:407
  51.8 1.1 %collective-permute-done.8 = bf16[48,512]{1,0:T(8,128)(2,1)S(1)} collective-permute-done((bf16[48,512]{1,0:T(8,128)(2,1)S(1)}, bf16[48,512]{1,0:T(8,128)(2,1)S(1)}, u32[]{:S(2)}, u32[]{:S(2)}) %collective-permute-start.8) | collective-permute-done | bytes 49184 | tf_op jit(solution)/shard_map/ppermute | solution.py:407
  52.9 3.9 %collective-permute-done.10 = bf16[48,512]{1,0:T(8,128)(2,1)S(1)} collective-permute-done((bf16[48,512]{1,0:T(8,128)(2,1)S(1)}, bf16[48,512]{1,0:T(8,128)(2,1)S(1)}, u32[]{:S(2)}, u32[]{:S(2)}) %collective-permute-start.10) | collective-permute-done | bytes 49184 | tf_op jit(solution)/shard_map/ppermute | solution.py:407
  56.8 0.0 collective-permute-done.9
  56.8 0.1 collective-permute-start.13
  56.9 0.2 collective-permute-start.12
  57.1 0.3 collective-permute-start.11
  57.4 2.7 %collective-permute-done.13.refs_3_ = f32[48,512]{1,0:T(8,128)S(1)} collective-permute-done((f32[48,512]{1,0:T(8,128)S(1)}, f32[48,512]{1,0:T(8,128)S(1)}, u32[]{:S(2)}, u32[]{:S(2)}) %collective-permute-start.13) | collective-permute-done | bytes 98336 | tf_op jit(solution)/shard_map/ppermute | solution.py:409
  60.0 2.5 %collective-permute-done.12.refs_2_ = f32[48,512]{1,0:T(8,128)S(1)} collective-permute-done((f32[48,512]{1,0:T(8,128)S(1)}, f32[48,512]{1,0:T(8,128)S(1)}, u32[]{:S(2)}, u32[]{:S(2)}) %collective-permute-start.12) | collective-permute-done | bytes 98336 | tf_op jit(solution)/shard_map/ppermute | solution.py:409
  62.5 0.6 collective-permute-done.11.refs_1_
  63.1 1.4 %price.1 = f32[12,16,512]{2,1,0:T(8,128)} custom-call(s32[2]{0:T(128)S(1)} %pad_add_fusion.place_smem, f32[48,512]{1,0:T(8,128)S(1)} %fusion.1.refs_0_, f32[48,512]{1,0:T(8,128)S(1)} %collective-permute-done.11.refs_1_, f32[48,512]{1,0:T(8,128)S(1)} %collective-permute-done.12.refs_2_, f32[48,512]{1,0:T(8,128)S(1)} %collective-permute-done.13.refs_3_), custom_call_target="tpu_custom_call" | custom-call | tf_op jit(solution)/shard_map/price/pallas_call | solution.py:412
  (2 shorter events, 0.1 us)
Async XLA Ops:
  23.2 6.2 %collective-permute-start.2 = (bf16[48,512]{1,0:T(8,128)(2,1)S(1)}, bf16[48,512]{1,0:T(8,128)(2,1)S(1)}, u32[]{:S(2)}, u32[]{:S(2)}) collective-permute-start(bf16[48,512]{1,0:T(8,128)(2,1)S(1)} %net.1.own_ref), channel_id=1, source_target_pairs={{0,6},{1,7},{2,0},{3,1},{4,2},{5,3},{6,4},{7,5},{8,14},{9,15},{10,... | collective-permute-start | bytes 147464 | tf_op jit(solution)/shard_map/ppermute | solution.py:372
  26.9 5.1 %collective-permute-start.1 = (bf16[48,512]{1,0:T(8,128)(2,1)S(1)}, bf16[48,512]{1,0:T(8,128)(2,1)}, u32[]{:S(2)}, u32[]{:S(2)}) collective-permute-start(bf16[48,512]{1,0:T(8,128)(2,1)S(1)} %net.1.own_ref), channel_id=1, source_target_pairs={{0,4},{1,5},{2,6},{3,7},{4,0},{5,1},{6,2},{7,3},{8,12},{9,13},{10,... | collective-permute-start | bytes 147464 | tf_op jit(solution)/shard_map/ppermute | solution.py:372
  26.9 6.6 %collective-permute-start = (bf16[48,512]{1,0:T(8,128)(2,1)S(1)}, bf16[48,512]{1,0:T(8,128)(2,1)}, u32[]{:S(2)}, u32[]{:S(2)}) collective-permute-start(bf16[48,512]{1,0:T(8,128)(2,1)S(1)} %net.1.own_ref), channel_id=1, source_target_pairs={{0,2},{1,3},{2,4},{3,5},{4,6},{5,7},{6,0},{7,1},{8,10},{9,11},{10,... | collective-permute-start | bytes 147464 | tf_op jit(solution)/shard_map/ppermute | solution.py:372
  27.9 6.6 %collective-permute-start.3 = (bf16[48,512]{1,0:T(8,128)(2,1)S(1)}, bf16[48,512]{1,0:T(8,128)(2,1)S(1)}, u32[]{:S(2)}, u32[]{:S(2)}) collective-permute-start(bf16[48,512]{1,0:T(8,128)(2,1)S(1)} %net.1.own_ref), channel_id=1, source_target_pairs={{0,1},{1,0},{2,3},{3,2},{4,5},{5,4},{6,7},{7,6},{8,9},{9,8},{10,11... | collective-permute-start | bytes 147464 | tf_op jit(solution)/shard_map/ppermute | solution.py:373
  29.4 5.1 %collective-permute-start.6 = (bf16[48,512]{1,0:T(8,128)(2,1)S(1)}, bf16[48,512]{1,0:T(8,128)(2,1)S(1)}, u32[]{:S(2)}, u32[]{:S(2)}) collective-permute-start(bf16[48,512]{1,0:T(8,128)(2,1)S(1)} %collective-permute-done.2.refs_2_), channel_id=1, source_target_pairs={{0,1},{1,0},{2,3},{3,2},{4,5},{5,4},{6,7},{7,6},{8,9},{9,8},{10,11... | collective-permute-start | bytes 147464 | tf_op jit(solution)/shard_map/ppermute | solution.py:373
  32.0 4.3 %collective-permute-start.5 = (bf16[48,512]{1,0:T(8,128)(2,1)}, bf16[48,512]{1,0:T(8,128)(2,1)S(1)}, u32[]{:S(2)}, u32[]{:S(2)}) collective-permute-start(bf16[48,512]{1,0:T(8,128)(2,1)} %collective-permute-done.1.refs_1_), channel_id=1, source_target_pairs={{0,1},{1,0},{2,3},{3,2},{4,5},{5,4},{6,7},{7,6},{8,9},{9,8},{10,11... | collective-permute-start | bytes 147464 | tf_op jit(solution)/shard_map/ppermute | solution.py:373
  33.5 4.3 %collective-permute-start.4 = (bf16[48,512]{1,0:T(8,128)(2,1)}, bf16[48,512]{1,0:T(8,128)(2,1)S(1)}, u32[]{:S(2)}, u32[]{:S(2)}) collective-permute-start(bf16[48,512]{1,0:T(8,128)(2,1)} %collective-permute-done.refs_0_), channel_id=1, source_target_pairs={{0,1},{1,0},{2,3},{3,2},{4,5},{5,4},{6,7},{7,6},{8,9},{9,8},{10,11... | collective-permute-start | bytes 147464 | tf_op jit(solution)/shard_map/ppermute | solution.py:373
  43.0 5.7 %collective-permute-start.7 = (bf16[4,48,512]{2,1,0:T(8,128)(2,1)S(1)}, bf16[4,48,512]{2,1,0:T(8,128)(2,1)S(1)}, u32[]{:S(2)}, u32[]{:S(2)}) collective-permute-start(bf16[4,48,512]{2,1,0:T(8,128)(2,1)S(1)} %get-tuple-element.19), channel_id=1, source_target_pairs={{0,1},{1,0},{2,3},{3,2},{4,5},{5,4},{6,7},{7,6},{8,9},{9,8},{10,11... | collective-permute-start | bytes 589832 | tf_op jit(solution)/shard_map/ppermute | solution.py:403
  48.8 4.1 %collective-permute-start.8 = (bf16[48,512]{1,0:T(8,128)(2,1)S(1)}, bf16[48,512]{1,0:T(8,128)(2,1)S(1)}, u32[]{:S(2)}, u32[]{:S(2)}) collective-permute-start(bf16[48,512]{1,0:T(8,128)(2,1)S(1)} %get-tuple-element.20), channel_id=1, source_target_pairs={{0,6},{1,7},{2,0},{3,1},{4,2},{5,3},{6,4},{7,5},{8,14},{9,15},{10,... | collective-permute-start | bytes 147464 | tf_op jit(solution)/shard_map/ppermute | solution.py:407
  50.9 5.9 %collective-permute-start.10 = (bf16[48,512]{1,0:T(8,128)(2,1)S(1)}, bf16[48,512]{1,0:T(8,128)(2,1)S(1)}, u32[]{:S(2)}, u32[]{:S(2)}) collective-permute-start(bf16[48,512]{1,0:T(8,128)(2,1)S(1)} %get-tuple-element.21), channel_id=1, source_target_pairs={{0,2},{1,3},{2,4},{3,5},{4,6},{5,7},{6,0},{7,1},{8,10},{9,11},{10,... | collective-permute-start | bytes 147464 | tf_op jit(solution)/shard_map/ppermute | solution.py:407
  50.9 5.9 %collective-permute-start.9 = (bf16[48,512]{1,0:T(8,128)(2,1)S(1)}, bf16[48,512]{1,0:T(8,128)(2,1)S(1)}, u32[]{:S(2)}, u32[]{:S(2)}) collective-permute-start(bf16[48,512]{1,0:T(8,128)(2,1)S(1)} %get-tuple-element.22), channel_id=1, source_target_pairs={{0,4},{1,5},{2,6},{3,7},{4,0},{5,1},{6,2},{7,3},{8,12},{9,13},{10,... | collective-permute-start | bytes 147464 | tf_op jit(solution)/shard_map/ppermute | solution.py:407
  56.8 3.2 %collective-permute-start.13 = (f32[48,512]{1,0:T(8,128)S(1)}, f32[48,512]{1,0:T(8,128)S(1)}, u32[]{:S(2)}, u32[]{:S(2)}) collective-permute-start(f32[48,512]{1,0:T(8,128)S(1)} %fusion.1.refs_0_), channel_id=1, source_target_pairs={{0,24},{8,0},{16,8},{24,16},{1,25},{9,1},{17,9},{25,17},{2,26},{10... | collective-permute-start | bytes 294920 | tf_op jit(solution)/shard_map/ppermute | solution.py:409
  56.9 5.7 %collective-permute-start.12 = (f32[48,512]{1,0:T(8,128)S(1)}, f32[48,512]{1,0:T(8,128)S(1)}, u32[]{:S(2)}, u32[]{:S(2)}) collective-permute-start(f32[48,512]{1,0:T(8,128)S(1)} %fusion.1.refs_0_), channel_id=1, source_target_pairs={{0,16},{8,24},{16,0},{24,8},{1,17},{9,25},{17,1},{25,9},{2,18},{10... | collective-permute-start | bytes 294920 | tf_op jit(solution)/shard_map/ppermute | solution.py:409
  57.1 6.0 %collective-permute-start.11 = (f32[48,512]{1,0:T(8,128)S(1)}, f32[48,512]{1,0:T(8,128)S(1)}, u32[]{:S(2)}, u32[]{:S(2)}) collective-permute-start(f32[48,512]{1,0:T(8,128)S(1)} %fusion.1.refs_0_), channel_id=1, source_target_pairs={{0,8},{8,16},{16,24},{24,0},{1,9},{9,17},{17,25},{25,1},{2,10},{10... | collective-permute-start | bytes 294920 | tf_op jit(solution)/shard_map/ppermute | solution.py:409

commit v5 on v4

--- a/solution.py
+++ b/solution.py
@@ -242,23 +242,18 @@
     net_ref[...] = (injections - demand).astype(jnp.bfloat16)
 
 
-def line_kernel(
-    pattern_smem,
-    place_smem,
-    own_ref,
-    *refs,
-    half,
-):
-    net_refs, refs = (own_ref,) + refs[: 2 * half - 1], refs[2 * half - 1 :]
-    blocks_ref, limits_ref, old_ref, price_hbm, new_ref, near_out, far_out = refs[:7]
-    net_all, spread_all, price_ref, sem = refs[7:]
-    price_copy = pltpu.make_async_copy(price_hbm, price_ref, sem)
+def line_kernel(pattern_smem, *refs, half):
+    net_refs, refs = refs[: 2 * half], refs[2 * half :]
+    blocks_ref, limits_ref, old_ref, price_hbm, new_hbm, spread_all, far_out = refs[:7]
+    net_all, new_ref, price_ref, sems = refs[7:]
+    price_copy = pltpu.make_async_copy(price_hbm, price_ref, sems.at[0])
     price_copy.start()
+    new_copy = pltpu.make_async_copy(new_ref, new_hbm, sems.at[1])
     line_blocks, branches = pattern_smem.shape
     _, hours, scn_dev, _ = old_ref.shape
-    row_total, bus_dev = own_ref.shape
+    bus_dev = net_refs[0].shape[1]
     per_dev = bus_dev // BLK
-    me = place_smem[0]
+    me = lax.axis_index("bus")
     my_pair, my_side = me // 2, lax.rem(me, 2)
 
     for at, net_ref in enumerate(net_refs):
@@ -269,16 +264,19 @@
         block = pattern_smem[line, branch]
         owner = block // per_dev
         column = pl.multiple_of(lax.rem(block, per_dev) * BLK, BLK)
-        step = lax.rem(my_pair - owner // 2 + half, half)
+        step = lax.bitwise_xor(my_pair, owner // 2)
         side = jnp.where(lax.rem(owner, 2) == my_side, 0, half)
         return side + step, column
 
+    spots = [[spot(line, branch) for branch in range(branches)] for line in range(line_blocks)]
+    tables = [blocks_ref.at[line] for line in range(line_blocks)]
+    changes = []
     for line in range(line_blocks):
-        spots = [spot(line, branch) for branch in range(branches)]
-        picked = [net_all[at, :, pl.ds(column, BLK)] for at, column in spots]
-        table = blocks_ref[line].reshape(branches * BLK, BLK)
+        picked = [net_all[at, :, pl.ds(column, BLK)] for at, column in spots[line]]
         flow = jnp.dot(
-            jnp.concatenate(picked, axis=1), table, preferred_element_type=jnp.float32
+            jnp.concatenate(picked, axis=1),
+            tables[line][...].reshape(branches * BLK, BLK),
+            preferred_element_type=jnp.float32,
         )
         lanes = pl.ds(line * BLK, BLK)
         limit = limits_ref[lanes].reshape(1, BLK)
@@ -290,33 +288,74 @@
             here = slice(hour * scn_dev, (hour + 1) * scn_dev)
             new_ref[0, hour, :, lanes] = upper[here]
             new_ref[1, hour, :, lanes] = lower[here]
-        change = ((upper - upper_old) - (lower - lower_old)).astype(jnp.bfloat16)
+        changes.append(((upper - upper_old) - (lower - lower_old)).astype(jnp.bfloat16))
+    new_copy.start()
+    for line in range(line_blocks):
         spread = lax.dot_general(
-            change, table, (((1,), (1,)), ((), ())), preferred_element_type=jnp.float32
+            changes[line],
+            tables[line][...].reshape(branches * BLK, BLK),
+            (((1,), (1,)), ((), ())),
+            preferred_element_type=jnp.float32,
         )
-        for branch, (at, column) in enumerate(spots):
-            spread_all[at, :, pl.ds(column, BLK)] += spread[:, branch * BLK : (branch + 1) * BLK]
+        held = [spread_all[at, :, pl.ds(column, BLK)] for at, column in spots[line]]
+        for branch, (at, column) in enumerate(spots[line]):
+            spread_all[at, :, pl.ds(column, BLK)] = (
+                held[branch] + spread[:, branch * BLK : (branch + 1) * BLK]
+            )
     far_out[...] = spread_all[half:].astype(jnp.bfloat16)
-    near_out[...] = spread_all[:half]
     price_copy.wait()
-    part = place_smem[1]
+    part = lax.axis_index("gen")
     for hour in range(hours):
         price = price_ref[hour, :scn_dev, :]
         for other in range(1, price_ref.shape[1] // scn_dev):
             price = jnp.where(part == other, price_ref[hour, other * scn_dev : (other + 1) * scn_dev, :], price)
         here = slice(hour * scn_dev, (hour + 1) * scn_dev)
-        near_out[0, here, :] = spread_all[0, here, :] - price
-
-
-def price_kernel(place_smem, *refs):
+        spread_all[0, here, :] = spread_all[0, here, :] - price
+    new_copy.wait()
+
+
+def run_lines(pattern, nets, blocks, limits, old, bus_price):
+    ring = len(nets)
+    half = ring // 2
+    smem = pl.BlockSpec(memory_space=pltpu.SMEM)
+    vmem = pl.BlockSpec(memory_space=pltpu.VMEM)
+    hbm = pl.BlockSpec(memory_space=pltpu.HBM)
+    return pl.pallas_call(
+        functools.partial(line_kernel, half=half),
+        out_shape=(
+            jax.ShapeDtypeStruct(old.shape, jnp.float32),
+            jax.ShapeDtypeStruct((ring,) + nets[0].shape, jnp.float32),
+            jax.ShapeDtypeStruct((half,) + nets[0].shape, jnp.bfloat16),
+        ),
+        in_specs=[smem] + [vmem] * (ring + 3) + [hbm],
+        out_specs=(hbm, vmem, vmem),
+        scratch_shapes=[
+            pltpu.VMEM((ring,) + nets[0].shape, jnp.bfloat16),
+            pltpu.VMEM(old.shape, jnp.float32),
+            pltpu.VMEM(bus_price.shape, jnp.float32),
+            pltpu.SemaphoreType.DMA((2,)),
+        ],
+        compiler_params=pltpu.CompilerParams(vmem_limit_bytes=24 * 2**20),
+        name="lines",
+    )(
+        pattern,
+        *nets,
+        blocks,
+        limits,
+        old,
+        pltpu.with_memory_space_constraint(bus_price, pltpu.HBM),
+    )
+
+
+def price_kernel(*refs):
     share_refs, (out_ref, share_all) = refs[:-2], refs[-2:]
     hours = out_ref.shape[0]
     parts = len(share_refs)
     scn_dev = out_ref.shape[1] // parts
-    me = place_smem[1]
+    me = lax.axis_index("gen")
     for step, share in enumerate(share_refs):
         share_all[step] = share[...]
-    steps = [lax.rem(me - part + parts, parts) for part in range(parts)]
+    steps = [lax.bitwise_xor(me, part) for part in range(parts)]
     for hour in range(hours):
         less = [share_all[step, hour * scn_dev : (hour + 1) * scn_dev, :] for step in steps]
         out_ref[hour] = -jnp.concatenate(less, axis=0)
@@ -341,14 +380,11 @@
     half = ring // 2
     gens = state_level.shape[0]
     row_total = scn_dev * hours
-    place = jnp.stack([lax.axis_index("bus"), lax.axis_index("gen")]).astype(jnp.int32)
-    smem = pl.BlockSpec(memory_space=pltpu.SMEM)
     vmem = pl.BlockSpec(memory_space=pltpu.VMEM)
     roomy = pltpu.CompilerParams(vmem_limit_bytes=24 * 2**20)
-    pairs = [(i, i ^ 1) for i in range(ring)]
-
-    def shifted(step):
-        return [(i, (i + 2 * step) % ring) for i in range(ring)]
+
+    def trade(size, step):
+        return [(i, i ^ step) for i in range(size)]
 
     bus_price = jnp.transpose(bus_price, (1, 0, 2))
     bus_demand = jnp.transpose(bus_demand, (1, 0, 2))
@@ -369,55 +405,30 @@
         name="net",
     )(received, bus_demand)
 
-    far = [lax.ppermute(net, "bus", shifted(step)) for step in range(1, half)]
-    other = [lax.ppermute(piece, "bus", pairs) for piece in [net] + far]
-    new_multipliers, near_part, far_part = pl.pallas_call(
-        functools.partial(line_kernel, half=half),
-        out_shape=(
-            jax.ShapeDtypeStruct(multipliers.shape, jnp.float32),
-            jax.ShapeDtypeStruct((half, row_total, bus_dev), jnp.float32),
-            jax.ShapeDtypeStruct((half, row_total, bus_dev), jnp.bfloat16),
-        ),
-        in_specs=[smem, smem] + [vmem] * (ring + 3) + [pl.BlockSpec(memory_space=pltpu.HBM)],
-        out_specs=(vmem, vmem, vmem),
-        scratch_shapes=[
-            pltpu.VMEM((ring, row_total, bus_dev), jnp.bfloat16),
-            pltpu.VMEM((ring, row_total, bus_dev), jnp.float32),
-            pltpu.VMEM(bus_price.shape, jnp.float32),
-            pltpu.SemaphoreType.DMA,
-        ],
-        compiler_params=roomy,
-        name="lines",
-    )(
-        ptdf_pattern,
-        place,
-        net,
-        *far,
-        *other,
-        ptdf_blocks,
-        line_limits,
-        multipliers,
-        pltpu.with_memory_space_constraint(bus_price, pltpu.HBM),
-    )
-
-    traded = lax.ppermute(far_part, "bus", pairs)
-    own_change = near_part[0] + traded[0].astype(jnp.float32)
+    far = [lax.ppermute(net, "bus", trade(ring, 2 * step)) for step in range(1, half)]
+    other = [lax.ppermute(piece, "bus", trade(ring, 1)) for piece in [net] + far]
+    new_multipliers, spread, far_part = run_lines(
+        ptdf_pattern, [net] + far + other, ptdf_blocks, line_limits, multipliers, bus_price
+    )
+
+    traded = [lax.ppermute(far_part[step], "bus", trade(ring, 1)).astype(jnp.float32) for step in range(half)]
+    own_change = spread[0] + traded[0]
     for step in range(1, half):
-        share = (near_part[step] + traded[step].astype(jnp.float32)).astype(jnp.bfloat16)
-        own_change = own_change + lax.ppermute(share, "bus", shifted(half - step)).astype(jnp.float32)
-    shares = [own_change] + [
-        lax.ppermute(own_change, "gen", [(i, (i + step) % parts) for i in range(parts)])
-        for step in range(1, parts)
-    ]
+        share = (spread[step] + traded[step]).astype(jnp.bfloat16)
+        own_change = own_change + lax.ppermute(share, "bus", trade(ring, 2 * step)).astype(jnp.float32)
+    shares = [own_change]
+    for step in range(1, parts):
+        moved, by = (shares[step - 1], 1) if step % 2 else (own_change, step)
+        shares.append(lax.ppermute(moved, "gen", trade(parts, by)))
     new_price = pl.pallas_call(
         price_kernel,
         out_shape=jax.ShapeDtypeStruct(bus_price.shape, jnp.float32),
-        in_specs=[smem] + [vmem] * parts,
+        in_specs=[vmem] * parts,
         out_specs=vmem,
         scratch_shapes=[pltpu.VMEM((parts, row_total, bus_dev), jnp.float32)],
         compiler_params=roomy,
         name="price",
-    )(place, *shares)
+    )(*shares)
     return (jnp.transpose(new_multipliers, (0, 2, 1, 3)), jnp.transpose(new_price, (1, 0, 2)))
 
 

time: 64.7 us -> 62.8 us (0.971)
  waiting for transfers between devices: 20.5 us -> 17.1 us
  starting transfers between devices: 14.1 us -> 17.3 us
  Pallas kernels: 21.2 us -> 19.5 us
    ppermute x14 -> x17, waiting for transfers between devices: 20.5 us -> 17.1 us  [the longest x3 5.8 us: shards(): shares.append(lax.ppermute(moved, 'gen', trade(parts, by)))]
    ppermute x14 -> x17, starting transfers between devices: 14.1 us -> 17.3 us  [the longest x4 5 us: shards(): lax.ppermute(piece, 'bus', trade(ring, 1))]
    pallas_call x1, Pallas kernels: 5.18 us -> 4.02 us  [run_lines(): pl.pallas_call(functools.partial(line_kernel, half=half), out_shape=(jax....]
  transfers between devices with their start and end apart: 14 -> 17, of which waited for: 9 -> 11; matrix products, arithmetic and copies ran while one was open for 0% -> 0% of each run, Pallas kernels for 0% -> 0%
where the time goes in v5:
time: 62.8 us; the launch traced here: 62.6 us
  Pallas kernels  19.5 us (31%)
  starting transfers between devices  17.3 us (28%)
  waiting for transfers between devices  17.1 us (27%)
  blocking collectives  7.9 us (13%)
  between operations  0.7 us (1%)
    pallas_call x1, Pallas kernels, run_plan(): pl.pallas_call(functools.partial(plan_kernel, gens=gens, parts=parts), ou...  14.2 us
    all_to_all x1, blocking collectives, shards(): lax.all_to_all(plan, 'gen', split_axis=0, concat_axis=0, tiled=True)  7.9 us
    ppermute x3, waiting for transfers between devices, shards(): shares.append(lax.ppermute(moved, 'gen', trade(parts, by)))  5.8 us
    ppermute x4, starting transfers between devices, shards(): lax.ppermute(piece, 'bus', trade(ring, 1))  5 us
    ppermute x3, starting transfers between devices, shards(): lax.ppermute(net, 'bus', trade(ring, 2 * step))  4.45 us
    ppermute x3, waiting for transfers between devices, shards(): lax.ppermute(share, 'bus', trade(ring, 2 * step)).astype(jnp.float32)  4.44 us
    ppermute x4, starting transfers between devices, shards(): lax.ppermute(far_part[step], 'bus', trade(ring, 1)).astype(jnp.float32)  4.12 us
    pallas_call x1, Pallas kernels, run_lines(): pl.pallas_call(functools.partial(line_kernel, half=half), out_shape=(jax....  4.02 us
  transfers between devices with their start and end apart: 17, of which 11 were waited for; matrix products, arithmetic and copies ran while one was open for 0% of the time, Pallas kernels for 0%

profile of v5, /device:TPU:0, one launch (start us, length us, event | category | flops | bytes accessed | tf_op | source)
XLA Modules:
  0.0 62.6 jit_solution(16613469792485696639)
XLA Ops:
  0.6 14.2 %plan.1 = (f32[4,2,4,128]{3,2,1,0:T(4,128)S(1)}, f32[12,4,512]{2,1,0:T(4,128)S(1)}, bf16[6,16,128,128]{3,2,1,0:T(8,128)(2,1)S(1)}, f32[2,12,4,768]{3,2,1,0:T(4,1...) custom-call(s32[16]{0:T(128)} %refs_0_.1, s32[16]{0:T(128)} %refs_1_.1, s32[3,16,512]{2,1,0:T(8,128)} %bitcast.38, ...), custom_call_target="tpu_custom_call" | custom-call | tf_op jit(solution)/shard_map/plan/pallas_call | solution.py:169
  14.8 7.9 %all_to_all.5.plan_ref = f32[4,2,4,128]{3,2,1,0:T(4,128)S(1)} all-to-all(f32[4,2,4,128]{3,2,1,0:T(4,128)S(1)} %get-tuple-element.12), channel_id=1, replica_groups=mesh['gen'=4,'bus'=8] {'gen'}, dimensions={0} | all-to-all | bytes 32768 | tf_op jit(solution)/shard_map/all_to_all | solution.py:398
  22.7 0.5 net.1.refs_0_
  23.2 3.7 %collective-permute-start.2 = (bf16[48,512]{1,0:T(8,128)(2,1)S(1)}, bf16[48,512]{1,0:T(8,128)(2,1)S(1)}, u32[]{:S(2)}, u32[]{:S(2)}) collective-permute-start(bf16[48,512]{1,0:T(8,128)(2,1)S(1)} %net.1.refs_0_), channel_id=1, source_target_pairs={{0,6},{1,7},{2,4},{3,5},{4,2},{5,3},{6,0},{7,1},{8,14},{9,15},{10,... | collective-permute-start | bytes 147464 | tf_op jit(solution)/shard_map/ppermute | solution.py:408
  26.9 0.0 collective-permute-start.1
  26.9 0.8 %collective-permute-start = (bf16[48,512]{1,0:T(8,128)(2,1)S(1)}, bf16[48,512]{1,0:T(8,128)(2,1)S(1)}, u32[]{:S(2)}, u32[]{:S(2)}) collective-permute-start(bf16[48,512]{1,0:T(8,128)(2,1)S(1)} %net.1.refs_0_), channel_id=1, source_target_pairs={{0,2},{1,3},{2,0},{3,1},{4,6},{5,7},{6,4},{7,5},{8,10},{9,11},{10,... | collective-permute-start | bytes 147464 | tf_op jit(solution)/shard_map/ppermute | solution.py:408
  27.7 1.5 %collective-permute-start.3 = (bf16[48,512]{1,0:T(8,128)(2,1)S(1)}, bf16[48,512]{1,0:T(8,128)(2,1)S(1)}, u32[]{:S(2)}, u32[]{:S(2)}) collective-permute-start(bf16[48,512]{1,0:T(8,128)(2,1)S(1)} %net.1.refs_0_), channel_id=1, source_target_pairs={{0,1},{1,0},{2,3},{3,2},{4,5},{5,4},{6,7},{7,6},{8,9},{9,8},{10,11... | collective-permute-start | bytes 147464 | tf_op jit(solution)/shard_map/ppermute | solution.py:409
  29.2 0.3 collective-permute-done.2.refs_3_
  29.5 1.5 %collective-permute-start.6 = (bf16[48,512]{1,0:T(8,128)(2,1)S(1)}, bf16[48,512]{1,0:T(8,128)(2,1)S(1)}, u32[]{:S(2)}, u32[]{:S(2)}) collective-permute-start(bf16[48,512]{1,0:T(8,128)(2,1)S(1)} %collective-permute-done.2.refs_3_), channel_id=1, source_target_pairs={{0,1},{1,0},{2,3},{3,2},{4,5},{5,4},{6,7},{7,6},{8,9},{9,8},{10,11... | collective-permute-start | bytes 147464 | tf_op jit(solution)/shard_map/ppermute | solution.py:409
  31.0 0.9 %collective-permute-done.1.refs_2_ = bf16[48,512]{1,0:T(8,128)(2,1)S(1)} collective-permute-done((bf16[48,512]{1,0:T(8,128)(2,1)S(1)}, bf16[48,512]{1,0:T(8,128)(2,1)S(1)}, u32[]{:S(2)}, u32[]{:S(2)}) %collective-permute-start.1) | collective-permute-done | bytes 49184 | tf_op jit(solution)/shard_map/ppermute | solution.py:408
  31.9 1.5 %collective-permute-start.5 = (bf16[48,512]{1,0:T(8,128)(2,1)S(1)}, bf16[48,512]{1,0:T(8,128)(2,1)S(1)}, u32[]{:S(2)}, u32[]{:S(2)}) collective-permute-start(bf16[48,512]{1,0:T(8,128)(2,1)S(1)} %collective-permute-done.1.refs_2_), channel_id=1, source_target_pairs={{0,1},{1,0},{2,3},{3,2},{4,5},{5,4},{6,7},{7,6},{8,9},{9,8},{10,11... | collective-permute-start | bytes 147464 | tf_op jit(solution)/shard_map/ppermute | solution.py:409
  33.4 0.0 collective-permute-done.refs_1_
  33.4 0.5 collective-permute-start.4
  33.9 0.0 collective-permute-done.3.refs_4_
  33.9 0.0 collective-permute-done.6.refs_7_
  33.9 2.1 %collective-permute-done.5.refs_6_ = bf16[48,512]{1,0:T(8,128)(2,1)S(1)} collective-permute-done((bf16[48,512]{1,0:T(8,128)(2,1)S(1)}, bf16[48,512]{1,0:T(8,128)(2,1)S(1)}, u32[]{:S(2)}, u32[]{:S(2)}) %collective-permute-start.5) | collective-permute-done | bytes 49184 | tf_op jit(solution)/shard_map/ppermute | solution.py:409
  36.0 1.5 %collective-permute-done.4.refs_5_ = bf16[48,512]{1,0:T(8,128)(2,1)S(1)} collective-permute-done((bf16[48,512]{1,0:T(8,128)(2,1)S(1)}, bf16[48,512]{1,0:T(8,128)(2,1)S(1)}, u32[]{:S(2)}, u32[]{:S(2)}) %collective-permute-start.4) | collective-permute-done | bytes 49184 | tf_op jit(solution)/shard_map/ppermute | solution.py:409
  37.5 4.0 %lines.1 = (f32[2,12,4,768]{3,2,1,0:T(4,128)}, f32[8,48,512]{2,1,0:T(8,128)S(1)}, bf16[4,48,512]{2,1,0:T(8,128)(2,1)S(1)}) custom-call(s32[6,16]{1,0:T(8,128)S(1)} %get-tuple-element.11.pattern_smem, bf16[48,512]{1,0:T(8,128)(2,1)S(1)} %net.1.refs_0_, bf16[48,512]{1,0:T(8,128)(2,1)S(1)} %collective-permute-done.refs_1_, ...), custom_call_target="tpu_custom_call" | custom-call | tf_op jit(solution)/shard_map/lines/pallas_call | solution.py:323
  41.5 0.6 collective-permute-start.12
  42.1 1.5 %collective-permute-start.10 = (bf16[48,512]{1,0:T(8,128)(2,1)S(1)}, bf16[48,512]{1,0:T(8,128)(2,1)S(1)}, u32[]{:S(2)}, u32[]{:S(2)}) collective-permute-start(bf16[48,512]{1,0:T(8,128)(2,1)S(1)} %get-tuple-element.25), channel_id=1, source_target_pairs={{0,1},{1,0},{2,3},{3,2},{4,5},{5,4},{6,7},{7,6},{8,9},{9,8},{10,11... | collective-permute-start | bytes 147464 | tf_op jit(solution)/shard_map/ppermute | solution.py:414
  43.6 0.5 collective-permute-start.8
  44.2 1.5 %collective-permute-start.7 = (bf16[48,512]{1,0:T(8,128)(2,1)S(1)}, bf16[48,512]{1,0:T(8,128)(2,1)S(1)}, u32[]{:S(2)}, u32[]{:S(2)}) collective-permute-start(bf16[48,512]{1,0:T(8,128)(2,1)S(1)} %get-tuple-element.23), channel_id=1, source_target_pairs={{0,1},{1,0},{2,3},{3,2},{4,5},{5,4},{6,7},{7,6},{8,9},{9,8},{10,11... | collective-permute-start | bytes 147464 | tf_op jit(solution)/shard_map/ppermute | solution.py:414
  45.7 0.0 collective-permute-done.12
  45.7 0.5 collective-permute-done.10
  46.2 1.5 %collective-permute-done.8 = bf16[48,512]{1,0:T(8,128)(2,1)S(1)} collective-permute-done((bf16[48,512]{1,0:T(8,128)(2,1)S(1)}, bf16[48,512]{1,0:T(8,128)(2,1)S(1)}, u32[]{:S(2)}, u32[]{:S(2)}) %collective-permute-start.8) | collective-permute-done | bytes 49184 | tf_op jit(solution)/shard_map/ppermute | solution.py:414
  47.8 0.1 collective-permute-start.9
  47.8 2.4 %collective-permute-start.13 = (bf16[48,512]{1,0:T(8,128)(2,1)S(1)}, bf16[48,512]{1,0:T(8,128)(2,1)S(1)}, u32[]{:S(2)}, u32[]{:S(2)}) collective-permute-start(bf16[48,512]{1,0:T(8,128)(2,1)S(1)} %get-tuple-element.21), channel_id=1, source_target_pairs={{0,6},{1,7},{2,4},{3,5},{4,2},{5,3},{6,0},{7,1},{8,14},{9,15},{10,... | collective-permute-start | bytes 147464 | tf_op jit(solution)/shard_map/ppermute | solution.py:418
  50.2 1.1 %collective-permute-start.11 = (bf16[48,512]{1,0:T(8,128)(2,1)S(1)}, bf16[48,512]{1,0:T(8,128)(2,1)S(1)}, u32[]{:S(2)}, u32[]{:S(2)}) collective-permute-start(bf16[48,512]{1,0:T(8,128)(2,1)S(1)} %get-tuple-element.22), channel_id=1, source_target_pairs={{0,4},{1,5},{2,6},{3,7},{4,0},{5,1},{6,2},{7,3},{8,12},{9,13},{10,... | collective-permute-start | bytes 147464 | tf_op jit(solution)/shard_map/ppermute | solution.py:418
  51.3 0.0 collective-permute-done.7
  51.3 0.6 collective-permute-done.9
  51.9 2.0 %collective-permute-done.13 = bf16[48,512]{1,0:T(8,128)(2,1)S(1)} collective-permute-done((bf16[48,512]{1,0:T(8,128)(2,1)S(1)}, bf16[48,512]{1,0:T(8,128)(2,1)S(1)}, u32[]{:S(2)}, u32[]{:S(2)}) %collective-permute-start.13) | collective-permute-done | bytes 49184 | tf_op jit(solution)/shard_map/ppermute | solution.py:418
  53.9 1.9 %collective-permute-done.11 = bf16[48,512]{1,0:T(8,128)(2,1)S(1)} collective-permute-done((bf16[48,512]{1,0:T(8,128)(2,1)S(1)}, bf16[48,512]{1,0:T(8,128)(2,1)S(1)}, u32[]{:S(2)}, u32[]{:S(2)}) %collective-permute-start.11) | collective-permute-done | bytes 49184 | tf_op jit(solution)/shard_map/ppermute | solution.py:418
  55.8 0.2 collective-permute-start.15
  56.0 0.0 collective-permute-start.14
  56.0 4.5 %collective-permute-done.15.refs_2_ = f32[48,512]{1,0:T(8,128)S(1)} collective-permute-done((f32[48,512]{1,0:T(8,128)S(1)}, f32[48,512]{1,0:T(8,128)S(1)}, u32[]{:S(2)}, u32[]{:S(2)}) %collective-permute-start.15) | collective-permute-done | bytes 98336 | tf_op jit(solution)/shard_map/ppermute | solution.py:422
  60.5 0.0 collective-permute-start.16
  60.5 0.0 collective-permute-done.14.refs_1_
  60.5 1.3 %collective-permute-done.16.refs_3_ = f32[48,512]{1,0:T(8,128)S(1)} collective-permute-done((f32[48,512]{1,0:T(8,128)S(1)}, f32[48,512]{1,0:T(8,128)S(1)}, u32[]{:S(2)}, u32[]{:S(2)}) %collective-permute-start.16) | collective-permute-done | bytes 98336 | tf_op jit(solution)/shard_map/ppermute | solution.py:422
  61.8 0.8 %price.1 = f32[12,16,512]{2,1,0:T(8,128)} custom-call(f32[48,512]{1,0:T(8,128)S(1)} %fusion.5.refs_0_, f32[48,512]{1,0:T(8,128)S(1)} %collective-permute-done.14.refs_1_, f32[48,512]{1,0:T(8,128)S(1)} %collective-permute-done.15.refs_2_, f32[48,512]{1,0:T(8,128)S(1)} %collective-permute-done.16.refs_3_), custom_call_target="tpu_custom_call" | custom-call | tf_op jit(solution)/shard_map/price/pallas_call | solution.py:423
  (3 shorter events, 0.1 us)
Async XLA Ops:
  23.2 6.3 %collective-permute-start.2 = (bf16[48,512]{1,0:T(8,128)(2,1)S(1)}, bf16[48,512]{1,0:T(8,128)(2,1)S(1)}, u32[]{:S(2)}, u32[]{:S(2)}) collective-permute-start(bf16[48,512]{1,0:T(8,128)(2,1)S(1)} %net.1.refs_0_), channel_id=1, source_target_pairs={{0,6},{1,7},{2,4},{3,5},{4,2},{5,3},{6,0},{7,1},{8,14},{9,15},{10,... | collective-permute-start | bytes 147464 | tf_op jit(solution)/shard_map/ppermute | solution.py:408
  26.9 5.0 %collective-permute-start.1 = (bf16[48,512]{1,0:T(8,128)(2,1)S(1)}, bf16[48,512]{1,0:T(8,128)(2,1)S(1)}, u32[]{:S(2)}, u32[]{:S(2)}) collective-permute-start(bf16[48,512]{1,0:T(8,128)(2,1)S(1)} %net.1.refs_0_), channel_id=1, source_target_pairs={{0,4},{1,5},{2,6},{3,7},{4,0},{5,1},{6,2},{7,3},{8,12},{9,13},{10,... | collective-permute-start | bytes 147464 | tf_op jit(solution)/shard_map/ppermute | solution.py:408
  26.9 6.5 %collective-permute-start = (bf16[48,512]{1,0:T(8,128)(2,1)S(1)}, bf16[48,512]{1,0:T(8,128)(2,1)S(1)}, u32[]{:S(2)}, u32[]{:S(2)}) collective-permute-start(bf16[48,512]{1,0:T(8,128)(2,1)S(1)} %net.1.refs_0_), channel_id=1, source_target_pairs={{0,2},{1,3},{2,0},{3,1},{4,6},{5,7},{6,4},{7,5},{8,10},{9,11},{10,... | collective-permute-start | bytes 147464 | tf_op jit(solution)/shard_map/ppermute | solution.py:408
  27.7 6.2 %collective-permute-start.3 = (bf16[48,512]{1,0:T(8,128)(2,1)S(1)}, bf16[48,512]{1,0:T(8,128)(2,1)S(1)}, u32[]{:S(2)}, u32[]{:S(2)}) collective-permute-start(bf16[48,512]{1,0:T(8,128)(2,1)S(1)} %net.1.refs_0_), channel_id=1, source_target_pairs={{0,1},{1,0},{2,3},{3,2},{4,5},{5,4},{6,7},{7,6},{8,9},{9,8},{10,11... | collective-permute-start | bytes 147464 | tf_op jit(solution)/shard_map/ppermute | solution.py:409
  29.5 4.4 %collective-permute-start.6 = (bf16[48,512]{1,0:T(8,128)(2,1)S(1)}, bf16[48,512]{1,0:T(8,128)(2,1)S(1)}, u32[]{:S(2)}, u32[]{:S(2)}) collective-permute-start(bf16[48,512]{1,0:T(8,128)(2,1)S(1)} %collective-permute-done.2.refs_3_), channel_id=1, source_target_pairs={{0,1},{1,0},{2,3},{3,2},{4,5},{5,4},{6,7},{7,6},{8,9},{9,8},{10,11... | collective-permute-start | bytes 147464 | tf_op jit(solution)/shard_map/ppermute | solution.py:409
  31.9 4.1 %collective-permute-start.5 = (bf16[48,512]{1,0:T(8,128)(2,1)S(1)}, bf16[48,512]{1,0:T(8,128)(2,1)S(1)}, u32[]{:S(2)}, u32[]{:S(2)}) collective-permute-start(bf16[48,512]{1,0:T(8,128)(2,1)S(1)} %collective-permute-done.1.refs_2_), channel_id=1, source_target_pairs={{0,1},{1,0},{2,3},{3,2},{4,5},{5,4},{6,7},{7,6},{8,9},{9,8},{10,11... | collective-permute-start | bytes 147464 | tf_op jit(solution)/shard_map/ppermute | solution.py:409
  33.4 4.1 %collective-permute-start.4 = (bf16[48,512]{1,0:T(8,128)(2,1)S(1)}, bf16[48,512]{1,0:T(8,128)(2,1)S(1)}, u32[]{:S(2)}, u32[]{:S(2)}) collective-permute-start(bf16[48,512]{1,0:T(8,128)(2,1)S(1)} %collective-permute-done.refs_1_), channel_id=1, source_target_pairs={{0,1},{1,0},{2,3},{3,2},{4,5},{5,4},{6,7},{7,6},{8,9},{9,8},{10,11... | collective-permute-start | bytes 147464 | tf_op jit(solution)/shard_map/ppermute | solution.py:409
  41.5 4.2 %collective-permute-start.12 = (bf16[48,512]{1,0:T(8,128)(2,1)S(1)}, bf16[48,512]{1,0:T(8,128)(2,1)S(1)}, u32[]{:S(2)}, u32[]{:S(2)}) collective-permute-start(bf16[48,512]{1,0:T(8,128)(2,1)S(1)} %get-tuple-element.24), channel_id=1, source_target_pairs={{0,1},{1,0},{2,3},{3,2},{4,5},{5,4},{6,7},{7,6},{8,9},{9,8},{10,11... | collective-permute-start | bytes 147464 | tf_op jit(solution)/shard_map/ppermute | solution.py:414
  42.1 4.1 %collective-permute-start.10 = (bf16[48,512]{1,0:T(8,128)(2,1)S(1)}, bf16[48,512]{1,0:T(8,128)(2,1)S(1)}, u32[]{:S(2)}, u32[]{:S(2)}) collective-permute-start(bf16[48,512]{1,0:T(8,128)(2,1)S(1)} %get-tuple-element.25), channel_id=1, source_target_pairs={{0,1},{1,0},{2,3},{3,2},{4,5},{5,4},{6,7},{7,6},{8,9},{9,8},{10,11... | collective-permute-start | bytes 147464 | tf_op jit(solution)/shard_map/ppermute | solution.py:414
  43.6 4.1 %collective-permute-start.8 = (bf16[48,512]{1,0:T(8,128)(2,1)S(1)}, bf16[48,512]{1,0:T(8,128)(2,1)S(1)}, u32[]{:S(2)}, u32[]{:S(2)}) collective-permute-start(bf16[48,512]{1,0:T(8,128)(2,1)S(1)} %get-tuple-element.26), channel_id=1, source_target_pairs={{0,1},{1,0},{2,3},{3,2},{4,5},{5,4},{6,7},{7,6},{8,9},{9,8},{10,11... | collective-permute-start | bytes 147464 | tf_op jit(solution)/shard_map/ppermute | solution.py:414
  44.2 7.2 %collective-permute-start.7 = (bf16[48,512]{1,0:T(8,128)(2,1)S(1)}, bf16[48,512]{1,0:T(8,128)(2,1)S(1)}, u32[]{:S(2)}, u32[]{:S(2)}) collective-permute-start(bf16[48,512]{1,0:T(8,128)(2,1)S(1)} %get-tuple-element.23), channel_id=1, source_target_pairs={{0,1},{1,0},{2,3},{3,2},{4,5},{5,4},{6,7},{7,6},{8,9},{9,8},{10,11... | collective-permute-start | bytes 147464 | tf_op jit(solution)/shard_map/ppermute | solution.py:414
  47.8 4.2 %collective-permute-start.9 = (bf16[48,512]{1,0:T(8,128)(2,1)S(1)}, bf16[48,512]{1,0:T(8,128)(2,1)S(1)}, u32[]{:S(2)}, u32[]{:S(2)}) collective-permute-start(bf16[48,512]{1,0:T(8,128)(2,1)S(1)} %get-tuple-element.20), channel_id=1, source_target_pairs={{0,2},{1,3},{2,0},{3,1},{4,6},{5,7},{6,4},{7,5},{8,10},{9,11},{10,... | collective-permute-start | bytes 147464 | tf_op jit(solution)/shard_map/ppermute | solution.py:418
  47.8 6.1 %collective-permute-start.13 = (bf16[48,512]{1,0:T(8,128)(2,1)S(1)}, bf16[48,512]{1,0:T(8,128)(2,1)S(1)}, u32[]{:S(2)}, u32[]{:S(2)}) collective-permute-start(bf16[48,512]{1,0:T(8,128)(2,1)S(1)} %get-tuple-element.21), channel_id=1, source_target_pairs={{0,6},{1,7},{2,4},{3,5},{4,2},{5,3},{6,0},{7,1},{8,14},{9,15},{10,... | collective-permute-start | bytes 147464 | tf_op jit(solution)/shard_map/ppermute | solution.py:418
  50.2 5.5 %collective-permute-start.11 = (bf16[48,512]{1,0:T(8,128)(2,1)S(1)}, bf16[48,512]{1,0:T(8,128)(2,1)S(1)}, u32[]{:S(2)}, u32[]{:S(2)}) collective-permute-start(bf16[48,512]{1,0:T(8,128)(2,1)S(1)} %get-tuple-element.22), channel_id=1, source_target_pairs={{0,4},{1,5},{2,6},{3,7},{4,0},{5,1},{6,2},{7,3},{8,12},{9,13},{10,... | collective-permute-start | bytes 147464 | tf_op jit(solution)/shard_map/ppermute | solution.py:418
  55.8 4.7 %collective-permute-start.15 = (f32[48,512]{1,0:T(8,128)S(1)}, f32[48,512]{1,0:T(8,128)S(1)}, u32[]{:S(2)}, u32[]{:S(2)}) collective-permute-start(f32[48,512]{1,0:T(8,128)S(1)} %fusion.5.refs_0_), channel_id=1, source_target_pairs={{0,16},{8,24},{16,0},{24,8},{1,17},{9,25},{17,1},{25,9},{2,18},{10... | collective-permute-start | bytes 294920 | tf_op jit(solution)/shard_map/ppermute | solution.py:422
  56.0 4.5 %collective-permute-start.14 = (f32[48,512]{1,0:T(8,128)S(1)}, f32[48,512]{1,0:T(8,128)S(1)}, u32[]{:S(2)}, u32[]{:S(2)}) collective-permute-start(f32[48,512]{1,0:T(8,128)S(1)} %fusion.5.refs_0_), channel_id=1, source_target_pairs={{0,8},{8,0},{16,24},{24,16},{1,9},{9,1},{17,25},{25,17},{2,10},{10... | collective-permute-start | bytes 294920 | tf_op jit(solution)/shard_map/ppermute | solution.py:422
  60.5 1.3 %collective-permute-start.16 = (f32[48,512]{1,0:T(8,128)S(1)}, f32[48,512]{1,0:T(8,128)S(1)}, u32[]{:S(2)}, u32[]{:S(2)}) collective-permute-start(f32[48,512]{1,0:T(8,128)S(1)} %collective-permute-done.15.refs_2_), channel_id=1, source_target_pairs={{0,8},{8,0},{16,24},{24,16},{1,9},{9,1},{17,25},{25,17},{2,10},{10... | collective-permute-start | bytes 294920 | tf_op jit(solution)/shard_map/ppermute | solution.py:422

commit v6 on v5

--- a/solution.py
+++ b/solution.py
@@ -15,6 +15,7 @@
 BIG_GROUP = 6
 LANES = 128
 AHEAD = 5
+DIRECT = 1
 SUBLANES = 8
 EXACT = lax.Precision.HIGHEST
 
@@ -302,7 +303,8 @@
             spread_all[at, :, pl.ds(column, BLK)] = (
                 held[branch] + spread[:, branch * BLK : (branch + 1) * BLK]
             )
-    far_out[...] = spread_all[half:].astype(jnp.bfloat16)
+    far_out[:half] = spread_all[half:].astype(jnp.bfloat16)
+    far_out[half] = spread_all[DIRECT].astype(jnp.bfloat16)
     price_copy.wait()
     part = lax.axis_index("gen")
     for hour in range(hours):
@@ -325,7 +327,7 @@
         out_shape=(
             jax.ShapeDtypeStruct(old.shape, jnp.float32),
             jax.ShapeDtypeStruct((ring,) + nets[0].shape, jnp.float32),
-            jax.ShapeDtypeStruct((half,) + nets[0].shape, jnp.bfloat16),
+            jax.ShapeDtypeStruct((half + 1,) + nets[0].shape, jnp.bfloat16),
         ),
         in_specs=[smem] + [vmem] * (ring + 3) + [hbm],
         out_specs=(hbm, vmem, vmem),
@@ -406,16 +408,31 @@
     )(received, bus_demand)
 
     far = [lax.ppermute(net, "bus", trade(ring, 2 * step)) for step in range(1, half)]
-    other = [lax.ppermute(piece, "bus", trade(ring, 1)) for piece in [net] + far]
+    handed = [net] + far
+    other = [
+        lax.ppermute(net, "bus", trade(ring, 2 * step + 1))
+        if step == DIRECT
+        else lax.ppermute(handed[step], "bus", trade(ring, 1))
+        for step in range(half)
+    ]
     new_multipliers, spread, far_part = run_lines(
         ptdf_pattern, [net] + far + other, ptdf_blocks, line_limits, multipliers, bus_price
     )
 
-    traded = [lax.ppermute(far_part[step], "bus", trade(ring, 1)).astype(jnp.float32) for step in range(half)]
-    own_change = spread[0] + traded[0]
-    for step in range(1, half):
-        share = (spread[step] + traded[step]).astype(jnp.bfloat16)
-        own_change = own_change + lax.ppermute(share, "bus", trade(ring, 2 * step)).astype(jnp.float32)
+    own_change = spread[0]
+    for step in range(half):
+        if step == DIRECT:
+            shares = [
+                lax.ppermute(far_part[half], "bus", trade(ring, 2 * step)),
+                lax.ppermute(far_part[step], "bus", trade(ring, 2 * step + 1)),
+            ]
+        else:
+            shares = [lax.ppermute(far_part[step], "bus", trade(ring, 1))]
+            if step:
+                share = (spread[step] + shares[0].astype(jnp.float32)).astype(jnp.bfloat16)
+                shares = [lax.ppermute(share, "bus", trade(ring, 2 * step))]
+        for share in shares:
+            own_change = own_change + share.astype(jnp.float32)
     shares = [own_change]
     for step in range(1, parts):
         moved, by = (shares[step - 1], 1) if step % 2 else (own_change, step)

time: 62.8 us -> 61.6 us (0.981)
  waiting for transfers between devices: 17.1 us -> 14.3 us
  starting transfers between devices: 17.3 us -> 18.9 us
    ppermute x11, waiting for transfers between devices: 10.1 us -> 8.33 us  [the longest x2 5.54 us: shards(): shares = [lax.ppermute(share, 'bus', trade(ring, 2 * step))]]
    ppermute x11, starting transfers between devices: 12.7 us -> 13.8 us  [the longest x3 3.6 us: shards(): shares = [lax.ppermute(far_part[step], 'bus', trade(ring, 1))]]
    ppermute x3, waiting for transfers between devices: 1.23 us -> 0.11 us  [shards(): lax.ppermute(net, 'bus', trade(ring, 2 * step))]
  transfers between devices with their start and end apart: 17 -> 17, of which waited for: 11 -> 9; matrix products, arithmetic and copies ran while one was open for 0% -> 0% of each run, Pallas kernels for 0% -> 0%
where the time goes in v6:
time: 61.6 us; the launch traced here: 61.4 us
  Pallas kernels  19.5 us (32%)
  starting transfers between devices  18.9 us (31%)
  waiting for transfers between devices  14.3 us (23%)
  blocking collectives  7.9 us (13%)
  between operations  0.71 us (1%)
    pallas_call x1, Pallas kernels, run_plan(): pl.pallas_call(functools.partial(plan_kernel, gens=gens, parts=parts), ou...  14.2 us
    all_to_all x1, blocking collectives, shards(): lax.all_to_all(plan, 'gen', split_axis=0, concat_axis=0, tiled=True)  7.9 us
    ppermute x3, waiting for transfers between devices, shards(): shares.append(lax.ppermute(moved, 'gen', trade(parts, by)))  5.82 us
    ppermute x2, waiting for transfers between devices, shards(): shares = [lax.ppermute(share, 'bus', trade(ring, 2 * step))]  5.54 us
    ppermute x3, starting transfers between devices, shards(): lax.ppermute(net, 'bus', trade(ring, 2 * step))  4.92 us
    pallas_call x1, Pallas kernels, run_lines(): pl.pallas_call(functools.partial(line_kernel, half=half), out_shape=(jax....  4.01 us
    ppermute x3, starting transfers between devices, shards(): shares = [lax.ppermute(far_part[step], 'bus', trade(ring, 1))]  3.6 us
    ppermute x3, starting transfers between devices, shards(): lax.ppermute(handed[step], 'bus', trade(ring, 1))  3.52 us
  transfers between devices with their start and end apart: 17, of which 9 were waited for; matrix products, arithmetic and copies ran while one was open for 0% of the time, Pallas kernels for 0%

profile of v6, /device:TPU:0, one launch (start us, length us, event | category | flops | bytes accessed | tf_op | source)
XLA Modules:
  0.0 61.4 jit_solution(15825127440028428393)
XLA Ops:
  0.6 14.2 %plan.1 = (f32[4,2,4,128]{3,2,1,0:T(4,128)S(1)}, f32[12,4,512]{2,1,0:T(4,128)S(1)}, bf16[6,16,128,128]{3,2,1,0:T(8,128)(2,1)S(1)}, f32[2,12,4,768]{3,2,1,0:T(4,1...) custom-call(s32[16]{0:T(128)} %refs_0_.1, s32[16]{0:T(128)} %refs_1_.1, s32[3,16,512]{2,1,0:T(8,128)} %bitcast.38, ...), custom_call_target="tpu_custom_call" | custom-call | tf_op jit(solution)/shard_map/plan/pallas_call | solution.py:170
  14.8 7.9 %all_to_all.5.plan_ref = f32[4,2,4,128]{3,2,1,0:T(4,128)S(1)} all-to-all(f32[4,2,4,128]{3,2,1,0:T(4,128)S(1)} %get-tuple-element.12), channel_id=1, replica_groups=mesh['gen'=4,'bus'=8] {'gen'}, dimensions={0} | all-to-all | bytes 32768 | tf_op jit(solution)/shard_map/all_to_all | solution.py:400
  22.7 0.5 net.1.refs_0_
  23.2 3.7 %collective-permute-start.2 = (bf16[48,512]{1,0:T(8,128)(2,1)S(1)}, bf16[48,512]{1,0:T(8,128)(2,1)S(1)}, u32[]{:S(2)}, u32[]{:S(2)}) collective-permute-start(bf16[48,512]{1,0:T(8,128)(2,1)S(1)} %net.1.refs_0_), channel_id=1, source_target_pairs={{0,6},{1,7},{2,4},{3,5},{4,2},{5,3},{6,0},{7,1},{8,14},{9,15},{10,... | collective-permute-start | bytes 147464 | tf_op jit(solution)/shard_map/ppermute | solution.py:410
  26.9 0.0 collective-permute-start.1
  26.9 1.7 %collective-permute-start.4 = (bf16[48,512]{1,0:T(8,128)(2,1)S(1)}, bf16[48,512]{1,0:T(8,128)(2,1)S(1)}, u32[]{:S(2)}, u32[]{:S(2)}) collective-permute-start(bf16[48,512]{1,0:T(8,128)(2,1)S(1)} %net.1.refs_0_), channel_id=1, source_target_pairs={{0,3},{1,2},{2,1},{3,0},{4,7},{5,6},{6,5},{7,4},{8,11},{9,10},{10,... | collective-permute-start | bytes 147464 | tf_op jit(solution)/shard_map/ppermute | solution.py:413
  28.6 0.5 collective-permute-start.3
  29.2 1.2 %collective-permute-start = (bf16[48,512]{1,0:T(8,128)(2,1)S(1)}, bf16[48,512]{1,0:T(8,128)(2,1)S(1)}, u32[]{:S(2)}, u32[]{:S(2)}) collective-permute-start(bf16[48,512]{1,0:T(8,128)(2,1)S(1)} %net.1.refs_0_), channel_id=1, source_target_pairs={{0,2},{1,3},{2,0},{3,1},{4,6},{5,7},{6,4},{7,5},{8,10},{9,11},{10,... | collective-permute-start | bytes 147464 | tf_op jit(solution)/shard_map/ppermute | solution.py:410
  30.4 0.0 collective-permute-done.2.refs_3_
  30.4 1.5 %collective-permute-start.6 = (bf16[48,512]{1,0:T(8,128)(2,1)S(1)}, bf16[48,512]{1,0:T(8,128)(2,1)S(1)}, u32[]{:S(2)}, u32[]{:S(2)}) collective-permute-start(bf16[48,512]{1,0:T(8,128)(2,1)S(1)} %collective-permute-done.2.refs_3_), channel_id=1, source_target_pairs={{0,1},{1,0},{2,3},{3,2},{4,5},{5,4},{6,7},{7,6},{8,9},{9,8},{10,11... | collective-permute-start | bytes 147464 | tf_op jit(solution)/shard_map/ppermute | solution.py:415
  31.9 0.1 collective-permute-done.1.refs_2_
  32.0 1.5 %collective-permute-start.5 = (bf16[48,512]{1,0:T(8,128)(2,1)S(1)}, bf16[48,512]{1,0:T(8,128)(2,1)S(1)}, u32[]{:S(2)}, u32[]{:S(2)}) collective-permute-start(bf16[48,512]{1,0:T(8,128)(2,1)S(1)} %collective-permute-done.1.refs_2_), channel_id=1, source_target_pairs={{0,1},{1,0},{2,3},{3,2},{4,5},{5,4},{6,7},{7,6},{8,9},{9,8},{10,11... | collective-permute-start | bytes 147464 | tf_op jit(solution)/shard_map/ppermute | solution.py:415
  33.5 0.0 collective-permute-done.4.refs_5_
  33.5 0.0 collective-permute-done.3.refs_4_
  33.5 0.0 collective-permute-done.refs_1_
  33.5 1.0 %collective-permute-done.6.refs_7_ = bf16[48,512]{1,0:T(8,128)(2,1)S(1)} collective-permute-done((bf16[48,512]{1,0:T(8,128)(2,1)S(1)}, bf16[48,512]{1,0:T(8,128)(2,1)S(1)}, u32[]{:S(2)}, u32[]{:S(2)}) %collective-permute-start.6) | collective-permute-done | bytes 49184 | tf_op jit(solution)/shard_map/ppermute | solution.py:415
  34.5 1.6 %collective-permute-done.5.refs_6_ = bf16[48,512]{1,0:T(8,128)(2,1)S(1)} collective-permute-done((bf16[48,512]{1,0:T(8,128)(2,1)S(1)}, bf16[48,512]{1,0:T(8,128)(2,1)S(1)}, u32[]{:S(2)}, u32[]{:S(2)}) %collective-permute-start.5) | collective-permute-done | bytes 49184 | tf_op jit(solution)/shard_map/ppermute | solution.py:415
  36.1 4.0 %lines.1 = (f32[2,12,4,768]{3,2,1,0:T(4,128)}, f32[8,48,512]{2,1,0:T(8,128)S(1)}, bf16[5,48,512]{2,1,0:T(8,128)(2,1)S(1)}) custom-call(s32[6,16]{1,0:T(8,128)S(1)} %get-tuple-element.11.pattern_smem, bf16[48,512]{1,0:T(8,128)(2,1)S(1)} %net.1.refs_0_, bf16[48,512]{1,0:T(8,128)(2,1)S(1)} %collective-permute-done.refs_1_, ...), custom_call_target="tpu_custom_call" | custom-call | tf_op jit(solution)/shard_map/lines/pallas_call | solution.py:325
  40.1 1.6 %collective-permute-start.12 = (bf16[48,512]{1,0:T(8,128)(2,1)S(1)}, bf16[48,512]{1,0:T(8,128)(2,1)S(1)}, u32[]{:S(2)}, u32[]{:S(2)}) collective-permute-start(bf16[48,512]{1,0:T(8,128)(2,1)S(1)} %get-tuple-element.23), channel_id=1, source_target_pairs={{0,1},{1,0},{2,3},{3,2},{4,5},{5,4},{6,7},{7,6},{8,9},{9,8},{10,11... | collective-permute-start | bytes 147464 | tf_op jit(solution)/shard_map/ppermute | solution.py:430
  41.7 0.5 collective-permute-start.10
  42.2 1.5 %collective-permute-start.7 = (bf16[48,512]{1,0:T(8,128)(2,1)S(1)}, bf16[48,512]{1,0:T(8,128)(2,1)S(1)}, u32[]{:S(2)}, u32[]{:S(2)}) collective-permute-start(bf16[48,512]{1,0:T(8,128)(2,1)S(1)} %get-tuple-element.22), channel_id=1, source_target_pairs={{0,1},{1,0},{2,3},{3,2},{4,5},{5,4},{6,7},{7,6},{8,9},{9,8},{10,11... | collective-permute-start | bytes 147464 | tf_op jit(solution)/shard_map/ppermute | solution.py:430
  43.7 0.6 %collective-permute-start.9 = (bf16[48,512]{1,0:T(8,128)(2,1)S(1)}, bf16[48,512]{1,0:T(8,128)(2,1)S(1)}, u32[]{:S(2)}, u32[]{:S(2)}) collective-permute-start(bf16[48,512]{1,0:T(8,128)(2,1)S(1)} %get-tuple-element.25), channel_id=1, source_target_pairs={{0,3},{1,2},{2,1},{3,0},{4,7},{5,6},{6,5},{7,4},{8,11},{9,10},{10,... | collective-permute-start | bytes 147464 | tf_op jit(solution)/shard_map/ppermute | solution.py:427
  44.4 1.3 %collective-permute-start.8 = (bf16[48,512]{1,0:T(8,128)(2,1)S(1)}, bf16[48,512]{1,0:T(8,128)(2,1)S(1)}, u32[]{:S(2)}, u32[]{:S(2)}) collective-permute-start(bf16[48,512]{1,0:T(8,128)(2,1)S(1)} %get-tuple-element.26), channel_id=1, source_target_pairs={{0,2},{1,3},{2,0},{3,1},{4,6},{5,7},{6,4},{7,5},{8,10},{9,11},{10,... | collective-permute-start | bytes 147464 | tf_op jit(solution)/shard_map/ppermute | solution.py:426
  45.7 0.0 collective-permute-done.12
  45.7 0.1 collective-permute-done.10
  45.8 2.8 %collective-permute-start.11 = (bf16[48,512]{1,0:T(8,128)(2,1)S(1)}, bf16[48,512]{1,0:T(8,128)(2,1)S(1)}, u32[]{:S(2)}, u32[]{:S(2)}) collective-permute-start(bf16[48,512]{1,0:T(8,128)(2,1)S(1)} %get-tuple-element.20), channel_id=1, source_target_pairs={{0,4},{1,5},{2,6},{3,7},{4,0},{5,1},{6,2},{7,3},{8,12},{9,13},{10,... | collective-permute-start | bytes 147464 | tf_op jit(solution)/shard_map/ppermute | solution.py:433
  48.6 0.2 collective-permute-start.13
  48.9 0.0 collective-permute-done.7
  48.9 0.0 collective-permute-done.9
  48.9 0.1 collective-permute-done.8
  49.0 2.4 %collective-permute-done.11 = bf16[48,512]{1,0:T(8,128)(2,1)S(1)} collective-permute-done((bf16[48,512]{1,0:T(8,128)(2,1)S(1)}, bf16[48,512]{1,0:T(8,128)(2,1)S(1)}, u32[]{:S(2)}, u32[]{:S(2)}) %collective-permute-start.11) | collective-permute-done | bytes 49184 | tf_op jit(solution)/shard_map/ppermute | solution.py:433
  51.4 3.1 %collective-permute-done.13 = bf16[48,512]{1,0:T(8,128)(2,1)S(1)} collective-permute-done((bf16[48,512]{1,0:T(8,128)(2,1)S(1)}, bf16[48,512]{1,0:T(8,128)(2,1)S(1)}, u32[]{:S(2)}, u32[]{:S(2)}) %collective-permute-start.13) | collective-permute-done | bytes 49184 | tf_op jit(solution)/shard_map/ppermute | solution.py:433
  54.6 0.1 collective-permute-start.15
  54.7 0.1 collective-permute-start.14
  54.7 4.5 %collective-permute-done.15.refs_2_ = f32[48,512]{1,0:T(8,128)S(1)} collective-permute-done((f32[48,512]{1,0:T(8,128)S(1)}, f32[48,512]{1,0:T(8,128)S(1)}, u32[]{:S(2)}, u32[]{:S(2)}) %collective-permute-start.15) | collective-permute-done | bytes 98336 | tf_op jit(solution)/shard_map/ppermute | solution.py:439
  59.3 0.0 collective-permute-start.16
  59.3 0.0 collective-permute-done.14.refs_1_
  59.3 1.3 %collective-permute-done.16.refs_3_ = f32[48,512]{1,0:T(8,128)S(1)} collective-permute-done((f32[48,512]{1,0:T(8,128)S(1)}, f32[48,512]{1,0:T(8,128)S(1)}, u32[]{:S(2)}, u32[]{:S(2)}) %collective-permute-start.16) | collective-permute-done | bytes 98336 | tf_op jit(solution)/shard_map/ppermute | solution.py:439
  60.6 0.8 %price.1 = f32[12,16,512]{2,1,0:T(8,128)} custom-call(f32[48,512]{1,0:T(8,128)S(1)} %fusion.5.refs_0_, f32[48,512]{1,0:T(8,128)S(1)} %collective-permute-done.14.refs_1_, f32[48,512]{1,0:T(8,128)S(1)} %collective-permute-done.15.refs_2_, f32[48,512]{1,0:T(8,128)S(1)} %collective-permute-done.16.refs_3_), custom_call_target="tpu_custom_call" | custom-call | tf_op jit(solution)/shard_map/price/pallas_call | solution.py:440
  (3 shorter events, 0.1 us)
Async XLA Ops:
  23.2 7.2 %collective-permute-start.2 = (bf16[48,512]{1,0:T(8,128)(2,1)S(1)}, bf16[48,512]{1,0:T(8,128)(2,1)S(1)}, u32[]{:S(2)}, u32[]{:S(2)}) collective-permute-start(bf16[48,512]{1,0:T(8,128)(2,1)S(1)} %net.1.refs_0_), channel_id=1, source_target_pairs={{0,6},{1,7},{2,4},{3,5},{4,2},{5,3},{6,0},{7,1},{8,14},{9,15},{10,... | collective-permute-start | bytes 147464 | tf_op jit(solution)/shard_map/ppermute | solution.py:410
  26.9 5.1 %collective-permute-start.1 = (bf16[48,512]{1,0:T(8,128)(2,1)S(1)}, bf16[48,512]{1,0:T(8,128)(2,1)S(1)}, u32[]{:S(2)}, u32[]{:S(2)}) collective-permute-start(bf16[48,512]{1,0:T(8,128)(2,1)S(1)} %net.1.refs_0_), channel_id=1, source_target_pairs={{0,4},{1,5},{2,6},{3,7},{4,0},{5,1},{6,2},{7,3},{8,12},{9,13},{10,... | collective-permute-start | bytes 147464 | tf_op jit(solution)/shard_map/ppermute | solution.py:410
  26.9 6.6 %collective-permute-start.4 = (bf16[48,512]{1,0:T(8,128)(2,1)S(1)}, bf16[48,512]{1,0:T(8,128)(2,1)S(1)}, u32[]{:S(2)}, u32[]{:S(2)}) collective-permute-start(bf16[48,512]{1,0:T(8,128)(2,1)S(1)} %net.1.refs_0_), channel_id=1, source_target_pairs={{0,3},{1,2},{2,1},{3,0},{4,7},{5,6},{6,5},{7,4},{8,11},{9,10},{10,... | collective-permute-start | bytes 147464 | tf_op jit(solution)/shard_map/ppermute | solution.py:413
  28.6 4.9 %collective-permute-start.3 = (bf16[48,512]{1,0:T(8,128)(2,1)S(1)}, bf16[48,512]{1,0:T(8,128)(2,1)S(1)}, u32[]{:S(2)}, u32[]{:S(2)}) collective-permute-start(bf16[48,512]{1,0:T(8,128)(2,1)S(1)} %net.1.refs_0_), channel_id=1, source_target_pairs={{0,1},{1,0},{2,3},{3,2},{4,5},{5,4},{6,7},{7,6},{8,9},{9,8},{10,11... | collective-permute-start | bytes 147464 | tf_op jit(solution)/shard_map/ppermute | solution.py:415
  29.2 4.4 %collective-permute-start = (bf16[48,512]{1,0:T(8,128)(2,1)S(1)}, bf16[48,512]{1,0:T(8,128)(2,1)S(1)}, u32[]{:S(2)}, u32[]{:S(2)}) collective-permute-start(bf16[48,512]{1,0:T(8,128)(2,1)S(1)} %net.1.refs_0_), channel_id=1, source_target_pairs={{0,2},{1,3},{2,0},{3,1},{4,6},{5,7},{6,4},{7,5},{8,10},{9,11},{10,... | collective-permute-start | bytes 147464 | tf_op jit(solution)/shard_map/ppermute | solution.py:410
  30.4 4.1 %collective-permute-start.6 = (bf16[48,512]{1,0:T(8,128)(2,1)S(1)}, bf16[48,512]{1,0:T(8,128)(2,1)S(1)}, u32[]{:S(2)}, u32[]{:S(2)}) collective-permute-start(bf16[48,512]{1,0:T(8,128)(2,1)S(1)} %collective-permute-done.2.refs_3_), channel_id=1, source_target_pairs={{0,1},{1,0},{2,3},{3,2},{4,5},{5,4},{6,7},{7,6},{8,9},{9,8},{10,11... | collective-permute-start | bytes 147464 | tf_op jit(solution)/shard_map/ppermute | solution.py:415
  32.0 4.1 %collective-permute-start.5 = (bf16[48,512]{1,0:T(8,128)(2,1)S(1)}, bf16[48,512]{1,0:T(8,128)(2,1)S(1)}, u32[]{:S(2)}, u32[]{:S(2)}) collective-permute-start(bf16[48,512]{1,0:T(8,128)(2,1)S(1)} %collective-permute-done.1.refs_2_), channel_id=1, source_target_pairs={{0,1},{1,0},{2,3},{3,2},{4,5},{5,4},{6,7},{7,6},{8,9},{9,8},{10,11... | collective-permute-start | bytes 147464 | tf_op jit(solution)/shard_map/ppermute | solution.py:415
  40.1 5.6 %collective-permute-start.12 = (bf16[48,512]{1,0:T(8,128)(2,1)S(1)}, bf16[48,512]{1,0:T(8,128)(2,1)S(1)}, u32[]{:S(2)}, u32[]{:S(2)}) collective-permute-start(bf16[48,512]{1,0:T(8,128)(2,1)S(1)} %get-tuple-element.23), channel_id=1, source_target_pairs={{0,1},{1,0},{2,3},{3,2},{4,5},{5,4},{6,7},{7,6},{8,9},{9,8},{10,11... | collective-permute-start | bytes 147464 | tf_op jit(solution)/shard_map/ppermute | solution.py:430
  41.7 4.1 %collective-permute-start.10 = (bf16[48,512]{1,0:T(8,128)(2,1)S(1)}, bf16[48,512]{1,0:T(8,128)(2,1)S(1)}, u32[]{:S(2)}, u32[]{:S(2)}) collective-permute-start(bf16[48,512]{1,0:T(8,128)(2,1)S(1)} %get-tuple-element.24), channel_id=1, source_target_pairs={{0,1},{1,0},{2,3},{3,2},{4,5},{5,4},{6,7},{7,6},{8,9},{9,8},{10,11... | collective-permute-start | bytes 147464 | tf_op jit(solution)/shard_map/ppermute | solution.py:430
  42.2 6.6 %collective-permute-start.7 = (bf16[48,512]{1,0:T(8,128)(2,1)S(1)}, bf16[48,512]{1,0:T(8,128)(2,1)S(1)}, u32[]{:S(2)}, u32[]{:S(2)}) collective-permute-start(bf16[48,512]{1,0:T(8,128)(2,1)S(1)} %get-tuple-element.22), channel_id=1, source_target_pairs={{0,1},{1,0},{2,3},{3,2},{4,5},{5,4},{6,7},{7,6},{8,9},{9,8},{10,11... | collective-permute-start | bytes 147464 | tf_op jit(solution)/shard_map/ppermute | solution.py:430
  43.7 5.1 %collective-permute-start.9 = (bf16[48,512]{1,0:T(8,128)(2,1)S(1)}, bf16[48,512]{1,0:T(8,128)(2,1)S(1)}, u32[]{:S(2)}, u32[]{:S(2)}) collective-permute-start(bf16[48,512]{1,0:T(8,128)(2,1)S(1)} %get-tuple-element.25), channel_id=1, source_target_pairs={{0,3},{1,2},{2,1},{3,0},{4,7},{5,6},{6,5},{7,4},{8,11},{9,10},{10,... | collective-permute-start | bytes 147464 | tf_op jit(solution)/shard_map/ppermute | solution.py:427
  44.4 4.6 %collective-permute-start.8 = (bf16[48,512]{1,0:T(8,128)(2,1)S(1)}, bf16[48,512]{1,0:T(8,128)(2,1)S(1)}, u32[]{:S(2)}, u32[]{:S(2)}) collective-permute-start(bf16[48,512]{1,0:T(8,128)(2,1)S(1)} %get-tuple-element.26), channel_id=1, source_target_pairs={{0,2},{1,3},{2,0},{3,1},{4,6},{5,7},{6,4},{7,5},{8,10},{9,11},{10,... | collective-permute-start | bytes 147464 | tf_op jit(solution)/shard_map/ppermute | solution.py:426
  45.8 5.6 %collective-permute-start.11 = (bf16[48,512]{1,0:T(8,128)(2,1)S(1)}, bf16[48,512]{1,0:T(8,128)(2,1)S(1)}, u32[]{:S(2)}, u32[]{:S(2)}) collective-permute-start(bf16[48,512]{1,0:T(8,128)(2,1)S(1)} %get-tuple-element.20), channel_id=1, source_target_pairs={{0,4},{1,5},{2,6},{3,7},{4,0},{5,1},{6,2},{7,3},{8,12},{9,13},{10,... | collective-permute-start | bytes 147464 | tf_op jit(solution)/shard_map/ppermute | solution.py:433
  48.6 5.9 %collective-permute-start.13 = (bf16[48,512]{1,0:T(8,128)(2,1)S(1)}, bf16[48,512]{1,0:T(8,128)(2,1)S(1)}, u32[]{:S(2)}, u32[]{:S(2)}) collective-permute-start(bf16[48,512]{1,0:T(8,128)(2,1)S(1)} %get-tuple-element.21), channel_id=1, source_target_pairs={{0,6},{1,7},{2,4},{3,5},{4,2},{5,3},{6,0},{7,1},{8,14},{9,15},{10,... | collective-permute-start | bytes 147464 | tf_op jit(solution)/shard_map/ppermute | solution.py:433
  54.6 4.7 %collective-permute-start.15 = (f32[48,512]{1,0:T(8,128)S(1)}, f32[48,512]{1,0:T(8,128)S(1)}, u32[]{:S(2)}, u32[]{:S(2)}) collective-permute-start(f32[48,512]{1,0:T(8,128)S(1)} %fusion.5.refs_0_), channel_id=1, source_target_pairs={{0,16},{8,24},{16,0},{24,8},{1,17},{9,25},{17,1},{25,9},{2,18},{10... | collective-permute-start | bytes 294920 | tf_op jit(solution)/shard_map/ppermute | solution.py:439
  54.7 4.6 %collective-permute-start.14 = (f32[48,512]{1,0:T(8,128)S(1)}, f32[48,512]{1,0:T(8,128)S(1)}, u32[]{:S(2)}, u32[]{:S(2)}) collective-permute-start(f32[48,512]{1,0:T(8,128)S(1)} %fusion.5.refs_0_), channel_id=1, source_target_pairs={{0,8},{8,0},{16,24},{24,16},{1,9},{9,1},{17,25},{25,17},{2,10},{10... | collective-permute-start | bytes 294920 | tf_op jit(solution)/shard_map/ppermute | solution.py:439
  59.3 1.3 %collective-permute-start.16 = (f32[48,512]{1,0:T(8,128)S(1)}, f32[48,512]{1,0:T(8,128)S(1)}, u32[]{:S(2)}, u32[]{:S(2)}) collective-permute-start(f32[48,512]{1,0:T(8,128)S(1)} %collective-permute-done.15.refs_2_), channel_id=1, source_target_pairs={{0,8},{8,0},{16,24},{24,16},{1,9},{9,1},{17,25},{25,17},{2,10},{10... | collective-permute-start | bytes 294920 | tf_op jit(solution)/shard_map/ppermute | solution.py:439

commit v7 on v6

--- a/solution.py
+++ b/solution.py
@@ -17,7 +17,19 @@
 AHEAD = 5
 DIRECT = 1
 SUBLANES = 8
-EXACT = lax.Precision.HIGHEST
+
+
+def exact_pieces(values):
+    high = values.astype(jnp.bfloat16)
+    rest = values - high.astype(jnp.float32)
+    middle = rest.astype(jnp.bfloat16)
+    low = (rest - middle.astype(jnp.float32)).astype(jnp.bfloat16)
+    return jnp.concatenate([high, middle, low], axis=0)
+
+
+def add_pieces(product):
+    count = product.shape[0] // 3
+    return product[:count] + (product[count : 2 * count] + product[2 * count :])
 
 
 def plan_kernel(*refs, gens, parts):
@@ -76,15 +88,13 @@
         bus_row = jnp.where(lane == slot, local, bus_row)
     chooser = (
         lax.broadcasted_iota(jnp.int32, (bus_dev, LANES), 0) == local_row
-    ).astype(jnp.float32)
-    for hour in range(hours):
-        gen_price[hour] = lax.dot_general(
-            price_ref[hour],
-            chooser,
-            (((1,), (0,)), ((), ())),
-            precision=EXACT,
-            preferred_element_type=jnp.float32,
-        )
+    ).astype(jnp.bfloat16)
+    picked = jnp.dot(
+        exact_pieces(price_ref[...].reshape(hours * scn, bus_dev)),
+        chooser,
+        preferred_element_type=jnp.float32,
+    )
+    gen_price[...] = add_pieces(picked).reshape(hours, scn, LANES)
 
     state_ids = lax.broadcasted_iota(jnp.int32, (1, STATES), 1)
     spans = []
@@ -110,6 +120,7 @@
     def repeat_rows(block, copies):
         return block if copies == 1 else jnp.concatenate([block] * copies, axis=0)
 
+    shares = [None] * gens
     outs = [jnp.zeros((scn, LANES), jnp.float32) for _ in range(-(-hours // per_row))]
     for hour in range(hours - 1, -1, -1):
         chains = hours - 1 - hour
@@ -123,12 +134,12 @@
             cost = repeat_rows(cost_slot[slot][:, :span], scn // SUBLANES)
             price = gen_price[hour][:, slot : slot + 1]
             weight = jnp.exp(price * level - cost)
+            if chains > 0:
+                weight = weight * shares[slot]
             base = weight if chains == 0 else weight * state[:scn, :]
             total = jnp.sum(base, axis=-1, keepdims=True)
             if hour > 0:
-                share = 1.0 / total
-                base = base * share
-                weight = weight * share
+                shares[slot] = 1.0 / total
                 pieces = [base.astype(jnp.bfloat16)]
                 for chain in range(chains):
                     pieces.append(
@@ -227,18 +238,13 @@
             shift *= 2
         places.append((bus_ids == bus[:1, :]).astype(jnp.bfloat16))
     left = jnp.concatenate(left, axis=1)
-    high = left.astype(jnp.bfloat16)
-    rest = left - high.astype(jnp.float32)
-    middle = rest.astype(jnp.bfloat16)
-    low = (rest - middle.astype(jnp.float32)).astype(jnp.bfloat16)
     placed = lax.dot_general(
-        jnp.concatenate([high, middle, low], axis=0),
+        exact_pieces(left),
         jnp.concatenate(places, axis=1),
         (((1,), (1,)), ((), ())),
         preferred_element_type=jnp.float32,
     )
-    count = left.shape[0]
-    injections = placed[:count] + (placed[count : 2 * count] + placed[2 * count :])
+    injections = add_pieces(placed)
     demand = jnp.concatenate([demand_ref[hour] for hour in range(hours)], axis=0)
     net_ref[...] = (injections - demand).astype(jnp.bfloat16)
 

time: 61.6 us -> 58.1 us (0.943)
  Pallas kernels: 19.5 us -> 16 us
    pallas_call x1, Pallas kernels: 14.2 us -> 10.6 us  [run_plan(): pl.pallas_call(functools.partial(plan_kernel, gens=gens, parts=parts), ou...]
where the time goes in v7:
time: 58.1 us; the launch traced here: 57.8 us
  starting transfers between devices  18.9 us (33%)
  Pallas kernels  16 us (28%)
  waiting for transfers between devices  14.3 us (25%)
  blocking collectives  7.9 us (14%)
  between operations  0.71 us (1%)
    pallas_call x1, Pallas kernels, run_plan(): pl.pallas_call(functools.partial(plan_kernel, gens=gens, parts=parts), ou...  10.6 us
    all_to_all x1, blocking collectives, shards(): lax.all_to_all(plan, 'gen', split_axis=0, concat_axis=0, tiled=True)  7.9 us
    ppermute x3, waiting for transfers between devices, shards(): shares.append(lax.ppermute(moved, 'gen', trade(parts, by)))  5.82 us
    ppermute x2, waiting for transfers between devices, shards(): shares = [lax.ppermute(share, 'bus', trade(ring, 2 * step))]  5.53 us
    ppermute x3, starting transfers between devices, shards(): lax.ppermute(net, 'bus', trade(ring, 2 * step))  4.92 us
    pallas_call x1, Pallas kernels, run_lines(): pl.pallas_call(functools.partial(line_kernel, half=half), out_shape=(jax....  4.01 us
    ppermute x3, starting transfers between devices, shards(): shares = [lax.ppermute(far_part[step], 'bus', trade(ring, 1))]  3.58 us
    ppermute x3, starting transfers between devices, shards(): lax.ppermute(handed[step], 'bus', trade(ring, 1))  3.5 us
  transfers between devices with their start and end apart: 17, of which 9 were waited for; matrix products, arithmetic and copies ran while one was open for 0% of the time, Pallas kernels for 0%

profile of v7, /device:TPU:0, one launch (start us, length us, event | category | flops | bytes accessed | tf_op | source)
XLA Modules:
  0.0 57.8 jit_solution(2294038041712010621)
XLA Ops:
  0.6 10.6 %plan.1 = (f32[4,2,4,128]{3,2,1,0:T(4,128)S(1)}, f32[12,4,512]{2,1,0:T(4,128)S(1)}, bf16[6,16,128,128]{3,2,1,0:T(8,128)(2,1)S(1)}, f32[2,12,4,768]{3,2,1,0:T(4,1...) custom-call(s32[16]{0:T(128)} %refs_0_.1, s32[16]{0:T(128)} %refs_1_.1, s32[3,16,512]{2,1,0:T(8,128)} %bitcast.38, ...), custom_call_target="tpu_custom_call" | custom-call | tf_op jit(solution)/shard_map/plan/pallas_call | solution.py:181
  11.3 7.9 %all_to_all.5.plan_ref = f32[4,2,4,128]{3,2,1,0:T(4,128)S(1)} all-to-all(f32[4,2,4,128]{3,2,1,0:T(4,128)S(1)} %get-tuple-element.12), channel_id=1, replica_groups=mesh['gen'=4,'bus'=8] {'gen'}, dimensions={0} | all-to-all | bytes 32768 | tf_op jit(solution)/shard_map/all_to_all | solution.py:406
  19.2 0.5 net.1.refs_0_
  19.7 3.7 %collective-permute-start.2 = (bf16[48,512]{1,0:T(8,128)(2,1)S(1)}, bf16[48,512]{1,0:T(8,128)(2,1)S(1)}, u32[]{:S(2)}, u32[]{:S(2)}) collective-permute-start(bf16[48,512]{1,0:T(8,128)(2,1)S(1)} %net.1.refs_0_), channel_id=1, source_target_pairs={{0,6},{1,7},{2,4},{3,5},{4,2},{5,3},{6,0},{7,1},{8,14},{9,15},{10,... | collective-permute-start | bytes 147464 | tf_op jit(solution)/shard_map/ppermute | solution.py:416
  23.4 0.0 collective-permute-start.1
  23.4 1.7 %collective-permute-start.4 = (bf16[48,512]{1,0:T(8,128)(2,1)S(1)}, bf16[48,512]{1,0:T(8,128)(2,1)S(1)}, u32[]{:S(2)}, u32[]{:S(2)}) collective-permute-start(bf16[48,512]{1,0:T(8,128)(2,1)S(1)} %net.1.refs_0_), channel_id=1, source_target_pairs={{0,3},{1,2},{2,1},{3,0},{4,7},{5,6},{6,5},{7,4},{8,11},{9,10},{10,... | collective-permute-start | bytes 147464 | tf_op jit(solution)/shard_map/ppermute | solution.py:419
  25.1 0.5 collective-permute-start.3
  25.6 1.2 %collective-permute-start = (bf16[48,512]{1,0:T(8,128)(2,1)S(1)}, bf16[48,512]{1,0:T(8,128)(2,1)S(1)}, u32[]{:S(2)}, u32[]{:S(2)}) collective-permute-start(bf16[48,512]{1,0:T(8,128)(2,1)S(1)} %net.1.refs_0_), channel_id=1, source_target_pairs={{0,2},{1,3},{2,0},{3,1},{4,6},{5,7},{6,4},{7,5},{8,10},{9,11},{10,... | collective-permute-start | bytes 147464 | tf_op jit(solution)/shard_map/ppermute | solution.py:416
  26.9 0.0 collective-permute-done.2.refs_3_
  26.9 1.5 %collective-permute-start.6 = (bf16[48,512]{1,0:T(8,128)(2,1)S(1)}, bf16[48,512]{1,0:T(8,128)(2,1)S(1)}, u32[]{:S(2)}, u32[]{:S(2)}) collective-permute-start(bf16[48,512]{1,0:T(8,128)(2,1)S(1)} %collective-permute-done.2.refs_3_), channel_id=1, source_target_pairs={{0,1},{1,0},{2,3},{3,2},{4,5},{5,4},{6,7},{7,6},{8,9},{9,8},{10,11... | collective-permute-start | bytes 147464 | tf_op jit(solution)/shard_map/ppermute | solution.py:421
  28.3 0.1 collective-permute-done.1.refs_2_
  28.5 1.5 %collective-permute-start.5 = (bf16[48,512]{1,0:T(8,128)(2,1)S(1)}, bf16[48,512]{1,0:T(8,128)(2,1)S(1)}, u32[]{:S(2)}, u32[]{:S(2)}) collective-permute-start(bf16[48,512]{1,0:T(8,128)(2,1)S(1)} %collective-permute-done.1.refs_2_), channel_id=1, source_target_pairs={{0,1},{1,0},{2,3},{3,2},{4,5},{5,4},{6,7},{7,6},{8,9},{9,8},{10,11... | collective-permute-start | bytes 147464 | tf_op jit(solution)/shard_map/ppermute | solution.py:421
  29.9 0.0 collective-permute-done.4.refs_5_
  29.9 0.0 collective-permute-done.3.refs_4_
  29.9 0.0 collective-permute-done.refs_1_
  30.0 1.0 %collective-permute-done.6.refs_7_ = bf16[48,512]{1,0:T(8,128)(2,1)S(1)} collective-permute-done((bf16[48,512]{1,0:T(8,128)(2,1)S(1)}, bf16[48,512]{1,0:T(8,128)(2,1)S(1)}, u32[]{:S(2)}, u32[]{:S(2)}) %collective-permute-start.6) | collective-permute-done | bytes 49184 | tf_op jit(solution)/shard_map/ppermute | solution.py:421
  31.0 1.6 %collective-permute-done.5.refs_6_ = bf16[48,512]{1,0:T(8,128)(2,1)S(1)} collective-permute-done((bf16[48,512]{1,0:T(8,128)(2,1)S(1)}, bf16[48,512]{1,0:T(8,128)(2,1)S(1)}, u32[]{:S(2)}, u32[]{:S(2)}) %collective-permute-start.5) | collective-permute-done | bytes 49184 | tf_op jit(solution)/shard_map/ppermute | solution.py:421
  32.5 4.0 %lines.1 = (f32[2,12,4,768]{3,2,1,0:T(4,128)}, f32[8,48,512]{2,1,0:T(8,128)S(1)}, bf16[5,48,512]{2,1,0:T(8,128)(2,1)S(1)}) custom-call(s32[6,16]{1,0:T(8,128)S(1)} %get-tuple-element.11.pattern_smem, bf16[48,512]{1,0:T(8,128)(2,1)S(1)} %net.1.refs_0_, bf16[48,512]{1,0:T(8,128)(2,1)S(1)} %collective-permute-done.refs_1_, ...), custom_call_target="tpu_custom_call" | custom-call | tf_op jit(solution)/shard_map/lines/pallas_call | solution.py:331
  36.6 1.6 %collective-permute-start.12 = (bf16[48,512]{1,0:T(8,128)(2,1)S(1)}, bf16[48,512]{1,0:T(8,128)(2,1)S(1)}, u32[]{:S(2)}, u32[]{:S(2)}) collective-permute-start(bf16[48,512]{1,0:T(8,128)(2,1)S(1)} %get-tuple-element.23), channel_id=1, source_target_pairs={{0,1},{1,0},{2,3},{3,2},{4,5},{5,4},{6,7},{7,6},{8,9},{9,8},{10,11... | collective-permute-start | bytes 147464 | tf_op jit(solution)/shard_map/ppermute | solution.py:436
  38.1 0.5 collective-permute-start.10
  38.7 1.5 %collective-permute-start.7 = (bf16[48,512]{1,0:T(8,128)(2,1)S(1)}, bf16[48,512]{1,0:T(8,128)(2,1)S(1)}, u32[]{:S(2)}, u32[]{:S(2)}) collective-permute-start(bf16[48,512]{1,0:T(8,128)(2,1)S(1)} %get-tuple-element.22), channel_id=1, source_target_pairs={{0,1},{1,0},{2,3},{3,2},{4,5},{5,4},{6,7},{7,6},{8,9},{9,8},{10,11... | collective-permute-start | bytes 147464 | tf_op jit(solution)/shard_map/ppermute | solution.py:436
  40.2 0.7 %collective-permute-start.9 = (bf16[48,512]{1,0:T(8,128)(2,1)S(1)}, bf16[48,512]{1,0:T(8,128)(2,1)S(1)}, u32[]{:S(2)}, u32[]{:S(2)}) collective-permute-start(bf16[48,512]{1,0:T(8,128)(2,1)S(1)} %get-tuple-element.25), channel_id=1, source_target_pairs={{0,3},{1,2},{2,1},{3,0},{4,7},{5,6},{6,5},{7,4},{8,11},{9,10},{10,... | collective-permute-start | bytes 147464 | tf_op jit(solution)/shard_map/ppermute | solution.py:433
  40.8 1.3 %collective-permute-start.8 = (bf16[48,512]{1,0:T(8,128)(2,1)S(1)}, bf16[48,512]{1,0:T(8,128)(2,1)S(1)}, u32[]{:S(2)}, u32[]{:S(2)}) collective-permute-start(bf16[48,512]{1,0:T(8,128)(2,1)S(1)} %get-tuple-element.26), channel_id=1, source_target_pairs={{0,2},{1,3},{2,0},{3,1},{4,6},{5,7},{6,4},{7,5},{8,10},{9,11},{10,... | collective-permute-start | bytes 147464 | tf_op jit(solution)/shard_map/ppermute | solution.py:432
  42.2 0.0 collective-permute-done.12
  42.2 0.1 collective-permute-done.10
  42.3 2.8 %collective-permute-start.11 = (bf16[48,512]{1,0:T(8,128)(2,1)S(1)}, bf16[48,512]{1,0:T(8,128)(2,1)S(1)}, u32[]{:S(2)}, u32[]{:S(2)}) collective-permute-start(bf16[48,512]{1,0:T(8,128)(2,1)S(1)} %get-tuple-element.20), channel_id=1, source_target_pairs={{0,4},{1,5},{2,6},{3,7},{4,0},{5,1},{6,2},{7,3},{8,12},{9,13},{10,... | collective-permute-start | bytes 147464 | tf_op jit(solution)/shard_map/ppermute | solution.py:439
  45.1 0.2 collective-permute-start.13
  45.3 0.0 collective-permute-done.7
  45.3 0.0 collective-permute-done.9
  45.3 0.1 collective-permute-done.8
  45.4 2.4 %collective-permute-done.11 = bf16[48,512]{1,0:T(8,128)(2,1)S(1)} collective-permute-done((bf16[48,512]{1,0:T(8,128)(2,1)S(1)}, bf16[48,512]{1,0:T(8,128)(2,1)S(1)}, u32[]{:S(2)}, u32[]{:S(2)}) %collective-permute-start.11) | collective-permute-done | bytes 49184 | tf_op jit(solution)/shard_map/ppermute | solution.py:439
  47.8 3.1 %collective-permute-done.13 = bf16[48,512]{1,0:T(8,128)(2,1)S(1)} collective-permute-done((bf16[48,512]{1,0:T(8,128)(2,1)S(1)}, bf16[48,512]{1,0:T(8,128)(2,1)S(1)}, u32[]{:S(2)}, u32[]{:S(2)}) %collective-permute-start.13) | collective-permute-done | bytes 49184 | tf_op jit(solution)/shard_map/ppermute | solution.py:439
  51.0 0.1 collective-permute-start.15
  51.1 0.1 collective-permute-start.14
  51.2 4.5 %collective-permute-done.15.refs_2_ = f32[48,512]{1,0:T(8,128)S(1)} collective-permute-done((f32[48,512]{1,0:T(8,128)S(1)}, f32[48,512]{1,0:T(8,128)S(1)}, u32[]{:S(2)}, u32[]{:S(2)}) %collective-permute-start.15) | collective-permute-done | bytes 98336 | tf_op jit(solution)/shard_map/ppermute | solution.py:445
  55.7 0.0 collective-permute-start.16
  55.7 0.0 collective-permute-done.14.refs_1_
  55.7 1.3 %collective-permute-done.16.refs_3_ = f32[48,512]{1,0:T(8,128)S(1)} collective-permute-done((f32[48,512]{1,0:T(8,128)S(1)}, f32[48,512]{1,0:T(8,128)S(1)}, u32[]{:S(2)}, u32[]{:S(2)}) %collective-permute-start.16) | collective-permute-done | bytes 98336 | tf_op jit(solution)/shard_map/ppermute | solution.py:445
  57.0 0.8 %price.1 = f32[12,16,512]{2,1,0:T(8,128)} custom-call(f32[48,512]{1,0:T(8,128)S(1)} %fusion.5.refs_0_, f32[48,512]{1,0:T(8,128)S(1)} %collective-permute-done.14.refs_1_, f32[48,512]{1,0:T(8,128)S(1)} %collective-permute-done.15.refs_2_, f32[48,512]{1,0:T(8,128)S(1)} %collective-permute-done.16.refs_3_), custom_call_target="tpu_custom_call" | custom-call | tf_op jit(solution)/shard_map/price/pallas_call | solution.py:446
  (3 shorter events, 0.1 us)
Async XLA Ops:
  19.7 7.2 %collective-permute-start.2 = (bf16[48,512]{1,0:T(8,128)(2,1)S(1)}, bf16[48,512]{1,0:T(8,128)(2,1)S(1)}, u32[]{:S(2)}, u32[]{:S(2)}) collective-permute-start(bf16[48,512]{1,0:T(8,128)(2,1)S(1)} %net.1.refs_0_), channel_id=1, source_target_pairs={{0,6},{1,7},{2,4},{3,5},{4,2},{5,3},{6,0},{7,1},{8,14},{9,15},{10,... | collective-permute-start | bytes 147464 | tf_op jit(solution)/shard_map/ppermute | solution.py:416
  23.4 5.1 %collective-permute-start.1 = (bf16[48,512]{1,0:T(8,128)(2,1)S(1)}, bf16[48,512]{1,0:T(8,128)(2,1)S(1)}, u32[]{:S(2)}, u32[]{:S(2)}) collective-permute-start(bf16[48,512]{1,0:T(8,128)(2,1)S(1)} %net.1.refs_0_), channel_id=1, source_target_pairs={{0,4},{1,5},{2,6},{3,7},{4,0},{5,1},{6,2},{7,3},{8,12},{9,13},{10,... | collective-permute-start | bytes 147464 | tf_op jit(solution)/shard_map/ppermute | solution.py:416
  23.4 6.6 %collective-permute-start.4 = (bf16[48,512]{1,0:T(8,128)(2,1)S(1)}, bf16[48,512]{1,0:T(8,128)(2,1)S(1)}, u32[]{:S(2)}, u32[]{:S(2)}) collective-permute-start(bf16[48,512]{1,0:T(8,128)(2,1)S(1)} %net.1.refs_0_), channel_id=1, source_target_pairs={{0,3},{1,2},{2,1},{3,0},{4,7},{5,6},{6,5},{7,4},{8,11},{9,10},{10,... | collective-permute-start | bytes 147464 | tf_op jit(solution)/shard_map/ppermute | solution.py:419
  25.1 4.9 %collective-permute-start.3 = (bf16[48,512]{1,0:T(8,128)(2,1)S(1)}, bf16[48,512]{1,0:T(8,128)(2,1)S(1)}, u32[]{:S(2)}, u32[]{:S(2)}) collective-permute-start(bf16[48,512]{1,0:T(8,128)(2,1)S(1)} %net.1.refs_0_), channel_id=1, source_target_pairs={{0,1},{1,0},{2,3},{3,2},{4,5},{5,4},{6,7},{7,6},{8,9},{9,8},{10,11... | collective-permute-start | bytes 147464 | tf_op jit(solution)/shard_map/ppermute | solution.py:421
  25.6 4.3 %collective-permute-start = (bf16[48,512]{1,0:T(8,128)(2,1)S(1)}, bf16[48,512]{1,0:T(8,128)(2,1)S(1)}, u32[]{:S(2)}, u32[]{:S(2)}) collective-permute-start(bf16[48,512]{1,0:T(8,128)(2,1)S(1)} %net.1.refs_0_), channel_id=1, source_target_pairs={{0,2},{1,3},{2,0},{3,1},{4,6},{5,7},{6,4},{7,5},{8,10},{9,11},{10,... | collective-permute-start | bytes 147464 | tf_op jit(solution)/shard_map/ppermute | solution.py:416
  26.9 4.1 %collective-permute-start.6 = (bf16[48,512]{1,0:T(8,128)(2,1)S(1)}, bf16[48,512]{1,0:T(8,128)(2,1)S(1)}, u32[]{:S(2)}, u32[]{:S(2)}) collective-permute-start(bf16[48,512]{1,0:T(8,128)(2,1)S(1)} %collective-permute-done.2.refs_3_), channel_id=1, source_target_pairs={{0,1},{1,0},{2,3},{3,2},{4,5},{5,4},{6,7},{7,6},{8,9},{9,8},{10,11... | collective-permute-start | bytes 147464 | tf_op jit(solution)/shard_map/ppermute | solution.py:421
  28.5 4.1 %collective-permute-start.5 = (bf16[48,512]{1,0:T(8,128)(2,1)S(1)}, bf16[48,512]{1,0:T(8,128)(2,1)S(1)}, u32[]{:S(2)}, u32[]{:S(2)}) collective-permute-start(bf16[48,512]{1,0:T(8,128)(2,1)S(1)} %collective-permute-done.1.refs_2_), channel_id=1, source_target_pairs={{0,1},{1,0},{2,3},{3,2},{4,5},{5,4},{6,7},{7,6},{8,9},{9,8},{10,11... | collective-permute-start | bytes 147464 | tf_op jit(solution)/shard_map/ppermute | solution.py:421
  36.6 5.6 %collective-permute-start.12 = (bf16[48,512]{1,0:T(8,128)(2,1)S(1)}, bf16[48,512]{1,0:T(8,128)(2,1)S(1)}, u32[]{:S(2)}, u32[]{:S(2)}) collective-permute-start(bf16[48,512]{1,0:T(8,128)(2,1)S(1)} %get-tuple-element.23), channel_id=1, source_target_pairs={{0,1},{1,0},{2,3},{3,2},{4,5},{5,4},{6,7},{7,6},{8,9},{9,8},{10,11... | collective-permute-start | bytes 147464 | tf_op jit(solution)/shard_map/ppermute | solution.py:436
  38.1 4.1 %collective-permute-start.10 = (bf16[48,512]{1,0:T(8,128)(2,1)S(1)}, bf16[48,512]{1,0:T(8,128)(2,1)S(1)}, u32[]{:S(2)}, u32[]{:S(2)}) collective-permute-start(bf16[48,512]{1,0:T(8,128)(2,1)S(1)} %get-tuple-element.24), channel_id=1, source_target_pairs={{0,1},{1,0},{2,3},{3,2},{4,5},{5,4},{6,7},{7,6},{8,9},{9,8},{10,11... | collective-permute-start | bytes 147464 | tf_op jit(solution)/shard_map/ppermute | solution.py:436
  38.7 6.6 %collective-permute-start.7 = (bf16[48,512]{1,0:T(8,128)(2,1)S(1)}, bf16[48,512]{1,0:T(8,128)(2,1)S(1)}, u32[]{:S(2)}, u32[]{:S(2)}) collective-permute-start(bf16[48,512]{1,0:T(8,128)(2,1)S(1)} %get-tuple-element.22), channel_id=1, source_target_pairs={{0,1},{1,0},{2,3},{3,2},{4,5},{5,4},{6,7},{7,6},{8,9},{9,8},{10,11... | collective-permute-start | bytes 147464 | tf_op jit(solution)/shard_map/ppermute | solution.py:436
  40.2 5.2 %collective-permute-start.9 = (bf16[48,512]{1,0:T(8,128)(2,1)S(1)}, bf16[48,512]{1,0:T(8,128)(2,1)S(1)}, u32[]{:S(2)}, u32[]{:S(2)}) collective-permute-start(bf16[48,512]{1,0:T(8,128)(2,1)S(1)} %get-tuple-element.25), channel_id=1, source_target_pairs={{0,3},{1,2},{2,1},{3,0},{4,7},{5,6},{6,5},{7,4},{8,11},{9,10},{10,... | collective-permute-start | bytes 147464 | tf_op jit(solution)/shard_map/ppermute | solution.py:433
  40.8 4.6 %collective-permute-start.8 = (bf16[48,512]{1,0:T(8,128)(2,1)S(1)}, bf16[48,512]{1,0:T(8,128)(2,1)S(1)}, u32[]{:S(2)}, u32[]{:S(2)}) collective-permute-start(bf16[48,512]{1,0:T(8,128)(2,1)S(1)} %get-tuple-element.26), channel_id=1, source_target_pairs={{0,2},{1,3},{2,0},{3,1},{4,6},{5,7},{6,4},{7,5},{8,10},{9,11},{10,... | collective-permute-start | bytes 147464 | tf_op jit(solution)/shard_map/ppermute | solution.py:432
  42.3 5.6 %collective-permute-start.11 = (bf16[48,512]{1,0:T(8,128)(2,1)S(1)}, bf16[48,512]{1,0:T(8,128)(2,1)S(1)}, u32[]{:S(2)}, u32[]{:S(2)}) collective-permute-start(bf16[48,512]{1,0:T(8,128)(2,1)S(1)} %get-tuple-element.20), channel_id=1, source_target_pairs={{0,4},{1,5},{2,6},{3,7},{4,0},{5,1},{6,2},{7,3},{8,12},{9,13},{10,... | collective-permute-start | bytes 147464 | tf_op jit(solution)/shard_map/ppermute | solution.py:439
  45.1 5.9 %collective-permute-start.13 = (bf16[48,512]{1,0:T(8,128)(2,1)S(1)}, bf16[48,512]{1,0:T(8,128)(2,1)S(1)}, u32[]{:S(2)}, u32[]{:S(2)}) collective-permute-start(bf16[48,512]{1,0:T(8,128)(2,1)S(1)} %get-tuple-element.21), channel_id=1, source_target_pairs={{0,6},{1,7},{2,4},{3,5},{4,2},{5,3},{6,0},{7,1},{8,14},{9,15},{10,... | collective-permute-start | bytes 147464 | tf_op jit(solution)/shard_map/ppermute | solution.py:439
  51.0 4.7 %collective-permute-start.15 = (f32[48,512]{1,0:T(8,128)S(1)}, f32[48,512]{1,0:T(8,128)S(1)}, u32[]{:S(2)}, u32[]{:S(2)}) collective-permute-start(f32[48,512]{1,0:T(8,128)S(1)} %fusion.5.refs_0_), channel_id=1, source_target_pairs={{0,16},{8,24},{16,0},{24,8},{1,17},{9,25},{17,1},{25,9},{2,18},{10... | collective-permute-start | bytes 294920 | tf_op jit(solution)/shard_map/ppermute | solution.py:445
  51.1 4.6 %collective-permute-start.14 = (f32[48,512]{1,0:T(8,128)S(1)}, f32[48,512]{1,0:T(8,128)S(1)}, u32[]{:S(2)}, u32[]{:S(2)}) collective-permute-start(f32[48,512]{1,0:T(8,128)S(1)} %fusion.5.refs_0_), channel_id=1, source_target_pairs={{0,8},{8,0},{16,24},{24,16},{1,9},{9,1},{17,25},{25,17},{2,10},{10... | collective-permute-start | bytes 294920 | tf_op jit(solution)/shard_map/ppermute | solution.py:445
  55.7 1.3 %collective-permute-start.16 = (f32[48,512]{1,0:T(8,128)S(1)}, f32[48,512]{1,0:T(8,128)S(1)}, u32[]{:S(2)}, u32[]{:S(2)}) collective-permute-start(f32[48,512]{1,0:T(8,128)S(1)} %collective-permute-done.15.refs_2_), channel_id=1, source_target_pairs={{0,8},{8,0},{16,24},{24,16},{1,9},{9,1},{17,25},{25,17},{2,10},{10... | collective-permute-start | bytes 294920 | tf_op jit(solution)/shard_map/ppermute | solution.py:445

commit v8 on v7

--- a/solution.py
+++ b/solution.py
@@ -160,13 +160,14 @@
                     mean = jnp.sum(marked, axis=-1, keepdims=True) / total
                     here = lane == (at % per_row) * gens + slot
                     outs[at // per_row] = jnp.where(here, mean, outs[at // per_row])
+    me = lax.axis_index("gen")
     for slot in range(gens):
         here = lane == (hours % per_row) * gens + slot
         bus = jnp.sum(jnp.where(lane == slot, bus_row, 0)).astype(jnp.float32)
         outs[-1] = jnp.where(here, bus, outs[-1])
     for part in range(parts):
         for row, block in enumerate(outs):
-            out_ref[part, row] = block[part * scn_dev : (part + 1) * scn_dev, :]
+            out_ref[lax.bitwise_xor(me, part), row] = block[part * scn_dev : (part + 1) * scn_dev, :]
     for copy in copies[6:]:
         copy.wait()
 
@@ -211,8 +212,9 @@
     )
 
 
-def net_kernel(plan_ref, demand_ref, net_ref, *, gens):
-    parts, rows, scn_dev, _ = plan_ref.shape
+def net_kernel(*refs, gens):
+    plan_refs, (demand_ref, net_ref) = refs[:-2], refs[-2:]
+    rows, scn_dev = plan_refs[0].shape[1:3]
     hours, _, bus_dev = demand_ref.shape
     per_row = LANES // gens
     lane = lax.broadcasted_iota(jnp.int32, (1, LANES), 1)
@@ -223,8 +225,8 @@
         return (lane >= start) & (lane < start + gens)
 
     left, places = [], []
-    for part in range(parts):
-        values = [plan_ref[part, row] for row in range(rows)]
+    for plan_ref in plan_refs:
+        values = [plan_ref[0, row] for row in range(rows)]
         left.append(
             jnp.concatenate(
                 [jnp.where(of_hour(hour), values[hour // per_row], 0.0) for hour in range(hours)], axis=0
@@ -403,15 +405,18 @@
         state_counts, gen_bus, transitions, state_level, state_cost, bus_price, ahead, parts
     )
     bus_demand, ptdf_blocks, multipliers, line_limits, ptdf_pattern = ahead
-    received = lax.all_to_all(plan, "gen", split_axis=0, concat_axis=0, tiled=True)
+    received = [plan, lax.ppermute(plan[1:2], "gen", trade(parts, 1))]
+    for step in range(2, parts, 2):
+        both = lax.ppermute(plan[step : step + 2], "gen", trade(parts, step))
+        received += [both, lax.ppermute(both[1:], "gen", trade(parts, 1))]
     net = pl.pallas_call(
         functools.partial(net_kernel, gens=gens),
         out_shape=jax.ShapeDtypeStruct((row_total, bus_dev), jnp.bfloat16),
-        in_specs=[vmem, vmem],
+        in_specs=[vmem] * (len(received) + 1),
         out_specs=vmem,
         compiler_params=roomy,
         name="net",
-    )(received, bus_demand)
+    )(*received, bus_demand)
 
     far = [lax.ppermute(net, "bus", trade(ring, 2 * step)) for step in range(1, half)]
     handed = [net] + far

time: 58.1 us -> 56.5 us (0.972)
  blocking collectives: 7.9 us -> 0 us
  starting transfers between devices: 18.9 us -> 23.4 us
  waiting for transfers between devices: 14.3 us -> 16.1 us
    all_to_all x1 -> x0, blocking collectives: 7.9 us -> none  [shards(): lax.all_to_all(plan, 'gen', split_axis=0, concat_axis=0, tiled=True)]
    ppermute x0 -> x3, starting transfers between devices: none -> 3.04 us  [the longest x1 3.03 us: shards(): both = lax.ppermute(plan[step:step + 2], 'gen', trade(parts, step))]
    ppermute x0 -> x3, waiting for transfers between devices: none -> 2.79 us  [the longest x1 1.63 us: shards(): both = lax.ppermute(plan[step:step + 2], 'gen', trade(parts, step))]
    ppermute x3, starting transfers between devices: 0.14 us -> 1.59 us  [shards(): shares.append(lax.ppermute(moved, 'gen', trade(parts, by)))]
    ppermute x3, waiting for transfers between devices: 5.82 us -> 4.39 us  [shards(): shares.append(lax.ppermute(moved, 'gen', trade(parts, by)))]
    ppermute x3, starting transfers between devices: 4.92 us -> 5.55 us  [shards(): lax.ppermute(net, 'bus', trade(ring, 2 * step))]
  transfers between devices with their start and end apart: 17 -> 20, of which waited for: 9 -> 11; matrix products, arithmetic and copies ran while one was open for 0% -> 0% of each run, Pallas kernels for 0% -> 0%
where the time goes in v8:
time: 56.5 us; the launch traced here: 56.3 us
  starting transfers between devices  23.4 us (41%)
  waiting for transfers between devices  16.1 us (28%)
  Pallas kernels  16 us (28%)
  between operations  0.71 us (1%)
    pallas_call x1, Pallas kernels, run_plan(): pl.pallas_call(functools.partial(plan_kernel, gens=gens, parts=parts), ou...  10.6 us
    ppermute x2, waiting for transfers between devices, shards(): shares = [lax.ppermute(share, 'bus', trade(ring, 2 * step))]  5.58 us
    ppermute x3, starting transfers between devices, shards(): lax.ppermute(net, 'bus', trade(ring, 2 * step))  5.55 us
    ppermute x3, waiting for transfers between devices, shards(): shares.append(lax.ppermute(moved, 'gen', trade(parts, by)))  4.39 us
    pallas_call x1, Pallas kernels, run_lines(): pl.pallas_call(functools.partial(line_kernel, half=half), out_shape=(jax....  4.01 us
    ppermute x3, starting transfers between devices, shards(): shares = [lax.ppermute(far_part[step], 'bus', trade(ring, 1))]  3.58 us
    ppermute x3, starting transfers between devices, shards(): lax.ppermute(handed[step], 'bus', trade(ring, 1))  3.37 us
    ppermute x1, starting transfers between devices, shards(): both = lax.ppermute(plan[step:step + 2], 'gen', trade(parts, step))  3.03 us
  transfers between devices with their start and end apart: 20, of which 11 were waited for; matrix products, arithmetic and copies ran while one was open for 0% of the time, Pallas kernels for 0%

profile of v8, /device:TPU:0, one launch (start us, length us, event | category | flops | bytes accessed | tf_op | source)
XLA Modules:
  0.0 56.3 jit_solution(11449910766023804689)
XLA Ops:
  0.6 10.6 %plan.1 = (f32[4,2,4,128]{3,2,1,0:T(4,128)S(1)}, f32[12,4,512]{2,1,0:T(4,128)S(1)}, bf16[6,16,128,128]{3,2,1,0:T(8,128)(2,1)S(1)}, f32[2,12,4,768]{3,2,1,0:T(4,1...) custom-call(s32[16]{0:T(128)} %refs_0_.1, s32[16]{0:T(128)} %refs_1_.1, s32[3,16,512]{2,1,0:T(8,128)} %bitcast.38, ...), custom_call_target="tpu_custom_call" | custom-call | tf_op jit(solution)/shard_map/plan/pallas_call | solution.py:182
  11.3 3.0 %collective-permute-start.1 = (f32[2,2,4,128]{3,2,1,0:T(4,128)S(1)}, f32[2,2,4,128]{3,2,1,0:T(4,128)S(1)}, u32[]{:S(2)}, u32[]{:S(2)}) collective-permute-start(f32[2,2,4,128]{3,2,1,0:T(4,128)S(1)} %slice.34), channel_id=1, source_target_pairs={{0,16},{8,24},{16,0},{24,8},{1,17},{9,25},{17,1},{25,9},{2,18},{10... | collective-permute-start | bytes 24584 | tf_op jit(solution)/shard_map/ppermute | solution.py:410
  14.3 0.0 collective-permute-start
  14.3 1.6 %collective-permute-done.1.refs_2_ = f32[2,2,4,128]{3,2,1,0:T(4,128)S(1)} collective-permute-done((f32[2,2,4,128]{3,2,1,0:T(4,128)S(1)}, f32[2,2,4,128]{3,2,1,0:T(4,128)S(1)}, u32[]{:S(2)}, u32[]{:S(2)}) %collective-permute-start.1) | collective-permute-done | bytes 8224 | tf_op jit(solution)/shard_map/ppermute | solution.py:410
  15.9 0.0 collective-permute-start.2
  15.9 0.0 collective-permute-done.refs_1_
  16.0 1.2 %collective-permute-done.2.refs_3_ = f32[1,2,4,128]{3,2,1,0:T(4,128)S(1)} collective-permute-done((f32[1,2,4,128]{3,2,1,0:T(4,128)S(1)}, f32[1,2,4,128]{3,2,1,0:T(4,128)S(1)}, u32[]{:S(2)}, u32[]{:S(2)}) %collective-permute-start.2) | collective-permute-done | bytes 4128 | tf_op jit(solution)/shard_map/ppermute | solution.py:411
  17.1 0.5 net.1.refs_0_
  17.7 4.2 %collective-permute-start.5 = (bf16[48,512]{1,0:T(8,128)(2,1)S(1)}, bf16[48,512]{1,0:T(8,128)(2,1)S(1)}, u32[]{:S(2)}, u32[]{:S(2)}) collective-permute-start(bf16[48,512]{1,0:T(8,128)(2,1)S(1)} %net.1.refs_0_), channel_id=1, source_target_pairs={{0,6},{1,7},{2,4},{3,5},{4,2},{5,3},{6,0},{7,1},{8,14},{9,15},{10,... | collective-permute-start | bytes 147464 | tf_op jit(solution)/shard_map/ppermute | solution.py:421
  21.8 0.0 collective-permute-start.4
  21.8 1.7 %collective-permute-start.7 = (bf16[48,512]{1,0:T(8,128)(2,1)S(1)}, bf16[48,512]{1,0:T(8,128)(2,1)S(1)}, u32[]{:S(2)}, u32[]{:S(2)}) collective-permute-start(bf16[48,512]{1,0:T(8,128)(2,1)S(1)} %net.1.refs_0_), channel_id=1, source_target_pairs={{0,3},{1,2},{2,1},{3,0},{4,7},{5,6},{6,5},{7,4},{8,11},{9,10},{10,... | collective-permute-start | bytes 147464 | tf_op jit(solution)/shard_map/ppermute | solution.py:424
  23.5 0.4 collective-permute-start.6
  23.9 1.4 %collective-permute-start.3 = (bf16[48,512]{1,0:T(8,128)(2,1)S(1)}, bf16[48,512]{1,0:T(8,128)(2,1)S(1)}, u32[]{:S(2)}, u32[]{:S(2)}) collective-permute-start(bf16[48,512]{1,0:T(8,128)(2,1)S(1)} %net.1.refs_0_), channel_id=1, source_target_pairs={{0,2},{1,3},{2,0},{3,1},{4,6},{5,7},{6,4},{7,5},{8,10},{9,11},{10,... | collective-permute-start | bytes 147464 | tf_op jit(solution)/shard_map/ppermute | solution.py:421
  25.3 0.0 collective-permute-done.5.refs_3_
  25.3 1.5 %collective-permute-start.9 = (bf16[48,512]{1,0:T(8,128)(2,1)S(1)}, bf16[48,512]{1,0:T(8,128)(2,1)S(1)}, u32[]{:S(2)}, u32[]{:S(2)}) collective-permute-start(bf16[48,512]{1,0:T(8,128)(2,1)S(1)} %collective-permute-done.5.refs_3_), channel_id=1, source_target_pairs={{0,1},{1,0},{2,3},{3,2},{4,5},{5,4},{6,7},{7,6},{8,9},{9,8},{10,11... | collective-permute-start | bytes 147464 | tf_op jit(solution)/shard_map/ppermute | solution.py:426
  26.8 0.1 collective-permute-done.4.refs_2_
  26.9 1.5 %collective-permute-start.8 = (bf16[48,512]{1,0:T(8,128)(2,1)S(1)}, bf16[48,512]{1,0:T(8,128)(2,1)S(1)}, u32[]{:S(2)}, u32[]{:S(2)}) collective-permute-start(bf16[48,512]{1,0:T(8,128)(2,1)S(1)} %collective-permute-done.4.refs_2_), channel_id=1, source_target_pairs={{0,1},{1,0},{2,3},{3,2},{4,5},{5,4},{6,7},{7,6},{8,9},{9,8},{10,11... | collective-permute-start | bytes 147464 | tf_op jit(solution)/shard_map/ppermute | solution.py:426
  28.4 0.0 collective-permute-done.7.refs_5_
  28.4 0.0 collective-permute-done.6.refs_4_
  28.4 0.0 collective-permute-done.3.refs_1_
  28.4 1.4 %collective-permute-done.9.refs_7_ = bf16[48,512]{1,0:T(8,128)(2,1)S(1)} collective-permute-done((bf16[48,512]{1,0:T(8,128)(2,1)S(1)}, bf16[48,512]{1,0:T(8,128)(2,1)S(1)}, u32[]{:S(2)}, u32[]{:S(2)}) %collective-permute-start.9) | collective-permute-done | bytes 49184 | tf_op jit(solution)/shard_map/ppermute | solution.py:426
  29.8 1.1 %collective-permute-done.8.refs_6_ = bf16[48,512]{1,0:T(8,128)(2,1)S(1)} collective-permute-done((bf16[48,512]{1,0:T(8,128)(2,1)S(1)}, bf16[48,512]{1,0:T(8,128)(2,1)S(1)}, u32[]{:S(2)}, u32[]{:S(2)}) %collective-permute-start.8) | collective-permute-done | bytes 49184 | tf_op jit(solution)/shard_map/ppermute | solution.py:426
  31.0 4.0 %lines.1 = (f32[2,12,4,768]{3,2,1,0:T(4,128)}, f32[8,48,512]{2,1,0:T(8,128)S(1)}, bf16[5,48,512]{2,1,0:T(8,128)(2,1)S(1)}) custom-call(s32[6,16]{1,0:T(8,128)S(1)} %get-tuple-element.11.pattern_smem, bf16[48,512]{1,0:T(8,128)(2,1)S(1)} %net.1.refs_0_, bf16[48,512]{1,0:T(8,128)(2,1)S(1)} %collective-permute-done.3.refs_1_, ...), custom_call_target="tpu_custom_call" | custom-call | tf_op jit(solution)/shard_map/lines/pallas_call | solution.py:333
  35.0 1.6 %collective-permute-start.15 = (bf16[48,512]{1,0:T(8,128)(2,1)S(1)}, bf16[48,512]{1,0:T(8,128)(2,1)S(1)}, u32[]{:S(2)}, u32[]{:S(2)}) collective-permute-start(bf16[48,512]{1,0:T(8,128)(2,1)S(1)} %get-tuple-element.23), channel_id=1, source_target_pairs={{0,1},{1,0},{2,3},{3,2},{4,5},{5,4},{6,7},{7,6},{8,9},{9,8},{10,11... | collective-permute-start | bytes 147464 | tf_op jit(solution)/shard_map/ppermute | solution.py:441
  36.6 0.5 collective-permute-start.13
  37.1 1.5 %collective-permute-start.10 = (bf16[48,512]{1,0:T(8,128)(2,1)S(1)}, bf16[48,512]{1,0:T(8,128)(2,1)S(1)}, u32[]{:S(2)}, u32[]{:S(2)}) collective-permute-start(bf16[48,512]{1,0:T(8,128)(2,1)S(1)} %get-tuple-element.22), channel_id=1, source_target_pairs={{0,1},{1,0},{2,3},{3,2},{4,5},{5,4},{6,7},{7,6},{8,9},{9,8},{10,11... | collective-permute-start | bytes 147464 | tf_op jit(solution)/shard_map/ppermute | solution.py:441
  38.6 0.7 %collective-permute-start.12 = (bf16[48,512]{1,0:T(8,128)(2,1)S(1)}, bf16[48,512]{1,0:T(8,128)(2,1)S(1)}, u32[]{:S(2)}, u32[]{:S(2)}) collective-permute-start(bf16[48,512]{1,0:T(8,128)(2,1)S(1)} %get-tuple-element.25), channel_id=1, source_target_pairs={{0,3},{1,2},{2,1},{3,0},{4,7},{5,6},{6,5},{7,4},{8,11},{9,10},{10,... | collective-permute-start | bytes 147464 | tf_op jit(solution)/shard_map/ppermute | solution.py:438
  39.3 1.3 %collective-permute-start.11 = (bf16[48,512]{1,0:T(8,128)(2,1)S(1)}, bf16[48,512]{1,0:T(8,128)(2,1)S(1)}, u32[]{:S(2)}, u32[]{:S(2)}) collective-permute-start(bf16[48,512]{1,0:T(8,128)(2,1)S(1)} %get-tuple-element.26), channel_id=1, source_target_pairs={{0,2},{1,3},{2,0},{3,1},{4,6},{5,7},{6,4},{7,5},{8,10},{9,11},{10,... | collective-permute-start | bytes 147464 | tf_op jit(solution)/shard_map/ppermute | solution.py:437
  40.6 0.0 collective-permute-done.15
  40.6 0.5 collective-permute-done.13
  41.2 2.4 %collective-permute-start.14 = (bf16[48,512]{1,0:T(8,128)(2,1)S(1)}, bf16[48,512]{1,0:T(8,128)(2,1)S(1)}, u32[]{:S(2)}, u32[]{:S(2)}) collective-permute-start(bf16[48,512]{1,0:T(8,128)(2,1)S(1)} %get-tuple-element.20), channel_id=1, source_target_pairs={{0,4},{1,5},{2,6},{3,7},{4,0},{5,1},{6,2},{7,3},{8,12},{9,13},{10,... | collective-permute-start | bytes 147464 | tf_op jit(solution)/shard_map/ppermute | solution.py:444
  43.6 0.2 collective-permute-start.16
  43.8 0.0 collective-permute-done.10
  43.8 0.1 collective-permute-done.12
  43.9 0.0 collective-permute-done.11
  43.9 2.7 %collective-permute-done.14 = bf16[48,512]{1,0:T(8,128)(2,1)S(1)} collective-permute-done((bf16[48,512]{1,0:T(8,128)(2,1)S(1)}, bf16[48,512]{1,0:T(8,128)(2,1)S(1)}, u32[]{:S(2)}, u32[]{:S(2)}) %collective-permute-start.14) | collective-permute-done | bytes 49184 | tf_op jit(solution)/shard_map/ppermute | solution.py:444
  46.5 2.9 %collective-permute-done.16 = bf16[48,512]{1,0:T(8,128)(2,1)S(1)} collective-permute-done((bf16[48,512]{1,0:T(8,128)(2,1)S(1)}, bf16[48,512]{1,0:T(8,128)(2,1)S(1)}, u32[]{:S(2)}, u32[]{:S(2)}) %collective-permute-start.16) | collective-permute-done | bytes 49184 | tf_op jit(solution)/shard_map/ppermute | solution.py:444
  49.5 1.6 %collective-permute-start.18 = (f32[48,512]{1,0:T(8,128)S(1)}, f32[48,512]{1,0:T(8,128)S(1)}, u32[]{:S(2)}, u32[]{:S(2)}) collective-permute-start(f32[48,512]{1,0:T(8,128)S(1)} %fusion.5.refs_0_), channel_id=1, source_target_pairs={{0,16},{8,24},{16,0},{24,8},{1,17},{9,25},{17,1},{25,9},{2,18},{10... | collective-permute-start | bytes 294920 | tf_op jit(solution)/shard_map/ppermute | solution.py:450
  51.1 0.0 collective-permute-start.17
  51.1 3.1 %collective-permute-done.18.refs_2_ = f32[48,512]{1,0:T(8,128)S(1)} collective-permute-done((f32[48,512]{1,0:T(8,128)S(1)}, f32[48,512]{1,0:T(8,128)S(1)}, u32[]{:S(2)}, u32[]{:S(2)}) %collective-permute-start.18) | collective-permute-done | bytes 98336 | tf_op jit(solution)/shard_map/ppermute | solution.py:450
  54.2 0.0 collective-permute-start.19
  54.2 0.0 collective-permute-done.17.refs_1_
  54.2 1.3 %collective-permute-done.19.refs_3_ = f32[48,512]{1,0:T(8,128)S(1)} collective-permute-done((f32[48,512]{1,0:T(8,128)S(1)}, f32[48,512]{1,0:T(8,128)S(1)}, u32[]{:S(2)}, u32[]{:S(2)}) %collective-permute-start.19) | collective-permute-done | bytes 98336 | tf_op jit(solution)/shard_map/ppermute | solution.py:450
  55.5 0.8 %price.1 = f32[12,16,512]{2,1,0:T(8,128)} custom-call(f32[48,512]{1,0:T(8,128)S(1)} %fusion.5.refs_0_, f32[48,512]{1,0:T(8,128)S(1)} %collective-permute-done.17.refs_1_, f32[48,512]{1,0:T(8,128)S(1)} %collective-permute-done.18.refs_2_, f32[48,512]{1,0:T(8,128)S(1)} %collective-permute-done.19.refs_3_), custom_call_target="tpu_custom_call" | custom-call | tf_op jit(solution)/shard_map/price/pallas_call | solution.py:451
  (6 shorter events, 0.1 us)
Async XLA Ops:
  11.3 4.7 %collective-permute-start.1 = (f32[2,2,4,128]{3,2,1,0:T(4,128)S(1)}, f32[2,2,4,128]{3,2,1,0:T(4,128)S(1)}, u32[]{:S(2)}, u32[]{:S(2)}) collective-permute-start(f32[2,2,4,128]{3,2,1,0:T(4,128)S(1)} %slice.34), channel_id=1, source_target_pairs={{0,16},{8,24},{16,0},{24,8},{1,17},{9,25},{17,1},{25,9},{2,18},{10... | collective-permute-start | bytes 24584 | tf_op jit(solution)/shard_map/ppermute | solution.py:410
  14.3 1.6 %collective-permute-start = (f32[1,2,4,128]{3,2,1,0:T(4,128)S(1)}, f32[1,2,4,128]{3,2,1,0:T(4,128)S(1)}, u32[]{:S(2)}, u32[]{:S(2)}) collective-permute-start(f32[1,2,4,128]{3,2,1,0:T(4,128)S(1)} %slice.33), channel_id=1, source_target_pairs={{0,8},{8,0},{16,24},{24,16},{1,9},{9,1},{17,25},{25,17},{2,10},{10... | collective-permute-start | bytes 12296 | tf_op jit(solution)/shard_map/ppermute | solution.py:408
  15.9 1.2 %collective-permute-start.2 = (f32[1,2,4,128]{3,2,1,0:T(4,128)S(1)}, f32[1,2,4,128]{3,2,1,0:T(4,128)S(1)}, u32[]{:S(2)}, u32[]{:S(2)}) collective-permute-start(f32[1,2,4,128]{3,2,1,0:T(4,128)S(1)} %slice.44), channel_id=1, source_target_pairs={{0,8},{8,0},{16,24},{24,16},{1,9},{9,1},{17,25},{25,17},{2,10},{10... | collective-permute-start | bytes 12296 | tf_op jit(solution)/shard_map/ppermute | solution.py:411
  17.7 7.7 %collective-permute-start.5 = (bf16[48,512]{1,0:T(8,128)(2,1)S(1)}, bf16[48,512]{1,0:T(8,128)(2,1)S(1)}, u32[]{:S(2)}, u32[]{:S(2)}) collective-permute-start(bf16[48,512]{1,0:T(8,128)(2,1)S(1)} %net.1.refs_0_), channel_id=1, source_target_pairs={{0,6},{1,7},{2,4},{3,5},{4,2},{5,3},{6,0},{7,1},{8,14},{9,15},{10,... | collective-permute-start | bytes 147464 | tf_op jit(solution)/shard_map/ppermute | solution.py:421
  21.8 5.1 %collective-permute-start.4 = (bf16[48,512]{1,0:T(8,128)(2,1)S(1)}, bf16[48,512]{1,0:T(8,128)(2,1)S(1)}, u32[]{:S(2)}, u32[]{:S(2)}) collective-permute-start(bf16[48,512]{1,0:T(8,128)(2,1)S(1)} %net.1.refs_0_), channel_id=1, source_target_pairs={{0,4},{1,5},{2,6},{3,7},{4,0},{5,1},{6,2},{7,3},{8,12},{9,13},{10,... | collective-permute-start | bytes 147464 | tf_op jit(solution)/shard_map/ppermute | solution.py:421
  21.8 6.5 %collective-permute-start.7 = (bf16[48,512]{1,0:T(8,128)(2,1)S(1)}, bf16[48,512]{1,0:T(8,128)(2,1)S(1)}, u32[]{:S(2)}, u32[]{:S(2)}) collective-permute-start(bf16[48,512]{1,0:T(8,128)(2,1)S(1)} %net.1.refs_0_), channel_id=1, source_target_pairs={{0,3},{1,2},{2,1},{3,0},{4,7},{5,6},{6,5},{7,4},{8,11},{9,10},{10,... | collective-permute-start | bytes 147464 | tf_op jit(solution)/shard_map/ppermute | solution.py:424
  23.5 4.8 %collective-permute-start.6 = (bf16[48,512]{1,0:T(8,128)(2,1)S(1)}, bf16[48,512]{1,0:T(8,128)(2,1)S(1)}, u32[]{:S(2)}, u32[]{:S(2)}) collective-permute-start(bf16[48,512]{1,0:T(8,128)(2,1)S(1)} %net.1.refs_0_), channel_id=1, source_target_pairs={{0,1},{1,0},{2,3},{3,2},{4,5},{5,4},{6,7},{7,6},{8,9},{9,8},{10,11... | collective-permute-start | bytes 147464 | tf_op jit(solution)/shard_map/ppermute | solution.py:426
  23.9 4.5 %collective-permute-start.3 = (bf16[48,512]{1,0:T(8,128)(2,1)S(1)}, bf16[48,512]{1,0:T(8,128)(2,1)S(1)}, u32[]{:S(2)}, u32[]{:S(2)}) collective-permute-start(bf16[48,512]{1,0:T(8,128)(2,1)S(1)} %net.1.refs_0_), channel_id=1, source_target_pairs={{0,2},{1,3},{2,0},{3,1},{4,6},{5,7},{6,4},{7,5},{8,10},{9,11},{10,... | collective-permute-start | bytes 147464 | tf_op jit(solution)/shard_map/ppermute | solution.py:421
  25.3 4.5 %collective-permute-start.9 = (bf16[48,512]{1,0:T(8,128)(2,1)S(1)}, bf16[48,512]{1,0:T(8,128)(2,1)S(1)}, u32[]{:S(2)}, u32[]{:S(2)}) collective-permute-start(bf16[48,512]{1,0:T(8,128)(2,1)S(1)} %collective-permute-done.5.refs_3_), channel_id=1, source_target_pairs={{0,1},{1,0},{2,3},{3,2},{4,5},{5,4},{6,7},{7,6},{8,9},{9,8},{10,11... | collective-permute-start | bytes 147464 | tf_op jit(solution)/shard_map/ppermute | solution.py:426
  26.9 4.1 %collective-permute-start.8 = (bf16[48,512]{1,0:T(8,128)(2,1)S(1)}, bf16[48,512]{1,0:T(8,128)(2,1)S(1)}, u32[]{:S(2)}, u32[]{:S(2)}) collective-permute-start(bf16[48,512]{1,0:T(8,128)(2,1)S(1)} %collective-permute-done.4.refs_2_), channel_id=1, source_target_pairs={{0,1},{1,0},{2,3},{3,2},{4,5},{5,4},{6,7},{7,6},{8,9},{9,8},{10,11... | collective-permute-start | bytes 147464 | tf_op jit(solution)/shard_map/ppermute | solution.py:426
  35.0 5.6 %collective-permute-start.15 = (bf16[48,512]{1,0:T(8,128)(2,1)S(1)}, bf16[48,512]{1,0:T(8,128)(2,1)S(1)}, u32[]{:S(2)}, u32[]{:S(2)}) collective-permute-start(bf16[48,512]{1,0:T(8,128)(2,1)S(1)} %get-tuple-element.23), channel_id=1, source_target_pairs={{0,1},{1,0},{2,3},{3,2},{4,5},{5,4},{6,7},{7,6},{8,9},{9,8},{10,11... | collective-permute-start | bytes 147464 | tf_op jit(solution)/shard_map/ppermute | solution.py:441
  36.6 4.6 %collective-permute-start.13 = (bf16[48,512]{1,0:T(8,128)(2,1)S(1)}, bf16[48,512]{1,0:T(8,128)(2,1)S(1)}, u32[]{:S(2)}, u32[]{:S(2)}) collective-permute-start(bf16[48,512]{1,0:T(8,128)(2,1)S(1)} %get-tuple-element.24), channel_id=1, source_target_pairs={{0,1},{1,0},{2,3},{3,2},{4,5},{5,4},{6,7},{7,6},{8,9},{9,8},{10,11... | collective-permute-start | bytes 147464 | tf_op jit(solution)/shard_map/ppermute | solution.py:441
  37.1 6.7 %collective-permute-start.10 = (bf16[48,512]{1,0:T(8,128)(2,1)S(1)}, bf16[48,512]{1,0:T(8,128)(2,1)S(1)}, u32[]{:S(2)}, u32[]{:S(2)}) collective-permute-start(bf16[48,512]{1,0:T(8,128)(2,1)S(1)} %get-tuple-element.22), channel_id=1, source_target_pairs={{0,1},{1,0},{2,3},{3,2},{4,5},{5,4},{6,7},{7,6},{8,9},{9,8},{10,11... | collective-permute-start | bytes 147464 | tf_op jit(solution)/shard_map/ppermute | solution.py:441
  38.6 5.3 %collective-permute-start.12 = (bf16[48,512]{1,0:T(8,128)(2,1)S(1)}, bf16[48,512]{1,0:T(8,128)(2,1)S(1)}, u32[]{:S(2)}, u32[]{:S(2)}) collective-permute-start(bf16[48,512]{1,0:T(8,128)(2,1)S(1)} %get-tuple-element.25), channel_id=1, source_target_pairs={{0,3},{1,2},{2,1},{3,0},{4,7},{5,6},{6,5},{7,4},{8,11},{9,10},{10,... | collective-permute-start | bytes 147464 | tf_op jit(solution)/shard_map/ppermute | solution.py:438
  39.3 4.6 %collective-permute-start.11 = (bf16[48,512]{1,0:T(8,128)(2,1)S(1)}, bf16[48,512]{1,0:T(8,128)(2,1)S(1)}, u32[]{:S(2)}, u32[]{:S(2)}) collective-permute-start(bf16[48,512]{1,0:T(8,128)(2,1)S(1)} %get-tuple-element.26), channel_id=1, source_target_pairs={{0,2},{1,3},{2,0},{3,1},{4,6},{5,7},{6,4},{7,5},{8,10},{9,11},{10,... | collective-permute-start | bytes 147464 | tf_op jit(solution)/shard_map/ppermute | solution.py:437
  41.2 5.4 %collective-permute-start.14 = (bf16[48,512]{1,0:T(8,128)(2,1)S(1)}, bf16[48,512]{1,0:T(8,128)(2,1)S(1)}, u32[]{:S(2)}, u32[]{:S(2)}) collective-permute-start(bf16[48,512]{1,0:T(8,128)(2,1)S(1)} %get-tuple-element.20), channel_id=1, source_target_pairs={{0,4},{1,5},{2,6},{3,7},{4,0},{5,1},{6,2},{7,3},{8,12},{9,13},{10,... | collective-permute-start | bytes 147464 | tf_op jit(solution)/shard_map/ppermute | solution.py:444
  43.6 5.9 %collective-permute-start.16 = (bf16[48,512]{1,0:T(8,128)(2,1)S(1)}, bf16[48,512]{1,0:T(8,128)(2,1)S(1)}, u32[]{:S(2)}, u32[]{:S(2)}) collective-permute-start(bf16[48,512]{1,0:T(8,128)(2,1)S(1)} %get-tuple-element.21), channel_id=1, source_target_pairs={{0,6},{1,7},{2,4},{3,5},{4,2},{5,3},{6,0},{7,1},{8,14},{9,15},{10,... | collective-permute-start | bytes 147464 | tf_op jit(solution)/shard_map/ppermute | solution.py:444
  49.5 4.7 %collective-permute-start.18 = (f32[48,512]{1,0:T(8,128)S(1)}, f32[48,512]{1,0:T(8,128)S(1)}, u32[]{:S(2)}, u32[]{:S(2)}) collective-permute-start(f32[48,512]{1,0:T(8,128)S(1)} %fusion.5.refs_0_), channel_id=1, source_target_pairs={{0,16},{8,24},{16,0},{24,8},{1,17},{9,25},{17,1},{25,9},{2,18},{10... | collective-permute-start | bytes 294920 | tf_op jit(solution)/shard_map/ppermute | solution.py:450
  51.1 3.1 %collective-permute-start.17 = (f32[48,512]{1,0:T(8,128)S(1)}, f32[48,512]{1,0:T(8,128)S(1)}, u32[]{:S(2)}, u32[]{:S(2)}) collective-permute-start(f32[48,512]{1,0:T(8,128)S(1)} %fusion.5.refs_0_), channel_id=1, source_target_pairs={{0,8},{8,0},{16,24},{24,16},{1,9},{9,1},{17,25},{25,17},{2,10},{10... | collective-permute-start | bytes 294920 | tf_op jit(solution)/shard_map/ppermute | solution.py:450
  54.2 1.3 %collective-permute-start.19 = (f32[48,512]{1,0:T(8,128)S(1)}, f32[48,512]{1,0:T(8,128)S(1)}, u32[]{:S(2)}, u32[]{:S(2)}) collective-permute-start(f32[48,512]{1,0:T(8,128)S(1)} %collective-permute-done.18.refs_2_), channel_id=1, source_target_pairs={{0,8},{8,0},{16,24},{24,16},{1,9},{9,1},{17,25},{25,17},{2,10},{10... | collective-permute-start | bytes 294920 | tf_op jit(solution)/shard_map/ppermute | solution.py:450

commit v9 on v8

--- a/solution.py
+++ b/solution.py
@@ -251,14 +251,16 @@
     net_ref[...] = (injections - demand).astype(jnp.bfloat16)
 
 
-def line_kernel(pattern_smem, *refs, half):
+def line_kernel(pattern_ref, *refs, half):
     net_refs, refs = refs[: 2 * half], refs[2 * half :]
     blocks_ref, limits_ref, old_ref, price_hbm, new_hbm, spread_all, far_out = refs[:7]
-    net_all, new_ref, price_ref, sems = refs[7:]
+    pattern_smem, net_all, new_ref, price_ref, sems = refs[7:]
+    pattern_copy = pltpu.make_async_copy(pattern_ref, pattern_smem, sems.at[2])
+    pattern_copy.start()
     price_copy = pltpu.make_async_copy(price_hbm, price_ref, sems.at[0])
     price_copy.start()
     new_copy = pltpu.make_async_copy(new_ref, new_hbm, sems.at[1])
-    line_blocks, branches = pattern_smem.shape
+    line_blocks, branches = pattern_ref.shape
     _, hours, scn_dev, _ = old_ref.shape
     bus_dev = net_refs[0].shape[1]
     per_dev = bus_dev // BLK
@@ -268,6 +270,7 @@
     for at, net_ref in enumerate(net_refs):
         net_all[at] = net_ref[...]
     spread_all[...] = jnp.zeros(spread_all.shape, jnp.float32)
+    pattern_copy.wait()
 
     def spot(line, branch):
         block = pattern_smem[line, branch]
@@ -327,7 +330,6 @@
 def run_lines(pattern, nets, blocks, limits, old, bus_price):
     ring = len(nets)
     half = ring // 2
-    smem = pl.BlockSpec(memory_space=pltpu.SMEM)
     vmem = pl.BlockSpec(memory_space=pltpu.VMEM)
     hbm = pl.BlockSpec(memory_space=pltpu.HBM)
     return pl.pallas_call(
@@ -337,13 +339,14 @@
             jax.ShapeDtypeStruct((ring,) + nets[0].shape, jnp.float32),
             jax.ShapeDtypeStruct((half + 1,) + nets[0].shape, jnp.bfloat16),
         ),
-        in_specs=[smem] + [vmem] * (ring + 3) + [hbm],
+        in_specs=[vmem] * (ring + 4) + [hbm],
         out_specs=(hbm, vmem, vmem),
         scratch_shapes=[
+            pltpu.SMEM(pattern.shape, jnp.int32),
             pltpu.VMEM((ring,) + nets[0].shape, jnp.bfloat16),
             pltpu.VMEM(old.shape, jnp.float32),
             pltpu.VMEM(bus_price.shape, jnp.float32),
-            pltpu.SemaphoreType.DMA((2,)),
+            pltpu.SemaphoreType.DMA((3,)),
         ],
         compiler_params=pltpu.CompilerParams(vmem_limit_bytes=24 * 2**20),
         name="lines",

time: 56.5 us -> 56 us (level)
  no operation moved by 1% of the time
where the time goes in v9:
time: 56 us; the launch traced here: 55.8 us
  starting transfers between devices  23.4 us (42%)
  waiting for transfers between devices  16.1 us (29%)
  Pallas kernels  15.5 us (28%)
  between operations  0.71 us (1%)
    pallas_call x1, Pallas kernels, run_plan(): pl.pallas_call(functools.partial(plan_kernel, gens=gens, parts=parts), ou...  10.6 us
    ppermute x2, waiting for transfers between devices, shards(): shares = [lax.ppermute(share, 'bus', trade(ring, 2 * step))]  5.57 us
    ppermute x3, starting transfers between devices, shards(): lax.ppermute(net, 'bus', trade(ring, 2 * step))  5.55 us
    ppermute x3, waiting for transfers between devices, shards(): shares.append(lax.ppermute(moved, 'gen', trade(parts, by)))  4.39 us
    ppermute x3, starting transfers between devices, shards(): shares = [lax.ppermute(far_part[step], 'bus', trade(ring, 1))]  3.58 us
    pallas_call x1, Pallas kernels, run_lines(): pl.pallas_call(functools.partial(line_kernel, half=half), out_shape=(jax....  3.54 us
    ppermute x3, starting transfers between devices, shards(): lax.ppermute(handed[step], 'bus', trade(ring, 1))  3.37 us
    ppermute x1, starting transfers between devices, shards(): both = lax.ppermute(plan[step:step + 2], 'gen', trade(parts, step))  3.03 us
  transfers between devices with their start and end apart: 20, of which 11 were waited for; matrix products, arithmetic and copies ran while one was open for 0% of the time, Pallas kernels for 0%

profile of v9, /device:TPU:0, one launch (start us, length us, event | category | flops | bytes accessed | tf_op | source)
XLA Modules:
  0.0 55.8 jit_solution(18437653060346968946)
XLA Ops:
  0.6 10.6 %plan.1 = (f32[4,2,4,128]{3,2,1,0:T(4,128)S(1)}, f32[12,4,512]{2,1,0:T(4,128)S(1)}, bf16[6,16,128,128]{3,2,1,0:T(8,128)(2,1)S(1)}, f32[2,12,4,768]{3,2,1,0:T(4,1...) custom-call(s32[16]{0:T(128)} %refs_0_.1, s32[16]{0:T(128)} %refs_1_.1, s32[3,16,512]{2,1,0:T(8,128)} %bitcast.38, ...), custom_call_target="tpu_custom_call" | custom-call | tf_op jit(solution)/shard_map/plan/pallas_call | solution.py:182
  11.3 3.0 %collective-permute-start.1 = (f32[2,2,4,128]{3,2,1,0:T(4,128)S(1)}, f32[2,2,4,128]{3,2,1,0:T(4,128)S(1)}, u32[]{:S(2)}, u32[]{:S(2)}) collective-permute-start(f32[2,2,4,128]{3,2,1,0:T(4,128)S(1)} %slice.34), channel_id=1, source_target_pairs={{0,16},{8,24},{16,0},{24,8},{1,17},{9,25},{17,1},{25,9},{2,18},{10... | collective-permute-start | bytes 24584 | tf_op jit(solution)/shard_map/ppermute | solution.py:413
  14.3 0.0 collective-permute-start
  14.3 1.6 %collective-permute-done.1.refs_2_ = f32[2,2,4,128]{3,2,1,0:T(4,128)S(1)} collective-permute-done((f32[2,2,4,128]{3,2,1,0:T(4,128)S(1)}, f32[2,2,4,128]{3,2,1,0:T(4,128)S(1)}, u32[]{:S(2)}, u32[]{:S(2)}) %collective-permute-start.1) | collective-permute-done | bytes 8224 | tf_op jit(solution)/shard_map/ppermute | solution.py:413
  15.9 0.0 collective-permute-start.2
  15.9 0.0 collective-permute-done.refs_1_
  16.0 1.2 %collective-permute-done.2.refs_3_ = f32[1,2,4,128]{3,2,1,0:T(4,128)S(1)} collective-permute-done((f32[1,2,4,128]{3,2,1,0:T(4,128)S(1)}, f32[1,2,4,128]{3,2,1,0:T(4,128)S(1)}, u32[]{:S(2)}, u32[]{:S(2)}) %collective-permute-start.2) | collective-permute-done | bytes 4128 | tf_op jit(solution)/shard_map/ppermute | solution.py:414
  17.1 0.5 net.1.refs_0_
  17.7 4.2 %collective-permute-start.5 = (bf16[48,512]{1,0:T(8,128)(2,1)S(1)}, bf16[48,512]{1,0:T(8,128)(2,1)S(1)}, u32[]{:S(2)}, u32[]{:S(2)}) collective-permute-start(bf16[48,512]{1,0:T(8,128)(2,1)S(1)} %net.1.refs_0_), channel_id=1, source_target_pairs={{0,6},{1,7},{2,4},{3,5},{4,2},{5,3},{6,0},{7,1},{8,14},{9,15},{10,... | collective-permute-start | bytes 147464 | tf_op jit(solution)/shard_map/ppermute | solution.py:424
  21.8 0.0 collective-permute-start.4
  21.8 1.7 %collective-permute-start.7 = (bf16[48,512]{1,0:T(8,128)(2,1)S(1)}, bf16[48,512]{1,0:T(8,128)(2,1)S(1)}, u32[]{:S(2)}, u32[]{:S(2)}) collective-permute-start(bf16[48,512]{1,0:T(8,128)(2,1)S(1)} %net.1.refs_0_), channel_id=1, source_target_pairs={{0,3},{1,2},{2,1},{3,0},{4,7},{5,6},{6,5},{7,4},{8,11},{9,10},{10,... | collective-permute-start | bytes 147464 | tf_op jit(solution)/shard_map/ppermute | solution.py:427
  23.5 0.4 collective-permute-start.6
  23.9 1.4 %collective-permute-start.3 = (bf16[48,512]{1,0:T(8,128)(2,1)S(1)}, bf16[48,512]{1,0:T(8,128)(2,1)S(1)}, u32[]{:S(2)}, u32[]{:S(2)}) collective-permute-start(bf16[48,512]{1,0:T(8,128)(2,1)S(1)} %net.1.refs_0_), channel_id=1, source_target_pairs={{0,2},{1,3},{2,0},{3,1},{4,6},{5,7},{6,4},{7,5},{8,10},{9,11},{10,... | collective-permute-start | bytes 147464 | tf_op jit(solution)/shard_map/ppermute | solution.py:424
  25.3 0.0 collective-permute-done.5.refs_3_
  25.3 1.5 %collective-permute-start.9 = (bf16[48,512]{1,0:T(8,128)(2,1)S(1)}, bf16[48,512]{1,0:T(8,128)(2,1)S(1)}, u32[]{:S(2)}, u32[]{:S(2)}) collective-permute-start(bf16[48,512]{1,0:T(8,128)(2,1)S(1)} %collective-permute-done.5.refs_3_), channel_id=1, source_target_pairs={{0,1},{1,0},{2,3},{3,2},{4,5},{5,4},{6,7},{7,6},{8,9},{9,8},{10,11... | collective-permute-start | bytes 147464 | tf_op jit(solution)/shard_map/ppermute | solution.py:429
  26.8 0.1 collective-permute-done.4.refs_2_
  26.9 1.5 %collective-permute-start.8 = (bf16[48,512]{1,0:T(8,128)(2,1)S(1)}, bf16[48,512]{1,0:T(8,128)(2,1)S(1)}, u32[]{:S(2)}, u32[]{:S(2)}) collective-permute-start(bf16[48,512]{1,0:T(8,128)(2,1)S(1)} %collective-permute-done.4.refs_2_), channel_id=1, source_target_pairs={{0,1},{1,0},{2,3},{3,2},{4,5},{5,4},{6,7},{7,6},{8,9},{9,8},{10,11... | collective-permute-start | bytes 147464 | tf_op jit(solution)/shard_map/ppermute | solution.py:429
  28.4 0.0 collective-permute-done.7.refs_5_
  28.4 0.0 collective-permute-done.6.refs_4_
  28.4 0.0 collective-permute-done.3.refs_1_
  28.4 1.4 %collective-permute-done.9.refs_7_ = bf16[48,512]{1,0:T(8,128)(2,1)S(1)} collective-permute-done((bf16[48,512]{1,0:T(8,128)(2,1)S(1)}, bf16[48,512]{1,0:T(8,128)(2,1)S(1)}, u32[]{:S(2)}, u32[]{:S(2)}) %collective-permute-start.9) | collective-permute-done | bytes 49184 | tf_op jit(solution)/shard_map/ppermute | solution.py:429
  29.8 1.1 %collective-permute-done.8.refs_6_ = bf16[48,512]{1,0:T(8,128)(2,1)S(1)} collective-permute-done((bf16[48,512]{1,0:T(8,128)(2,1)S(1)}, bf16[48,512]{1,0:T(8,128)(2,1)S(1)}, u32[]{:S(2)}, u32[]{:S(2)}) %collective-permute-start.8) | collective-permute-done | bytes 49184 | tf_op jit(solution)/shard_map/ppermute | solution.py:429
  31.0 3.5 %lines.1 = (f32[2,12,4,768]{3,2,1,0:T(4,128)}, f32[8,48,512]{2,1,0:T(8,128)S(1)}, bf16[5,48,512]{2,1,0:T(8,128)(2,1)S(1)}) custom-call(s32[6,16]{1,0:T(8,128)S(1)} %get-tuple-element.11.pattern_ref, bf16[48,512]{1,0:T(8,128)(2,1)S(1)} %net.1.refs_0_, bf16[48,512]{1,0:T(8,128)(2,1)S(1)} %collective-permute-done.3.refs_1_, ...), custom_call_target="tpu_custom_call" | custom-call | tf_op jit(solution)/shard_map/lines/pallas_call | solution.py:335
  34.5 1.6 %collective-permute-start.15 = (bf16[48,512]{1,0:T(8,128)(2,1)S(1)}, bf16[48,512]{1,0:T(8,128)(2,1)S(1)}, u32[]{:S(2)}, u32[]{:S(2)}) collective-permute-start(bf16[48,512]{1,0:T(8,128)(2,1)S(1)} %get-tuple-element.23), channel_id=1, source_target_pairs={{0,1},{1,0},{2,3},{3,2},{4,5},{5,4},{6,7},{7,6},{8,9},{9,8},{10,11... | collective-permute-start | bytes 147464 | tf_op jit(solution)/shard_map/ppermute | solution.py:444
  36.1 0.5 collective-permute-start.13
  36.6 1.5 %collective-permute-start.10 = (bf16[48,512]{1,0:T(8,128)(2,1)S(1)}, bf16[48,512]{1,0:T(8,128)(2,1)S(1)}, u32[]{:S(2)}, u32[]{:S(2)}) collective-permute-start(bf16[48,512]{1,0:T(8,128)(2,1)S(1)} %get-tuple-element.22), channel_id=1, source_target_pairs={{0,1},{1,0},{2,3},{3,2},{4,5},{5,4},{6,7},{7,6},{8,9},{9,8},{10,11... | collective-permute-start | bytes 147464 | tf_op jit(solution)/shard_map/ppermute | solution.py:444
  38.1 0.7 %collective-permute-start.12 = (bf16[48,512]{1,0:T(8,128)(2,1)S(1)}, bf16[48,512]{1,0:T(8,128)(2,1)S(1)}, u32[]{:S(2)}, u32[]{:S(2)}) collective-permute-start(bf16[48,512]{1,0:T(8,128)(2,1)S(1)} %get-tuple-element.25), channel_id=1, source_target_pairs={{0,3},{1,2},{2,1},{3,0},{4,7},{5,6},{6,5},{7,4},{8,11},{9,10},{10,... | collective-permute-start | bytes 147464 | tf_op jit(solution)/shard_map/ppermute | solution.py:441
  38.8 1.3 %collective-permute-start.11 = (bf16[48,512]{1,0:T(8,128)(2,1)S(1)}, bf16[48,512]{1,0:T(8,128)(2,1)S(1)}, u32[]{:S(2)}, u32[]{:S(2)}) collective-permute-start(bf16[48,512]{1,0:T(8,128)(2,1)S(1)} %get-tuple-element.26), channel_id=1, source_target_pairs={{0,2},{1,3},{2,0},{3,1},{4,6},{5,7},{6,4},{7,5},{8,10},{9,11},{10,... | collective-permute-start | bytes 147464 | tf_op jit(solution)/shard_map/ppermute | solution.py:440
  40.1 0.0 collective-permute-done.15
  40.1 0.6 collective-permute-done.13
  40.7 2.4 %collective-permute-start.14 = (bf16[48,512]{1,0:T(8,128)(2,1)S(1)}, bf16[48,512]{1,0:T(8,128)(2,1)S(1)}, u32[]{:S(2)}, u32[]{:S(2)}) collective-permute-start(bf16[48,512]{1,0:T(8,128)(2,1)S(1)} %get-tuple-element.20), channel_id=1, source_target_pairs={{0,4},{1,5},{2,6},{3,7},{4,0},{5,1},{6,2},{7,3},{8,12},{9,13},{10,... | collective-permute-start | bytes 147464 | tf_op jit(solution)/shard_map/ppermute | solution.py:447
  43.1 0.2 collective-permute-start.16
  43.3 0.0 collective-permute-done.10
  43.3 0.1 collective-permute-done.12
  43.4 0.0 collective-permute-done.11
  43.4 2.7 %collective-permute-done.14 = bf16[48,512]{1,0:T(8,128)(2,1)S(1)} collective-permute-done((bf16[48,512]{1,0:T(8,128)(2,1)S(1)}, bf16[48,512]{1,0:T(8,128)(2,1)S(1)}, u32[]{:S(2)}, u32[]{:S(2)}) %collective-permute-start.14) | collective-permute-done | bytes 49184 | tf_op jit(solution)/shard_map/ppermute | solution.py:447
  46.1 2.9 %collective-permute-done.16 = bf16[48,512]{1,0:T(8,128)(2,1)S(1)} collective-permute-done((bf16[48,512]{1,0:T(8,128)(2,1)S(1)}, bf16[48,512]{1,0:T(8,128)(2,1)S(1)}, u32[]{:S(2)}, u32[]{:S(2)}) %collective-permute-start.16) | collective-permute-done | bytes 49184 | tf_op jit(solution)/shard_map/ppermute | solution.py:447
  49.0 1.6 %collective-permute-start.18 = (f32[48,512]{1,0:T(8,128)S(1)}, f32[48,512]{1,0:T(8,128)S(1)}, u32[]{:S(2)}, u32[]{:S(2)}) collective-permute-start(f32[48,512]{1,0:T(8,128)S(1)} %fusion.5.refs_0_), channel_id=1, source_target_pairs={{0,16},{8,24},{16,0},{24,8},{1,17},{9,25},{17,1},{25,9},{2,18},{10... | collective-permute-start | bytes 294920 | tf_op jit(solution)/shard_map/ppermute | solution.py:453
  50.6 0.0 collective-permute-start.17
  50.6 3.1 %collective-permute-done.18.refs_2_ = f32[48,512]{1,0:T(8,128)S(1)} collective-permute-done((f32[48,512]{1,0:T(8,128)S(1)}, f32[48,512]{1,0:T(8,128)S(1)}, u32[]{:S(2)}, u32[]{:S(2)}) %collective-permute-start.18) | collective-permute-done | bytes 98336 | tf_op jit(solution)/shard_map/ppermute | solution.py:453
  53.7 0.0 collective-permute-start.19
  53.7 0.0 collective-permute-done.17.refs_1_
  53.7 1.3 %collective-permute-done.19.refs_3_ = f32[48,512]{1,0:T(8,128)S(1)} collective-permute-done((f32[48,512]{1,0:T(8,128)S(1)}, f32[48,512]{1,0:T(8,128)S(1)}, u32[]{:S(2)}, u32[]{:S(2)}) %collective-permute-start.19) | collective-permute-done | bytes 98336 | tf_op jit(solution)/shard_map/ppermute | solution.py:453
  55.0 0.8 %price.1 = f32[12,16,512]{2,1,0:T(8,128)} custom-call(f32[48,512]{1,0:T(8,128)S(1)} %fusion.5.refs_0_, f32[48,512]{1,0:T(8,128)S(1)} %collective-permute-done.17.refs_1_, f32[48,512]{1,0:T(8,128)S(1)} %collective-permute-done.18.refs_2_, f32[48,512]{1,0:T(8,128)S(1)} %collective-permute-done.19.refs_3_), custom_call_target="tpu_custom_call" | custom-call | tf_op jit(solution)/shard_map/price/pallas_call | solution.py:454
  (6 shorter events, 0.1 us)
Async XLA Ops:
  11.3 4.7 %collective-permute-start.1 = (f32[2,2,4,128]{3,2,1,0:T(4,128)S(1)}, f32[2,2,4,128]{3,2,1,0:T(4,128)S(1)}, u32[]{:S(2)}, u32[]{:S(2)}) collective-permute-start(f32[2,2,4,128]{3,2,1,0:T(4,128)S(1)} %slice.34), channel_id=1, source_target_pairs={{0,16},{8,24},{16,0},{24,8},{1,17},{9,25},{17,1},{25,9},{2,18},{10... | collective-permute-start | bytes 24584 | tf_op jit(solution)/shard_map/ppermute | solution.py:413
  14.3 1.6 %collective-permute-start = (f32[1,2,4,128]{3,2,1,0:T(4,128)S(1)}, f32[1,2,4,128]{3,2,1,0:T(4,128)S(1)}, u32[]{:S(2)}, u32[]{:S(2)}) collective-permute-start(f32[1,2,4,128]{3,2,1,0:T(4,128)S(1)} %slice.33), channel_id=1, source_target_pairs={{0,8},{8,0},{16,24},{24,16},{1,9},{9,1},{17,25},{25,17},{2,10},{10... | collective-permute-start | bytes 12296 | tf_op jit(solution)/shard_map/ppermute | solution.py:411
  15.9 1.2 %collective-permute-start.2 = (f32[1,2,4,128]{3,2,1,0:T(4,128)S(1)}, f32[1,2,4,128]{3,2,1,0:T(4,128)S(1)}, u32[]{:S(2)}, u32[]{:S(2)}) collective-permute-start(f32[1,2,4,128]{3,2,1,0:T(4,128)S(1)} %slice.44), channel_id=1, source_target_pairs={{0,8},{8,0},{16,24},{24,16},{1,9},{9,1},{17,25},{25,17},{2,10},{10... | collective-permute-start | bytes 12296 | tf_op jit(solution)/shard_map/ppermute | solution.py:414
  17.7 7.7 %collective-permute-start.5 = (bf16[48,512]{1,0:T(8,128)(2,1)S(1)}, bf16[48,512]{1,0:T(8,128)(2,1)S(1)}, u32[]{:S(2)}, u32[]{:S(2)}) collective-permute-start(bf16[48,512]{1,0:T(8,128)(2,1)S(1)} %net.1.refs_0_), channel_id=1, source_target_pairs={{0,6},{1,7},{2,4},{3,5},{4,2},{5,3},{6,0},{7,1},{8,14},{9,15},{10,... | collective-permute-start | bytes 147464 | tf_op jit(solution)/shard_map/ppermute | solution.py:424
  21.8 5.1 %collective-permute-start.4 = (bf16[48,512]{1,0:T(8,128)(2,1)S(1)}, bf16[48,512]{1,0:T(8,128)(2,1)S(1)}, u32[]{:S(2)}, u32[]{:S(2)}) collective-permute-start(bf16[48,512]{1,0:T(8,128)(2,1)S(1)} %net.1.refs_0_), channel_id=1, source_target_pairs={{0,4},{1,5},{2,6},{3,7},{4,0},{5,1},{6,2},{7,3},{8,12},{9,13},{10,... | collective-permute-start | bytes 147464 | tf_op jit(solution)/shard_map/ppermute | solution.py:424
  21.8 6.5 %collective-permute-start.7 = (bf16[48,512]{1,0:T(8,128)(2,1)S(1)}, bf16[48,512]{1,0:T(8,128)(2,1)S(1)}, u32[]{:S(2)}, u32[]{:S(2)}) collective-permute-start(bf16[48,512]{1,0:T(8,128)(2,1)S(1)} %net.1.refs_0_), channel_id=1, source_target_pairs={{0,3},{1,2},{2,1},{3,0},{4,7},{5,6},{6,5},{7,4},{8,11},{9,10},{10,... | collective-permute-start | bytes 147464 | tf_op jit(solution)/shard_map/ppermute | solution.py:427
  23.5 4.8 %collective-permute-start.6 = (bf16[48,512]{1,0:T(8,128)(2,1)S(1)}, bf16[48,512]{1,0:T(8,128)(2,1)S(1)}, u32[]{:S(2)}, u32[]{:S(2)}) collective-permute-start(bf16[48,512]{1,0:T(8,128)(2,1)S(1)} %net.1.refs_0_), channel_id=1, source_target_pairs={{0,1},{1,0},{2,3},{3,2},{4,5},{5,4},{6,7},{7,6},{8,9},{9,8},{10,11... | collective-permute-start | bytes 147464 | tf_op jit(solution)/shard_map/ppermute | solution.py:429
  23.9 4.5 %collective-permute-start.3 = (bf16[48,512]{1,0:T(8,128)(2,1)S(1)}, bf16[48,512]{1,0:T(8,128)(2,1)S(1)}, u32[]{:S(2)}, u32[]{:S(2)}) collective-permute-start(bf16[48,512]{1,0:T(8,128)(2,1)S(1)} %net.1.refs_0_), channel_id=1, source_target_pairs={{0,2},{1,3},{2,0},{3,1},{4,6},{5,7},{6,4},{7,5},{8,10},{9,11},{10,... | collective-permute-start | bytes 147464 | tf_op jit(solution)/shard_map/ppermute | solution.py:424
  25.3 4.5 %collective-permute-start.9 = (bf16[48,512]{1,0:T(8,128)(2,1)S(1)}, bf16[48,512]{1,0:T(8,128)(2,1)S(1)}, u32[]{:S(2)}, u32[]{:S(2)}) collective-permute-start(bf16[48,512]{1,0:T(8,128)(2,1)S(1)} %collective-permute-done.5.refs_3_), channel_id=1, source_target_pairs={{0,1},{1,0},{2,3},{3,2},{4,5},{5,4},{6,7},{7,6},{8,9},{9,8},{10,11... | collective-permute-start | bytes 147464 | tf_op jit(solution)/shard_map/ppermute | solution.py:429
  26.9 4.1 %collective-permute-start.8 = (bf16[48,512]{1,0:T(8,128)(2,1)S(1)}, bf16[48,512]{1,0:T(8,128)(2,1)S(1)}, u32[]{:S(2)}, u32[]{:S(2)}) collective-permute-start(bf16[48,512]{1,0:T(8,128)(2,1)S(1)} %collective-permute-done.4.refs_2_), channel_id=1, source_target_pairs={{0,1},{1,0},{2,3},{3,2},{4,5},{5,4},{6,7},{7,6},{8,9},{9,8},{10,11... | collective-permute-start | bytes 147464 | tf_op jit(solution)/shard_map/ppermute | solution.py:429
  34.5 5.6 %collective-permute-start.15 = (bf16[48,512]{1,0:T(8,128)(2,1)S(1)}, bf16[48,512]{1,0:T(8,128)(2,1)S(1)}, u32[]{:S(2)}, u32[]{:S(2)}) collective-permute-start(bf16[48,512]{1,0:T(8,128)(2,1)S(1)} %get-tuple-element.23), channel_id=1, source_target_pairs={{0,1},{1,0},{2,3},{3,2},{4,5},{5,4},{6,7},{7,6},{8,9},{9,8},{10,11... | collective-permute-start | bytes 147464 | tf_op jit(solution)/shard_map/ppermute | solution.py:444
  36.1 4.6 %collective-permute-start.13 = (bf16[48,512]{1,0:T(8,128)(2,1)S(1)}, bf16[48,512]{1,0:T(8,128)(2,1)S(1)}, u32[]{:S(2)}, u32[]{:S(2)}) collective-permute-start(bf16[48,512]{1,0:T(8,128)(2,1)S(1)} %get-tuple-element.24), channel_id=1, source_target_pairs={{0,1},{1,0},{2,3},{3,2},{4,5},{5,4},{6,7},{7,6},{8,9},{9,8},{10,11... | collective-permute-start | bytes 147464 | tf_op jit(solution)/shard_map/ppermute | solution.py:444
  36.6 6.7 %collective-permute-start.10 = (bf16[48,512]{1,0:T(8,128)(2,1)S(1)}, bf16[48,512]{1,0:T(8,128)(2,1)S(1)}, u32[]{:S(2)}, u32[]{:S(2)}) collective-permute-start(bf16[48,512]{1,0:T(8,128)(2,1)S(1)} %get-tuple-element.22), channel_id=1, source_target_pairs={{0,1},{1,0},{2,3},{3,2},{4,5},{5,4},{6,7},{7,6},{8,9},{9,8},{10,11... | collective-permute-start | bytes 147464 | tf_op jit(solution)/shard_map/ppermute | solution.py:444
  38.1 5.3 %collective-permute-start.12 = (bf16[48,512]{1,0:T(8,128)(2,1)S(1)}, bf16[48,512]{1,0:T(8,128)(2,1)S(1)}, u32[]{:S(2)}, u32[]{:S(2)}) collective-permute-start(bf16[48,512]{1,0:T(8,128)(2,1)S(1)} %get-tuple-element.25), channel_id=1, source_target_pairs={{0,3},{1,2},{2,1},{3,0},{4,7},{5,6},{6,5},{7,4},{8,11},{9,10},{10,... | collective-permute-start | bytes 147464 | tf_op jit(solution)/shard_map/ppermute | solution.py:441
  38.8 4.6 %collective-permute-start.11 = (bf16[48,512]{1,0:T(8,128)(2,1)S(1)}, bf16[48,512]{1,0:T(8,128)(2,1)S(1)}, u32[]{:S(2)}, u32[]{:S(2)}) collective-permute-start(bf16[48,512]{1,0:T(8,128)(2,1)S(1)} %get-tuple-element.26), channel_id=1, source_target_pairs={{0,2},{1,3},{2,0},{3,1},{4,6},{5,7},{6,4},{7,5},{8,10},{9,11},{10,... | collective-permute-start | bytes 147464 | tf_op jit(solution)/shard_map/ppermute | solution.py:440
  40.7 5.4 %collective-permute-start.14 = (bf16[48,512]{1,0:T(8,128)(2,1)S(1)}, bf16[48,512]{1,0:T(8,128)(2,1)S(1)}, u32[]{:S(2)}, u32[]{:S(2)}) collective-permute-start(bf16[48,512]{1,0:T(8,128)(2,1)S(1)} %get-tuple-element.20), channel_id=1, source_target_pairs={{0,4},{1,5},{2,6},{3,7},{4,0},{5,1},{6,2},{7,3},{8,12},{9,13},{10,... | collective-permute-start | bytes 147464 | tf_op jit(solution)/shard_map/ppermute | solution.py:447
  43.1 5.9 %collective-permute-start.16 = (bf16[48,512]{1,0:T(8,128)(2,1)S(1)}, bf16[48,512]{1,0:T(8,128)(2,1)S(1)}, u32[]{:S(2)}, u32[]{:S(2)}) collective-permute-start(bf16[48,512]{1,0:T(8,128)(2,1)S(1)} %get-tuple-element.21), channel_id=1, source_target_pairs={{0,6},{1,7},{2,4},{3,5},{4,2},{5,3},{6,0},{7,1},{8,14},{9,15},{10,... | collective-permute-start | bytes 147464 | tf_op jit(solution)/shard_map/ppermute | solution.py:447
  49.0 4.7 %collective-permute-start.18 = (f32[48,512]{1,0:T(8,128)S(1)}, f32[48,512]{1,0:T(8,128)S(1)}, u32[]{:S(2)}, u32[]{:S(2)}) collective-permute-start(f32[48,512]{1,0:T(8,128)S(1)} %fusion.5.refs_0_), channel_id=1, source_target_pairs={{0,16},{8,24},{16,0},{24,8},{1,17},{9,25},{17,1},{25,9},{2,18},{10... | collective-permute-start | bytes 294920 | tf_op jit(solution)/shard_map/ppermute | solution.py:453
  50.6 3.1 %collective-permute-start.17 = (f32[48,512]{1,0:T(8,128)S(1)}, f32[48,512]{1,0:T(8,128)S(1)}, u32[]{:S(2)}, u32[]{:S(2)}) collective-permute-start(f32[48,512]{1,0:T(8,128)S(1)} %fusion.5.refs_0_), channel_id=1, source_target_pairs={{0,8},{8,0},{16,24},{24,16},{1,9},{9,1},{17,25},{25,17},{2,10},{10... | collective-permute-start | bytes 294920 | tf_op jit(solution)/shard_map/ppermute | solution.py:453
  53.7 1.3 %collective-permute-start.19 = (f32[48,512]{1,0:T(8,128)S(1)}, f32[48,512]{1,0:T(8,128)S(1)}, u32[]{:S(2)}, u32[]{:S(2)}) collective-permute-start(f32[48,512]{1,0:T(8,128)S(1)} %collective-permute-done.18.refs_2_), channel_id=1, source_target_pairs={{0,8},{8,0},{16,24},{24,16},{1,9},{9,1},{17,25},{25,17},{2,10},{10... | collective-permute-start | bytes 294920 | tf_op jit(solution)/shard_map/ppermute | solution.py:453

commit v10 on v9

--- a/solution.py
+++ b/solution.py
@@ -120,11 +120,17 @@
     def repeat_rows(block, copies):
         return block if copies == 1 else jnp.concatenate([block] * copies, axis=0)
 
+    mixed = sorted(
+        range(gens),
+        key=lambda slot: (slot + 0.5) / big_total
+        if slot < big_total
+        else (slot - big_total + 0.5) / (gens - big_total),
+    )
     shares = [None] * gens
     outs = [jnp.zeros((scn, LANES), jnp.float32) for _ in range(-(-hours // per_row))]
     for hour in range(hours - 1, -1, -1):
         chains = hours - 1 - hour
-        for slot in range(gens):
+        for slot in mixed:
             span = spans[slot]
             if slot < big_total:
                 state, table = big_state.at[slot], big_table.at[slot]

time: 56 us -> 56 us (level)
  no operation moved by 1% of the time
where the time goes in v10:
time: 56 us; the launch traced here: 55.8 us
  starting transfers between devices  23.4 us (42%)
  waiting for transfers between devices  16.1 us (29%)
  Pallas kernels  15.5 us (28%)
  between operations  0.71 us (1%)
    pallas_call x1, Pallas kernels, run_plan(): pl.pallas_call(functools.partial(plan_kernel, gens=gens, parts=parts), ou...  10.6 us
    ppermute x2, waiting for transfers between devices, shards(): shares = [lax.ppermute(share, 'bus', trade(ring, 2 * step))]  5.57 us
    ppermute x3, starting transfers between devices, shards(): lax.ppermute(net, 'bus', trade(ring, 2 * step))  5.56 us
    ppermute x3, waiting for transfers between devices, shards(): shares.append(lax.ppermute(moved, 'gen', trade(parts, by)))  4.4 us
    ppermute x3, starting transfers between devices, shards(): shares = [lax.ppermute(far_part[step], 'bus', trade(ring, 1))]  3.58 us
    pallas_call x1, Pallas kernels, run_lines(): pl.pallas_call(functools.partial(line_kernel, half=half), out_shape=(jax....  3.54 us
    ppermute x3, starting transfers between devices, shards(): lax.ppermute(handed[step], 'bus', trade(ring, 1))  3.37 us
    ppermute x1, starting transfers between devices, shards(): both = lax.ppermute(plan[step:step + 2], 'gen', trade(parts, step))  3.03 us
  transfers between devices with their start and end apart: 20, of which 11 were waited for; matrix products, arithmetic and copies ran while one was open for 0% of the time, Pallas kernels for 0%

profile of v10, /device:TPU:0, one launch (start us, length us, event | category | flops | bytes accessed | tf_op | source)
XLA Modules:
  0.0 55.8 jit_solution(4922958357215407100)
XLA Ops:
  0.6 10.6 %plan.1 = (f32[4,2,4,128]{3,2,1,0:T(4,128)S(1)}, f32[12,4,512]{2,1,0:T(4,128)S(1)}, bf16[6,16,128,128]{3,2,1,0:T(8,128)(2,1)S(1)}, f32[2,12,4,768]{3,2,1,0:T(4,1...) custom-call(s32[16]{0:T(128)} %refs_0_.1, s32[16]{0:T(128)} %refs_1_.1, s32[3,16,512]{2,1,0:T(8,128)} %bitcast.38, ...), custom_call_target="tpu_custom_call" | custom-call | tf_op jit(solution)/shard_map/plan/pallas_call | solution.py:188
  11.2 3.0 %collective-permute-start.1 = (f32[2,2,4,128]{3,2,1,0:T(4,128)S(1)}, f32[2,2,4,128]{3,2,1,0:T(4,128)S(1)}, u32[]{:S(2)}, u32[]{:S(2)}) collective-permute-start(f32[2,2,4,128]{3,2,1,0:T(4,128)S(1)} %slice.34), channel_id=1, source_target_pairs={{0,16},{8,24},{16,0},{24,8},{1,17},{9,25},{17,1},{25,9},{2,18},{10... | collective-permute-start | bytes 24584 | tf_op jit(solution)/shard_map/ppermute | solution.py:419
  14.3 0.0 collective-permute-start
  14.3 1.6 %collective-permute-done.1.refs_2_ = f32[2,2,4,128]{3,2,1,0:T(4,128)S(1)} collective-permute-done((f32[2,2,4,128]{3,2,1,0:T(4,128)S(1)}, f32[2,2,4,128]{3,2,1,0:T(4,128)S(1)}, u32[]{:S(2)}, u32[]{:S(2)}) %collective-permute-start.1) | collective-permute-done | bytes 8224 | tf_op jit(solution)/shard_map/ppermute | solution.py:419
  15.9 0.0 collective-permute-start.2
  15.9 0.0 collective-permute-done.refs_1_
  15.9 1.2 %collective-permute-done.2.refs_3_ = f32[1,2,4,128]{3,2,1,0:T(4,128)S(1)} collective-permute-done((f32[1,2,4,128]{3,2,1,0:T(4,128)S(1)}, f32[1,2,4,128]{3,2,1,0:T(4,128)S(1)}, u32[]{:S(2)}, u32[]{:S(2)}) %collective-permute-start.2) | collective-permute-done | bytes 4128 | tf_op jit(solution)/shard_map/ppermute | solution.py:420
  17.1 0.5 net.1.refs_0_
  17.6 4.2 %collective-permute-start.5 = (bf16[48,512]{1,0:T(8,128)(2,1)S(1)}, bf16[48,512]{1,0:T(8,128)(2,1)S(1)}, u32[]{:S(2)}, u32[]{:S(2)}) collective-permute-start(bf16[48,512]{1,0:T(8,128)(2,1)S(1)} %net.1.refs_0_), channel_id=1, source_target_pairs={{0,6},{1,7},{2,4},{3,5},{4,2},{5,3},{6,0},{7,1},{8,14},{9,15},{10,... | collective-permute-start | bytes 147464 | tf_op jit(solution)/shard_map/ppermute | solution.py:430
  21.8 0.0 collective-permute-start.4
  21.8 1.7 %collective-permute-start.7 = (bf16[48,512]{1,0:T(8,128)(2,1)S(1)}, bf16[48,512]{1,0:T(8,128)(2,1)S(1)}, u32[]{:S(2)}, u32[]{:S(2)}) collective-permute-start(bf16[48,512]{1,0:T(8,128)(2,1)S(1)} %net.1.refs_0_), channel_id=1, source_target_pairs={{0,3},{1,2},{2,1},{3,0},{4,7},{5,6},{6,5},{7,4},{8,11},{9,10},{10,... | collective-permute-start | bytes 147464 | tf_op jit(solution)/shard_map/ppermute | solution.py:433
  23.5 0.4 collective-permute-start.6
  23.9 1.4 %collective-permute-start.3 = (bf16[48,512]{1,0:T(8,128)(2,1)S(1)}, bf16[48,512]{1,0:T(8,128)(2,1)S(1)}, u32[]{:S(2)}, u32[]{:S(2)}) collective-permute-start(bf16[48,512]{1,0:T(8,128)(2,1)S(1)} %net.1.refs_0_), channel_id=1, source_target_pairs={{0,2},{1,3},{2,0},{3,1},{4,6},{5,7},{6,4},{7,5},{8,10},{9,11},{10,... | collective-permute-start | bytes 147464 | tf_op jit(solution)/shard_map/ppermute | solution.py:430
  25.3 0.0 collective-permute-done.5.refs_3_
  25.3 1.5 %collective-permute-start.9 = (bf16[48,512]{1,0:T(8,128)(2,1)S(1)}, bf16[48,512]{1,0:T(8,128)(2,1)S(1)}, u32[]{:S(2)}, u32[]{:S(2)}) collective-permute-start(bf16[48,512]{1,0:T(8,128)(2,1)S(1)} %collective-permute-done.5.refs_3_), channel_id=1, source_target_pairs={{0,1},{1,0},{2,3},{3,2},{4,5},{5,4},{6,7},{7,6},{8,9},{9,8},{10,11... | collective-permute-start | bytes 147464 | tf_op jit(solution)/shard_map/ppermute | solution.py:435
  26.8 0.1 collective-permute-done.4.refs_2_
  26.8 1.5 %collective-permute-start.8 = (bf16[48,512]{1,0:T(8,128)(2,1)S(1)}, bf16[48,512]{1,0:T(8,128)(2,1)S(1)}, u32[]{:S(2)}, u32[]{:S(2)}) collective-permute-start(bf16[48,512]{1,0:T(8,128)(2,1)S(1)} %collective-permute-done.4.refs_2_), channel_id=1, source_target_pairs={{0,1},{1,0},{2,3},{3,2},{4,5},{5,4},{6,7},{7,6},{8,9},{9,8},{10,11... | collective-permute-start | bytes 147464 | tf_op jit(solution)/shard_map/ppermute | solution.py:435
  28.3 0.0 collective-permute-done.7.refs_5_
  28.3 0.0 collective-permute-done.6.refs_4_
  28.3 0.0 collective-permute-done.3.refs_1_
  28.3 1.4 %collective-permute-done.9.refs_7_ = bf16[48,512]{1,0:T(8,128)(2,1)S(1)} collective-permute-done((bf16[48,512]{1,0:T(8,128)(2,1)S(1)}, bf16[48,512]{1,0:T(8,128)(2,1)S(1)}, u32[]{:S(2)}, u32[]{:S(2)}) %collective-permute-start.9) | collective-permute-done | bytes 49184 | tf_op jit(solution)/shard_map/ppermute | solution.py:435
  29.8 1.1 %collective-permute-done.8.refs_6_ = bf16[48,512]{1,0:T(8,128)(2,1)S(1)} collective-permute-done((bf16[48,512]{1,0:T(8,128)(2,1)S(1)}, bf16[48,512]{1,0:T(8,128)(2,1)S(1)}, u32[]{:S(2)}, u32[]{:S(2)}) %collective-permute-start.8) | collective-permute-done | bytes 49184 | tf_op jit(solution)/shard_map/ppermute | solution.py:435
  30.9 3.5 %lines.1 = (f32[2,12,4,768]{3,2,1,0:T(4,128)}, f32[8,48,512]{2,1,0:T(8,128)S(1)}, bf16[5,48,512]{2,1,0:T(8,128)(2,1)S(1)}) custom-call(s32[6,16]{1,0:T(8,128)S(1)} %get-tuple-element.11.pattern_ref, bf16[48,512]{1,0:T(8,128)(2,1)S(1)} %net.1.refs_0_, bf16[48,512]{1,0:T(8,128)(2,1)S(1)} %collective-permute-done.3.refs_1_, ...), custom_call_target="tpu_custom_call" | custom-call | tf_op jit(solution)/shard_map/lines/pallas_call | solution.py:341
  34.5 1.6 %collective-permute-start.15 = (bf16[48,512]{1,0:T(8,128)(2,1)S(1)}, bf16[48,512]{1,0:T(8,128)(2,1)S(1)}, u32[]{:S(2)}, u32[]{:S(2)}) collective-permute-start(bf16[48,512]{1,0:T(8,128)(2,1)S(1)} %get-tuple-element.23), channel_id=1, source_target_pairs={{0,1},{1,0},{2,3},{3,2},{4,5},{5,4},{6,7},{7,6},{8,9},{9,8},{10,11... | collective-permute-start | bytes 147464 | tf_op jit(solution)/shard_map/ppermute | solution.py:450
  36.1 0.5 collective-permute-start.13
  36.6 1.5 %collective-permute-start.10 = (bf16[48,512]{1,0:T(8,128)(2,1)S(1)}, bf16[48,512]{1,0:T(8,128)(2,1)S(1)}, u32[]{:S(2)}, u32[]{:S(2)}) collective-permute-start(bf16[48,512]{1,0:T(8,128)(2,1)S(1)} %get-tuple-element.22), channel_id=1, source_target_pairs={{0,1},{1,0},{2,3},{3,2},{4,5},{5,4},{6,7},{7,6},{8,9},{9,8},{10,11... | collective-permute-start | bytes 147464 | tf_op jit(solution)/shard_map/ppermute | solution.py:450
  38.1 0.7 %collective-permute-start.12 = (bf16[48,512]{1,0:T(8,128)(2,1)S(1)}, bf16[48,512]{1,0:T(8,128)(2,1)S(1)}, u32[]{:S(2)}, u32[]{:S(2)}) collective-permute-start(bf16[48,512]{1,0:T(8,128)(2,1)S(1)} %get-tuple-element.25), channel_id=1, source_target_pairs={{0,3},{1,2},{2,1},{3,0},{4,7},{5,6},{6,5},{7,4},{8,11},{9,10},{10,... | collective-permute-start | bytes 147464 | tf_op jit(solution)/shard_map/ppermute | solution.py:447
  38.8 1.3 %collective-permute-start.11 = (bf16[48,512]{1,0:T(8,128)(2,1)S(1)}, bf16[48,512]{1,0:T(8,128)(2,1)S(1)}, u32[]{:S(2)}, u32[]{:S(2)}) collective-permute-start(bf16[48,512]{1,0:T(8,128)(2,1)S(1)} %get-tuple-element.26), channel_id=1, source_target_pairs={{0,2},{1,3},{2,0},{3,1},{4,6},{5,7},{6,4},{7,5},{8,10},{9,11},{10,... | collective-permute-start | bytes 147464 | tf_op jit(solution)/shard_map/ppermute | solution.py:446
  40.1 0.0 collective-permute-done.15
  40.1 0.6 collective-permute-done.13
  40.7 2.4 %collective-permute-start.14 = (bf16[48,512]{1,0:T(8,128)(2,1)S(1)}, bf16[48,512]{1,0:T(8,128)(2,1)S(1)}, u32[]{:S(2)}, u32[]{:S(2)}) collective-permute-start(bf16[48,512]{1,0:T(8,128)(2,1)S(1)} %get-tuple-element.20), channel_id=1, source_target_pairs={{0,4},{1,5},{2,6},{3,7},{4,0},{5,1},{6,2},{7,3},{8,12},{9,13},{10,... | collective-permute-start | bytes 147464 | tf_op jit(solution)/shard_map/ppermute | solution.py:453
  43.0 0.2 collective-permute-start.16
  43.3 0.0 collective-permute-done.10
  43.3 0.1 collective-permute-done.12
  43.4 0.0 collective-permute-done.11
  43.4 2.7 %collective-permute-done.14 = bf16[48,512]{1,0:T(8,128)(2,1)S(1)} collective-permute-done((bf16[48,512]{1,0:T(8,128)(2,1)S(1)}, bf16[48,512]{1,0:T(8,128)(2,1)S(1)}, u32[]{:S(2)}, u32[]{:S(2)}) %collective-permute-start.14) | collective-permute-done | bytes 49184 | tf_op jit(solution)/shard_map/ppermute | solution.py:453
  46.0 2.9 %collective-permute-done.16 = bf16[48,512]{1,0:T(8,128)(2,1)S(1)} collective-permute-done((bf16[48,512]{1,0:T(8,128)(2,1)S(1)}, bf16[48,512]{1,0:T(8,128)(2,1)S(1)}, u32[]{:S(2)}, u32[]{:S(2)}) %collective-permute-start.16) | collective-permute-done | bytes 49184 | tf_op jit(solution)/shard_map/ppermute | solution.py:453
  49.0 1.6 %collective-permute-start.18 = (f32[48,512]{1,0:T(8,128)S(1)}, f32[48,512]{1,0:T(8,128)S(1)}, u32[]{:S(2)}, u32[]{:S(2)}) collective-permute-start(f32[48,512]{1,0:T(8,128)S(1)} %fusion.5.refs_0_), channel_id=1, source_target_pairs={{0,16},{8,24},{16,0},{24,8},{1,17},{9,25},{17,1},{25,9},{2,18},{10... | collective-permute-start | bytes 294920 | tf_op jit(solution)/shard_map/ppermute | solution.py:459
  50.6 0.0 collective-permute-start.17
  50.6 3.1 %collective-permute-done.18.refs_2_ = f32[48,512]{1,0:T(8,128)S(1)} collective-permute-done((f32[48,512]{1,0:T(8,128)S(1)}, f32[48,512]{1,0:T(8,128)S(1)}, u32[]{:S(2)}, u32[]{:S(2)}) %collective-permute-start.18) | collective-permute-done | bytes 98336 | tf_op jit(solution)/shard_map/ppermute | solution.py:459
  53.7 0.0 collective-permute-start.19
  53.7 0.0 collective-permute-done.17.refs_1_
  53.7 1.3 %collective-permute-done.19.refs_3_ = f32[48,512]{1,0:T(8,128)S(1)} collective-permute-done((f32[48,512]{1,0:T(8,128)S(1)}, f32[48,512]{1,0:T(8,128)S(1)}, u32[]{:S(2)}, u32[]{:S(2)}) %collective-permute-start.19) | collective-permute-done | bytes 98336 | tf_op jit(solution)/shard_map/ppermute | solution.py:459
  55.0 0.8 %price.1 = f32[12,16,512]{2,1,0:T(8,128)} custom-call(f32[48,512]{1,0:T(8,128)S(1)} %fusion.5.refs_0_, f32[48,512]{1,0:T(8,128)S(1)} %collective-permute-done.17.refs_1_, f32[48,512]{1,0:T(8,128)S(1)} %collective-permute-done.18.refs_2_, f32[48,512]{1,0:T(8,128)S(1)} %collective-permute-done.19.refs_3_), custom_call_target="tpu_custom_call" | custom-call | tf_op jit(solution)/shard_map/price/pallas_call | solution.py:460
  (6 shorter events, 0.1 us)
Async XLA Ops:
  11.2 4.7 %collective-permute-start.1 = (f32[2,2,4,128]{3,2,1,0:T(4,128)S(1)}, f32[2,2,4,128]{3,2,1,0:T(4,128)S(1)}, u32[]{:S(2)}, u32[]{:S(2)}) collective-permute-start(f32[2,2,4,128]{3,2,1,0:T(4,128)S(1)} %slice.34), channel_id=1, source_target_pairs={{0,16},{8,24},{16,0},{24,8},{1,17},{9,25},{17,1},{25,9},{2,18},{10... | collective-permute-start | bytes 24584 | tf_op jit(solution)/shard_map/ppermute | solution.py:419
  14.3 1.6 %collective-permute-start = (f32[1,2,4,128]{3,2,1,0:T(4,128)S(1)}, f32[1,2,4,128]{3,2,1,0:T(4,128)S(1)}, u32[]{:S(2)}, u32[]{:S(2)}) collective-permute-start(f32[1,2,4,128]{3,2,1,0:T(4,128)S(1)} %slice.33), channel_id=1, source_target_pairs={{0,8},{8,0},{16,24},{24,16},{1,9},{9,1},{17,25},{25,17},{2,10},{10... | collective-permute-start | bytes 12296 | tf_op jit(solution)/shard_map/ppermute | solution.py:417
  15.9 1.2 %collective-permute-start.2 = (f32[1,2,4,128]{3,2,1,0:T(4,128)S(1)}, f32[1,2,4,128]{3,2,1,0:T(4,128)S(1)}, u32[]{:S(2)}, u32[]{:S(2)}) collective-permute-start(f32[1,2,4,128]{3,2,1,0:T(4,128)S(1)} %slice.44), channel_id=1, source_target_pairs={{0,8},{8,0},{16,24},{24,16},{1,9},{9,1},{17,25},{25,17},{2,10},{10... | collective-permute-start | bytes 12296 | tf_op jit(solution)/shard_map/ppermute | solution.py:420
  17.6 7.7 %collective-permute-start.5 = (bf16[48,512]{1,0:T(8,128)(2,1)S(1)}, bf16[48,512]{1,0:T(8,128)(2,1)S(1)}, u32[]{:S(2)}, u32[]{:S(2)}) collective-permute-start(bf16[48,512]{1,0:T(8,128)(2,1)S(1)} %net.1.refs_0_), channel_id=1, source_target_pairs={{0,6},{1,7},{2,4},{3,5},{4,2},{5,3},{6,0},{7,1},{8,14},{9,15},{10,... | collective-permute-start | bytes 147464 | tf_op jit(solution)/shard_map/ppermute | solution.py:430
  21.8 5.1 %collective-permute-start.4 = (bf16[48,512]{1,0:T(8,128)(2,1)S(1)}, bf16[48,512]{1,0:T(8,128)(2,1)S(1)}, u32[]{:S(2)}, u32[]{:S(2)}) collective-permute-start(bf16[48,512]{1,0:T(8,128)(2,1)S(1)} %net.1.refs_0_), channel_id=1, source_target_pairs={{0,4},{1,5},{2,6},{3,7},{4,0},{5,1},{6,2},{7,3},{8,12},{9,13},{10,... | collective-permute-start | bytes 147464 | tf_op jit(solution)/shard_map/ppermute | solution.py:430
  21.8 6.5 %collective-permute-start.7 = (bf16[48,512]{1,0:T(8,128)(2,1)S(1)}, bf16[48,512]{1,0:T(8,128)(2,1)S(1)}, u32[]{:S(2)}, u32[]{:S(2)}) collective-permute-start(bf16[48,512]{1,0:T(8,128)(2,1)S(1)} %net.1.refs_0_), channel_id=1, source_target_pairs={{0,3},{1,2},{2,1},{3,0},{4,7},{5,6},{6,5},{7,4},{8,11},{9,10},{10,... | collective-permute-start | bytes 147464 | tf_op jit(solution)/shard_map/ppermute | solution.py:433
  23.5 4.8 %collective-permute-start.6 = (bf16[48,512]{1,0:T(8,128)(2,1)S(1)}, bf16[48,512]{1,0:T(8,128)(2,1)S(1)}, u32[]{:S(2)}, u32[]{:S(2)}) collective-permute-start(bf16[48,512]{1,0:T(8,128)(2,1)S(1)} %net.1.refs_0_), channel_id=1, source_target_pairs={{0,1},{1,0},{2,3},{3,2},{4,5},{5,4},{6,7},{7,6},{8,9},{9,8},{10,11... | collective-permute-start | bytes 147464 | tf_op jit(solution)/shard_map/ppermute | solution.py:435
  23.9 4.4 %collective-permute-start.3 = (bf16[48,512]{1,0:T(8,128)(2,1)S(1)}, bf16[48,512]{1,0:T(8,128)(2,1)S(1)}, u32[]{:S(2)}, u32[]{:S(2)}) collective-permute-start(bf16[48,512]{1,0:T(8,128)(2,1)S(1)} %net.1.refs_0_), channel_id=1, source_target_pairs={{0,2},{1,3},{2,0},{3,1},{4,6},{5,7},{6,4},{7,5},{8,10},{9,11},{10,... | collective-permute-start | bytes 147464 | tf_op jit(solution)/shard_map/ppermute | solution.py:430
  25.3 4.5 %collective-permute-start.9 = (bf16[48,512]{1,0:T(8,128)(2,1)S(1)}, bf16[48,512]{1,0:T(8,128)(2,1)S(1)}, u32[]{:S(2)}, u32[]{:S(2)}) collective-permute-start(bf16[48,512]{1,0:T(8,128)(2,1)S(1)} %collective-permute-done.5.refs_3_), channel_id=1, source_target_pairs={{0,1},{1,0},{2,3},{3,2},{4,5},{5,4},{6,7},{7,6},{8,9},{9,8},{10,11... | collective-permute-start | bytes 147464 | tf_op jit(solution)/shard_map/ppermute | solution.py:435
  26.8 4.1 %collective-permute-start.8 = (bf16[48,512]{1,0:T(8,128)(2,1)S(1)}, bf16[48,512]{1,0:T(8,128)(2,1)S(1)}, u32[]{:S(2)}, u32[]{:S(2)}) collective-permute-start(bf16[48,512]{1,0:T(8,128)(2,1)S(1)} %collective-permute-done.4.refs_2_), channel_id=1, source_target_pairs={{0,1},{1,0},{2,3},{3,2},{4,5},{5,4},{6,7},{7,6},{8,9},{9,8},{10,11... | collective-permute-start | bytes 147464 | tf_op jit(solution)/shard_map/ppermute | solution.py:435
  34.5 5.6 %collective-permute-start.15 = (bf16[48,512]{1,0:T(8,128)(2,1)S(1)}, bf16[48,512]{1,0:T(8,128)(2,1)S(1)}, u32[]{:S(2)}, u32[]{:S(2)}) collective-permute-start(bf16[48,512]{1,0:T(8,128)(2,1)S(1)} %get-tuple-element.23), channel_id=1, source_target_pairs={{0,1},{1,0},{2,3},{3,2},{4,5},{5,4},{6,7},{7,6},{8,9},{9,8},{10,11... | collective-permute-start | bytes 147464 | tf_op jit(solution)/shard_map/ppermute | solution.py:450
  36.1 4.6 %collective-permute-start.13 = (bf16[48,512]{1,0:T(8,128)(2,1)S(1)}, bf16[48,512]{1,0:T(8,128)(2,1)S(1)}, u32[]{:S(2)}, u32[]{:S(2)}) collective-permute-start(bf16[48,512]{1,0:T(8,128)(2,1)S(1)} %get-tuple-element.24), channel_id=1, source_target_pairs={{0,1},{1,0},{2,3},{3,2},{4,5},{5,4},{6,7},{7,6},{8,9},{9,8},{10,11... | collective-permute-start | bytes 147464 | tf_op jit(solution)/shard_map/ppermute | solution.py:450
  36.6 6.7 %collective-permute-start.10 = (bf16[48,512]{1,0:T(8,128)(2,1)S(1)}, bf16[48,512]{1,0:T(8,128)(2,1)S(1)}, u32[]{:S(2)}, u32[]{:S(2)}) collective-permute-start(bf16[48,512]{1,0:T(8,128)(2,1)S(1)} %get-tuple-element.22), channel_id=1, source_target_pairs={{0,1},{1,0},{2,3},{3,2},{4,5},{5,4},{6,7},{7,6},{8,9},{9,8},{10,11... | collective-permute-start | bytes 147464 | tf_op jit(solution)/shard_map/ppermute | solution.py:450
  38.1 5.3 %collective-permute-start.12 = (bf16[48,512]{1,0:T(8,128)(2,1)S(1)}, bf16[48,512]{1,0:T(8,128)(2,1)S(1)}, u32[]{:S(2)}, u32[]{:S(2)}) collective-permute-start(bf16[48,512]{1,0:T(8,128)(2,1)S(1)} %get-tuple-element.25), channel_id=1, source_target_pairs={{0,3},{1,2},{2,1},{3,0},{4,7},{5,6},{6,5},{7,4},{8,11},{9,10},{10,... | collective-permute-start | bytes 147464 | tf_op jit(solution)/shard_map/ppermute | solution.py:447
  38.8 4.6 %collective-permute-start.11 = (bf16[48,512]{1,0:T(8,128)(2,1)S(1)}, bf16[48,512]{1,0:T(8,128)(2,1)S(1)}, u32[]{:S(2)}, u32[]{:S(2)}) collective-permute-start(bf16[48,512]{1,0:T(8,128)(2,1)S(1)} %get-tuple-element.26), channel_id=1, source_target_pairs={{0,2},{1,3},{2,0},{3,1},{4,6},{5,7},{6,4},{7,5},{8,10},{9,11},{10,... | collective-permute-start | bytes 147464 | tf_op jit(solution)/shard_map/ppermute | solution.py:446
  40.7 5.4 %collective-permute-start.14 = (bf16[48,512]{1,0:T(8,128)(2,1)S(1)}, bf16[48,512]{1,0:T(8,128)(2,1)S(1)}, u32[]{:S(2)}, u32[]{:S(2)}) collective-permute-start(bf16[48,512]{1,0:T(8,128)(2,1)S(1)} %get-tuple-element.20), channel_id=1, source_target_pairs={{0,4},{1,5},{2,6},{3,7},{4,0},{5,1},{6,2},{7,3},{8,12},{9,13},{10,... | collective-permute-start | bytes 147464 | tf_op jit(solution)/shard_map/ppermute | solution.py:453
  43.0 5.9 %collective-permute-start.16 = (bf16[48,512]{1,0:T(8,128)(2,1)S(1)}, bf16[48,512]{1,0:T(8,128)(2,1)S(1)}, u32[]{:S(2)}, u32[]{:S(2)}) collective-permute-start(bf16[48,512]{1,0:T(8,128)(2,1)S(1)} %get-tuple-element.21), channel_id=1, source_target_pairs={{0,6},{1,7},{2,4},{3,5},{4,2},{5,3},{6,0},{7,1},{8,14},{9,15},{10,... | collective-permute-start | bytes 147464 | tf_op jit(solution)/shard_map/ppermute | solution.py:453
  49.0 4.7 %collective-permute-start.18 = (f32[48,512]{1,0:T(8,128)S(1)}, f32[48,512]{1,0:T(8,128)S(1)}, u32[]{:S(2)}, u32[]{:S(2)}) collective-permute-start(f32[48,512]{1,0:T(8,128)S(1)} %fusion.5.refs_0_), channel_id=1, source_target_pairs={{0,16},{8,24},{16,0},{24,8},{1,17},{9,25},{17,1},{25,9},{2,18},{10... | collective-permute-start | bytes 294920 | tf_op jit(solution)/shard_map/ppermute | solution.py:459
  50.6 3.1 %collective-permute-start.17 = (f32[48,512]{1,0:T(8,128)S(1)}, f32[48,512]{1,0:T(8,128)S(1)}, u32[]{:S(2)}, u32[]{:S(2)}) collective-permute-start(f32[48,512]{1,0:T(8,128)S(1)} %fusion.5.refs_0_), channel_id=1, source_target_pairs={{0,8},{8,0},{16,24},{24,16},{1,9},{9,1},{17,25},{25,17},{2,10},{10... | collective-permute-start | bytes 294920 | tf_op jit(solution)/shard_map/ppermute | solution.py:459
  53.7 1.3 %collective-permute-start.19 = (f32[48,512]{1,0:T(8,128)S(1)}, f32[48,512]{1,0:T(8,128)S(1)}, u32[]{:S(2)}, u32[]{:S(2)}) collective-permute-start(f32[48,512]{1,0:T(8,128)S(1)} %collective-permute-done.18.refs_2_), channel_id=1, source_target_pairs={{0,8},{8,0},{16,24},{24,16},{1,9},{9,1},{17,25},{25,17},{2,10},{10... | collective-permute-start | bytes 294920 | tf_op jit(solution)/shard_map/ppermute | solution.py:459
